TPU v7x, 128 devices: a whole 4x4x4 slice. The times are simulated.
128 devices in a mesh: dp: 16 (over z, x), table: 8 (over y, core).
Axes of the slice: x: 4, y: 4, z: 4, core: 2. Of those that a mesh axis runs over, the one named last changes fastest.
Arguments:
- hot_grad: float32 [16, 8, 1024, 512], P('dp', 'table'), may hold values from -8 to 8
- first_moment: float32 [1024, 512], P('dp'), may hold values from -24 to 24
- second_moment: float32 [1024, 512], P('dp'), may hold values from 0.01 to 0.5
- hot_master: float32 [1024, 512], P('dp'), may hold values from -3 to 3
- hot_ids: int32 [16, 8, 4096], P('dp', 'table'), may hold values from 0 to 1023
- hot_lengths: int32 [16, 8, 1024], P('dp', 'table'), may hold values from 1 to 16, 4096 in all within a row
- cold_table: bfloat16 [16384, 512], P('table'), may hold values from -6 to 6
- cold_index: int32 [16, 8, 8, 128], P('dp', 'table'), may hold values from 0 to 2047
- cold_count: int32 [16, 8, 8], P('dp', 'table'), may hold values from 32 to 128, as said below
- cold_sample: int32 [16, 8, 8, 128], P('dp', 'table'), may hold values from 0 to 1023
- w_in: bfloat16 [1024, 2048], replicated, may hold values from -0.1875 to 0.1875
- b_in: float32 [2048], replicated, may hold values from -3 to 3
- w_out: bfloat16 [2048, 2048], replicated, may hold values from -0.125 to 0.125
- b_out: float32 [2048], replicated, may hold values from -3 to 3
Outputs:
- activations: float32 [16, 8, 1024, 2048], P('dp', 'table')
- new_master: float32 [1024, 512], P(('dp', 'table'))
- new_first: float32 [1024, 512], P(('dp', 'table'))
- new_second: float32 [1024, 512], P(('dp', 'table'))
Inputs may be any that keep to these rules, and one draw needn't show every extreme that they name: `hot_lengths`: each device's lengths sum to 4096. `cold_count`: for every owner and dp index some requester's block is full.
All inputs are finite; a program needn't handle non-finite values.
Results may differ from a plain program's by a relative error of at most 0.0036.
Values may be sent and summed in bfloat16 or wider, within the bound.
No kernel may reach another device: no remote copies, remote signals or barrier semaphores. Data moves between devices by JAX's collectives and lax.ppermute only.
A program may use at most 128 MiB of HBM per device.

v0:
```python
import jax
import jax.numpy as jnp
from jax import lax
from jax.sharding import PartitionSpec as P

beta_first = 0.9
beta_second = 0.999
adam_count = 10
learning_rate = 0.05
weight_decay = 0.01
epsilon = 1e-08


def adamw(master, first, second, grad):
    first_new = beta_first * first + (1.0 - beta_first) * grad
    second_new = beta_second * second + (1.0 - beta_second) * grad * grad
    corrected = first_new / (1.0 - beta_first**adam_count)
    scaled = second_new / (1.0 - beta_second**adam_count)
    master_new = master - learning_rate * (
        corrected / (jnp.sqrt(scaled) + epsilon) + weight_decay * master
    )
    return (master_new, first_new, second_new)


def on_device(
    hot_grad,
    first_moment,
    second_moment,
    hot_master,
    hot_ids,
    hot_lengths,
    cold_table,
    cold_index,
    cold_count,
    cold_sample,
    w_in,
    b_in,
    w_out,
    b_out,
):
    width = cold_table.shape[1]
    batch = hot_lengths.shape[2]
    index_rows = cold_index[0, 0]
    counts = cold_count[0, 0]
    picked = jnp.take(cold_table, index_rows, axis=0)
    slot_pos = lax.broadcasted_iota(jnp.int32, index_rows.shape, 1)
    used = slot_pos < counts[:, None]
    picked = jnp.where(used[..., None], picked, jnp.zeros((), jnp.bfloat16))
    received = lax.all_to_all(picked, "table", split_axis=0, concat_axis=0, tiled=True)
    cold_pool = jax.ops.segment_sum(
        received.reshape(-1, width).astype(jnp.float32),
        cold_sample[0, 0].reshape(-1),
        num_segments=batch,
    )
    grad = hot_grad[0, 0]
    own_rows = hot_master.shape[0] // lax.axis_size("table")
    offset = lax.axis_index("table") * own_rows
    shard_grad = lax.psum_scatter(grad, "dp", scatter_dimension=0, tiled=True)
    shard_grad = lax.psum(shard_grad, "table")
    whole_master, whole_first, whole_second = adamw(
        hot_master, first_moment, second_moment, shard_grad
    )
    new_master = lax.dynamic_slice_in_dim(whole_master, offset, own_rows, 0)
    new_first = lax.dynamic_slice_in_dim(whole_first, offset, own_rows, 0)
    new_second = lax.dynamic_slice_in_dim(whole_second, offset, own_rows, 0)
    fresh = new_master.astype(jnp.bfloat16)
    lookups = hot_ids[0, 0]
    fresh_all = lax.all_gather(fresh, ("dp", "table"), axis=0, tiled=True)
    looked = jnp.take(fresh_all, lookups, axis=0)
    ends = jnp.cumsum(hot_lengths[0, 0])
    positions = lax.broadcasted_iota(jnp.int32, (lookups.shape[0], 1), 0)
    segment = jnp.sum((positions >= ends[None, :]).astype(jnp.int32), axis=1)
    hot_pool = jax.ops.segment_sum(
        looked.astype(jnp.float32), segment, num_segments=batch, indices_are_sorted=True
    )
    hot_feat = hot_pool.astype(jnp.bfloat16)
    cold_feat = cold_pool.astype(jnp.bfloat16)
    features = jnp.concatenate([hot_feat, cold_feat], axis=1)
    pre = jnp.dot(features, w_in, preferred_element_type=jnp.float32)
    hidden = jnp.maximum(pre + b_in, 0.0).astype(jnp.bfloat16)
    result = jnp.dot(hidden, w_out, preferred_element_type=jnp.float32) + b_out
    return (result[None, None], new_master, new_first, new_second)


def solution(mesh):
    return jax.shard_map(
        on_device,
        mesh=mesh,
        in_specs=(
            P("dp", "table", None, None),
            P("dp", None),
            P("dp", None),
            P("dp", None),
            P("dp", "table", None),
            P("dp", "table", None),
            P("table", None),
            P("dp", "table", None, None),
            P("dp", "table", None),
            P("dp", "table", None, None),
            P(),
            P(),
            P(),
            P(),
        ),
        out_specs=(
            P("dp", "table", None, None),
            P(("dp", "table"), None),
            P(("dp", "table"), None),
            P(("dp", "table"), None),
        ),
        check_vma=False,
    )
```

profile of v0, /device:TPU:1, one launch (start us, length us, event | category | flops | bytes accessed | tf_op | source)
XLA Modules:
  0.0 304.5 jit_solution(17689454489409301434)
XLA Ops:
  7.2 0.0 copy-start
  7.2 0.0 reduce-scatter.2.cloned.1.call-start
  7.2 0.7 reduce-scatter.2.cloned.1.call-update
  7.9 0.0 all-reduce.2.cloned.1.call-start
  8.0 0.7 fusion.27
  8.7 0.1 copy-done
  8.8 0.0 copy-start.5
  8.8 0.0 copy-start.7
  8.8 4.0 %gather_fusion = bf16[1024,512]{1,0:T(8,128)(2,1)S(1)} fusion(bf16[2048,512]{1,0:T(8,128)(2,1)S(1)} %copy-done, s32[1024]{0:T(1024)S(1)} %fusion.27), kind=kCustom, calls=%fused_computation.1 | custom fusion | bytes 2101248 | tf_op jit(solution)/shard_map/jit(_take)/gather | solution.py:45
  12.7 0.0 copy-start.6
  12.7 0.0 copy-start.1
  12.8 0.0 copy-start.2
  12.8 0.0 copy-start.3
  12.8 0.0 copy-done.5
  12.8 0.0 copy-done.7
  12.8 0.1 iota_compare_fusion.1
  12.9 74.5 %reduce-scatter.2.cloned.1.call-done = f32[64,512]{1,0:T(8,128)} async-done(((f32[1024,512]{1,0:T(8,128)}), f32[64,512]{1,0:T(8,128)}) %reduce-scatter.2.cloned.1.call-update) | async-done | bytes 131088 | tf_op jit(solution)/shard_map/reduce_scatter | solution.py:58
  87.4 0.0 all-reduce.2.cloned.1.call-update
  87.4 1.2 select_select_fusion
  88.7 6.6 %all-to-all-start = ((bf16[8,128,512]{2,1,0:T(8,128)(2,1)}), bf16[8,128,512]{2,1,0:T(8,128)(2,1)S(1)}, u32[]{:S(2)}, u32[]{:S(2)}) async-start(bf16[8,128,512]{2,1,0:T(8,128)(2,1)} %select_select_fusion), calls=%async_computation.1 | async-start | bytes 2097152 | tf_op jit(solution)/shard_map/all_to_all | solution.py:49
  95.3 0.0 all-gather.2.cloned.1.call-start
  95.3 0.0 copy-done.6
  95.3 0.3 reduce-window.9
  95.6 0.0 copy-start.4
  95.6 0.1 slice.7
  95.6 0.6 reduce-window.12
  96.3 0.0 copy-done.4
  96.3 52.4 %all-reduce.2.cloned.1.call-done = f32[64,512]{1,0:T(8,128)} async-done(((f32[64,512]{1,0:T(8,128)}), f32[64,512]{1,0:T(8,128)}) %all-reduce.2.cloned.1.call-update) | async-done | bytes 131088 | tf_op jit(solution)/shard_map/psum | solution.py:59
  148.7 0.0 copy-done.1
  148.7 0.0 copy-done.2
  148.7 1.0 broadcast_multiply_fusion
  149.6 1.4 fusion.32
  151.0 0.0 all-gather.2.cloned.1.call-update
  151.0 0.8 slice_reduce_fusion
  151.8 0.0 copy-done.3
  151.9 0.7 add_bitcast_fusion.1
  152.6 1.8 convert_reduce_fusion
  154.4 0.0 all-to-all-done
  154.4 8.2 %scatter_custom_fusion.1 = f32[1024,512]{1,0:T(8,128)} fusion(s32[1024]{0:T(1024)} %bitcast.34, bf16[1024,512]{1,0:T(8,128)(2,1)S(1)} %bitcast.28, f32[]{:T(128)} %constant.20.clone.1), kind=kCustom, calls=%fused_computation.19 | custom fusion | flops 1048576 | bytes 3146240 | tf_op jit(solution)/shard_map/scatter-add | solution.py:50
  162.7 0.0 copy-start.8
  162.7 1.8 convert_element_type.30
  164.4 0.6 constant_dynamic-slice_fusion
  165.0 51.5 %all-gather.2.cloned.1.call-done = bf16[1024,512]{1,0:T(8,128)(2,1)} async-done(((bf16[8,512]{1,0:T(8,128)(2,1)}), bf16[1024,512]{1,0:T(8,128)(2,1)}) %all-gather.2.cloned.1.call-update) | async-done | bytes 1048592 | tf_op jit(solution)/shard_map/all_gather | solution.py:68
  216.6 57.2 %scatter_custom_fusion = f32[1024,512]{1,0:T(8,128)} fusion(s32[4096]{0:T(1024)S(1)} %convert_reduce_fusion, pred[4096]{0:T(1024)(128)(4,1)S(1)} %compare_and_fusion, bf16[]{:T(256)} %constant.63.clone.1, f32[]{:T(128)} %constant.20.clone.1, bf16[1024,512]{1,0:T(8,128)(2,1)} %all-gather.2.cloned.1.call-done, s32[4096]{0:T(1024)S(1)} %broadcast_clamp_fusion), kind=kCustom, calls=%fused_computation.8 | custom fusion | flops 6291456 | bytes 3166214 | tf_op jit(solution)/shard_map/scatter-add | solution.py:73
  273.8 2.7 convert_element_type.27
  276.5 0.0 copy-done.8
  276.5 0.0 copy-done.9
  276.5 21.5 %add_bitcast_fusion = f32[1,1,1024,2048]{3,2,1,0:T(8,128)} fusion(f32[2048]{0:T(1024)S(1)} %copy-done.8, bf16[2048,2048]{1,0:T(8,128)(2,1)} %param.26, bf16[1024,2048]{1,0:T(8,128)(2,1)} %param.24, f32[2048]{0:T(1024)S(1)} %copy-done.9, bf16[1024,512]{1,0:T(8,128)(2,1)S(1)} %convert_element_type.30, bf16[1024,512]{1,0:T(8,128)(2,1)} %convert_element_type.27), kind=kOutput, calls=%fused_computation.6 | convolution fusion | flops 12897484800 | bytes 23085056 | tf_op jit(solution)/shard_map/dot_general | solution.py:81
  (4 shorter events, 0.0 us)
Async XLA Ops:
  7.2 1.6 copy-start
  7.2 80.2 %reduce-scatter.2.cloned.1.call-start = ((), (), s32[]{:S(2)}) async-start(), calls=%async_computation.2 | async-start | bytes 2228224 | tf_op jit(solution)/shard_map/reduce_scatter | solution.py:58
  7.9 140.8 %all-reduce.2.cloned.1.call-start = ((), (), s32[]{:S(2)}) async-start(), calls=%async_computation.3 | async-start | bytes 262144 | tf_op jit(solution)/shard_map/psum | solution.py:59
  8.8 4.0 %copy-start.5 = (s32[1,1,8,128]{3,2,1,0:T(8,128)S(1)}, s32[1,1,8,128]{3,2,1,0:T(8,128)}, u32[]{:S(2)}) copy-start(s32[1,1,8,128]{3,2,1,0:T(8,128)} %param.21) | copy-start | bytes 12292
  8.8 4.0 %copy-start.7 = (s32[1,1,8]{2,1,0:T(1,128)S(1)}, s32[1,1,8]{2,1,0:T(1,128)}, u32[]{:S(2)}) copy-start(s32[1,1,8]{2,1,0:T(1,128)} %param.22) | copy-start | bytes 100
  12.7 82.6 %copy-start.6 = (s32[1,1,1024]{2,1,0:T(1,128)S(1)}, s32[1,1,1024]{2,1,0:T(1,128)}, u32[]{:S(2)}) copy-start(s32[1,1,1024]{2,1,0:T(1,128)} %param.19) | copy-start | bytes 12292
  12.7 135.9 %copy-start.1 = (f32[64,512]{1,0:T(8,128)S(1)}, f32[64,512]{1,0:T(8,128)}, u32[]{:S(2)}) copy-start(f32[64,512]{1,0:T(8,128)} %param.16) | copy-start | bytes 393220
  12.8 135.9 %copy-start.2 = (f32[64,512]{1,0:T(8,128)S(1)}, f32[64,512]{1,0:T(8,128)}, u32[]{:S(2)}) copy-start(f32[64,512]{1,0:T(8,128)} %param.15) | copy-start | bytes 393220
  12.8 139.1 %copy-start.3 = (s32[1,1,4096]{2,1,0:T(1,128)S(1)}, s32[1,1,4096]{2,1,0:T(1,128)}, u32[]{:S(2)}) copy-start(s32[1,1,4096]{2,1,0:T(1,128)} %param.18) | copy-start | bytes 49156
  88.7 65.7 %all-to-all-start = ((bf16[8,128,512]{2,1,0:T(8,128)(2,1)}), bf16[8,128,512]{2,1,0:T(8,128)(2,1)S(1)}, u32[]{:S(2)}, u32[]{:S(2)}) async-start(bf16[8,128,512]{2,1,0:T(8,128)(2,1)} %select_select_fusion), calls=%async_computation.1 | async-start | bytes 2097152 | tf_op jit(solution)/shard_map/all_to_all | solution.py:49
  95.3 121.3 %all-gather.2.cloned.1.call-start = ((), (), s32[]{:S(2)}) async-start(), calls=%async_computation.4 | async-start | bytes 1056768 | tf_op jit(solution)/shard_map/all_gather | solution.py:68
  95.6 0.7 copy-start.4
  162.7 113.8 %copy-start.8 = (f32[2048]{0:T(1024)S(1)}, f32[2048]{0:T(1024)}, u32[]{:S(2)}) copy-start(f32[2048]{0:T(1024)} %param.27) | copy-start | bytes 24580
  162.7 113.8 %copy-start.9 = (f32[2048]{0:T(1024)S(1)}, f32[2048]{0:T(1024)}, u32[]{:S(2)}) copy-start(f32[2048]{0:T(1024)} %param.25) | copy-start | bytes 24580
Sparse Core Ops, SparseCore 0:
  11.3 76.0 reduce-scatter.1
  89.8 58.7 all-reduce.1
  151.5 65.0 all-gather.1
where the time goes:
time: 305 us
  waiting for transfers between devices  179 us (59%)
  other arithmetic  77.7 us (25%)
  matrix products  21.5 us (7%)
  between operations  13.9 us (5%)
  starting transfers between devices  6.67 us (2%)
  local copies, waits for them, and re-layouts  5.61 us (2%)
    reduce_scatter x1, waiting for transfers between devices, on_device(): shard_grad = lax.psum_scatter(grad, 'dp', scatter_dimension=0, tiled=True)  74.5 us
    scatter-add x1, other arithmetic, on_device(): jax.ops.segment_sum(looked.astype(jnp.float32), segment, num_segments=bat...  57.2 us
    psum x1, waiting for transfers between devices, on_device(): shard_grad = lax.psum(shard_grad, 'table')  52.4 us
    all_gather x1, waiting for transfers between devices, on_device(): fresh_all = lax.all_gather(fresh, ('dp', 'table'), axis=0, tiled=True)  51.5 us
    dot_general x1, matrix products, on_device(): result = jnp.dot(hidden, w_out, preferred_element_type=jnp.float32) + b_out  21.5 us
    scatter-add x1, other arithmetic, on_device(): jax.ops.segment_sum(received.reshape(-1, width).astype(jnp.float32), cold...  8.25 us
    all_to_all x1, starting transfers between devices, on_device(): lax.all_to_all(picked, 'table', split_axis=0, concat_axis=0, tiled=True)  6.59 us
  transfers between devices with their start and end apart: 4, of which 3 were waited for; matrix products, arithmetic and copies ran while one was open for 8% of the time, Pallas kernels for 0%

commit v1 on v0

v1 whole, which is shorter than its diff:
```python
import functools

import jax
import jax.numpy as jnp
from jax import lax
from jax.experimental import pallas as pl
from jax.experimental.pallas import tpu as pltpu
from jax.sharding import PartitionSpec as P

beta_first = 0.9
beta_second = 0.999
adam_count = 10
learning_rate = 0.05
weight_decay = 0.01
epsilon = 1e-08

CHUNK = 256
BAGS = 128


def adamw(master, first, second, grad):
    first_new = beta_first * first + (1.0 - beta_first) * grad
    second_new = beta_second * second + (1.0 - beta_second) * grad * grad
    corrected = first_new / (1.0 - beta_first**adam_count)
    scaled = second_new / (1.0 - beta_second**adam_count)
    master_new = master - learning_rate * (
        corrected / (jnp.sqrt(scaled) + epsilon) + weight_decay * master
    )
    return (master_new, first_new, second_new)


def count_kernel(columns_ref, lengths_ref, out_ref, start_ref, end_ref, total_ref):
    chunks = columns_ref.shape[0]
    blocks = lengths_ref.shape[0]
    width = out_ref.shape[1]
    row = lax.broadcasted_iota(jnp.int32, (BAGS, BAGS), 0)
    col = lax.broadcasted_iota(jnp.int32, (BAGS, BAGS), 1)
    upto = (col <= row).astype(jnp.bfloat16)
    before = (col < row).astype(jnp.bfloat16)
    contract = (((1,), (1,)), ((), ()))
    offset = jnp.float32(0.0)
    firsts = []
    for k in range(blocks):
        lengths = lengths_ref[k].astype(jnp.float32)
        spread = jnp.broadcast_to(lengths, (BAGS, BAGS)).astype(jnp.bfloat16)
        end_ref[k] = offset + lax.dot_general(
            upto, spread, contract, preferred_element_type=jnp.float32
        )
        start_ref[k] = offset + lax.dot_general(
            before, spread, contract, preferred_element_type=jnp.float32
        )
        firsts.append(offset)
        offset = offset + jnp.sum(lengths)
    total_ref[...] = jnp.zeros_like(total_ref)
    firsts = [f.astype(jnp.int32) for f in firsts]

    def chunk_step(j, _):
        ids = columns_ref[j]
        rows = lax.broadcasted_iota(jnp.int32, (width, CHUNK), 0)
        hits = jnp.where(rows == ids, 1.0, 0.0).astype(jnp.bfloat16)
        low = j * CHUNK
        k_low = jnp.int32(-1)
        k_high = jnp.int32(0)
        for f in firsts:
            k_low = k_low + (f <= low).astype(jnp.int32)
            k_high = k_high + (f < low + CHUNK).astype(jnp.int32)
        where = (low + lax.broadcasted_iota(jnp.int32, (BAGS, BAGS), 1)).astype(jnp.float32)

        def block_step(k, _):
            start, end = start_ref[k], end_ref[k]
            parts = [
                jnp.where((start <= where + o) & (where + o < end), 1.0, 0.0)
                for o in range(0, CHUNK, BAGS)
            ]
            member = jnp.concatenate(parts, axis=1).astype(jnp.bfloat16)
            place = pl.ds(pl.multiple_of(k * BAGS, BAGS), BAGS)
            total_ref[place, :] += lax.dot_general(
                member, hits, contract, preferred_element_type=jnp.float32
            )
            return 0

        lax.fori_loop(k_low, k_high, block_step, 0)
        return 0

    lax.fori_loop(0, chunks, chunk_step, 0)
    out_ref[...] = total_ref[...].astype(out_ref.dtype)


def count_matrix(columns, lengths, width):
    look, batch = columns.shape[0], lengths.shape[0]
    chunks, blocks = look // CHUNK, batch // BAGS
    return pl.pallas_call(
        count_kernel,
        out_shape=jax.ShapeDtypeStruct((batch, width), jnp.bfloat16),
        in_specs=[pl.BlockSpec(memory_space=pltpu.VMEM)] * 2,
        out_specs=pl.BlockSpec(memory_space=pltpu.VMEM),
        scratch_shapes=[
            pltpu.VMEM((blocks, BAGS, BAGS), jnp.float32),
            pltpu.VMEM((blocks, BAGS, BAGS), jnp.float32),
            pltpu.VMEM((batch, width), jnp.float32),
        ],
        compiler_params=pltpu.CompilerParams(vmem_limit_bytes=24 << 20),
        cost_estimate=pl.CostEstimate(
            flops=24 * 2 * BAGS * CHUNK * width, bytes_accessed=2 * batch * width, transcendentals=0
        ),
    )(columns.reshape(chunks, 1, CHUNK), lengths.reshape(blocks, 1, BAGS))


def on_device(
    hot_grad,
    first_moment,
    second_moment,
    hot_master,
    hot_ids,
    hot_lengths,
    cold_table,
    cold_index,
    cold_count,
    cold_sample,
    w_in,
    b_in,
    w_out,
    b_out,
):
    width = cold_table.shape[1]
    batch = hot_lengths.shape[2]
    hot = hot_grad.shape[2]
    n_dp, n_table = lax.axis_size("dp"), lax.axis_size("table")
    lines = n_table // 2
    place = lax.axis_index("table")
    core, line = place % 2, place // 2
    swap = [(i, i ^ 1) for i in range(n_table)]
    own = hot // (n_dp * n_table)

    grad = hot_grad[0, 0].reshape(n_dp, lines, 2, own, width)
    send = lax.dynamic_index_in_dim(grad, 1 - core, 2, keepdims=False).astype(jnp.bfloat16)
    keep = lax.dynamic_index_in_dim(grad, core, 2, keepdims=False)
    other = lax.ppermute(send, "table", swap)
    chip = (keep + other.astype(jnp.float32)).astype(jnp.bfloat16)
    parts = lax.all_to_all(chip, "dp", split_axis=0, concat_axis=0, tiled=True)
    share = jnp.sum(parts.reshape(n_dp, lines * own, width).astype(jnp.float32), axis=0)
    for step in range(1, lines):
        share_in = lax.ppermute(
            share, "table", [(i, (i + 2 * step) % n_table) for i in range(n_table)]
        )
        total = share_in + (share if step == 1 else total)

    def rows_of(state):
        state = state.reshape(lines, 2, own, width)
        return lax.dynamic_index_in_dim(state, core, 1, keepdims=False)

    updated = adamw(
        rows_of(hot_master), rows_of(first_moment), rows_of(second_moment),
        total.reshape(lines, own, width),
    )
    new_master, new_first, new_second = (
        lax.dynamic_index_in_dim(u, line, 0, keepdims=False) for u in updated
    )
    fresh = updated[0].astype(jnp.bfloat16).reshape(lines * own, width)
    spread = jnp.broadcast_to(fresh[None], (n_dp,) + fresh.shape)
    fresh_own = lax.all_to_all(spread, "dp", split_axis=0, concat_axis=0, tiled=True)
    fresh_own = fresh_own.reshape(hot // 2, width)
    fresh_other = lax.ppermute(fresh_own, "table", swap)

    index_rows = cold_index[0, 0]
    counts = cold_count[0, 0]
    picked = jnp.take(cold_table, index_rows, axis=0)
    slot_pos = lax.broadcasted_iota(jnp.int32, index_rows.shape, 1)
    used = slot_pos < counts[:, None]
    picked = jnp.where(used[..., None], picked, jnp.zeros((), jnp.bfloat16))
    received = lax.all_to_all(picked, "table", split_axis=0, concat_axis=0, tiled=True)
    samples = cold_sample[0, 0].reshape(-1)
    bag = lax.broadcasted_iota(jnp.int32, (batch, samples.shape[0]), 0)
    member = (bag == samples[None, :]).astype(jnp.bfloat16)
    cold_pool = jnp.dot(
        member, received.reshape(-1, width), preferred_element_type=jnp.float32
    )
    cold_feat = cold_pool.astype(jnp.bfloat16)
    cold_pre = jnp.dot(cold_feat, w_in[width:], preferred_element_type=jnp.float32) + b_in

    ids = hot_ids[0, 0]
    half = ((ids // own) % 2) ^ core
    columns = (ids // (2 * own)) * own + ids % own + half * (hot // 2)
    counted = count_matrix(columns, hot_lengths[0, 0], hot)

    hot_pool = jnp.dot(
        counted[:, : hot // 2], fresh_own, preferred_element_type=jnp.float32
    ) + jnp.dot(counted[:, hot // 2 :], fresh_other, preferred_element_type=jnp.float32)
    hot_feat = hot_pool.astype(jnp.bfloat16)
    pre = jnp.dot(hot_feat, w_in[:width], preferred_element_type=jnp.float32) + cold_pre
    hidden = jnp.maximum(pre, 0.0).astype(jnp.bfloat16)
    result = jnp.dot(hidden, w_out, preferred_element_type=jnp.float32) + b_out
    return (result[None, None], new_master, new_first, new_second)


def solution(mesh):
    return jax.shard_map(
        on_device,
        mesh=mesh,
        in_specs=(
            P("dp", "table", None, None),
            P("dp", None),
            P("dp", None),
            P("dp", None),
            P("dp", "table", None),
            P("dp", "table", None),
            P("table", None),
            P("dp", "table", None, None),
            P("dp", "table", None),
            P("dp", "table", None, None),
            P(),
            P(),
            P(),
            P(),
        ),
        out_specs=(
            P("dp", "table", None, None),
            P(("dp", "table"), None),
            P(("dp", "table"), None),
            P(("dp", "table"), None),
        ),
        check_vma=False,
    )
```

time: 305 us -> 110 us (0.36)
  waiting for transfers between devices: 179 us -> 18.3 us
  other arithmetic: 77.7 us -> 7.82 us
  starting transfers between devices: 6.67 us -> 25.8 us
  matrix products: 21.5 us -> 36.7 us
  between operations: 13.9 us -> 0.85 us
  Pallas kernels: 0 us -> 10.2 us
  local copies, waits for them, and re-layouts: 5.61 us -> 9.97 us
    reduce_scatter x1 -> x0, waiting for transfers between devices: 74.5 us -> none  [on_device(): shard_grad = lax.psum_scatter(grad, 'dp', scatter_dimension=0, tiled=True)]
    scatter-add x2 -> x0, other arithmetic: 65.4 us -> none  [the longest x1 57.2 us: on_device(): jax.ops.segment_sum(looked.astype(jnp.float32), segment, num_segments=bat...]
    psum x1 -> x0, waiting for transfers between devices: 52.4 us -> none  [on_device(): shard_grad = lax.psum(shard_grad, 'table')]
    all_gather x1 -> x0, waiting for transfers between devices: 51.5 us -> none  [on_device(): fresh_all = lax.all_gather(fresh, ('dp', 'table'), axis=0, tiled=True)]
    all_to_all x0 -> x2, waiting for transfers between devices: none -> 16.6 us  [the longest x1 9.81 us: on_device(): parts = lax.all_to_all(chip, 'dp', split_axis=0, concat_axis=0, tiled=True)]
    dot_general x0 -> x3, matrix products: none -> 15.5 us  [the longest x1 8.71 us: on_device(): jnp.dot(hot_feat, w_in[:width], preferred_element_type=jnp.float32)]
    all_to_all x0 -> x2, starting transfers between devices: none -> 11.3 us  [the longest x1 7.73 us: on_device(): parts = lax.all_to_all(chip, 'dp', split_axis=0, concat_axis=0, tiled=True)]
    pallas_call x0 -> x1, Pallas kernels: none -> 10.2 us  [count_matrix(): pl.pallas_call(count_kernel, out_shape=jax.ShapeDtypeStruct((batch, width...]
  transfers between devices with their start and end apart: 4 -> 8, of which waited for: 3 -> 3; matrix products, arithmetic and copies ran while one was open for 8% -> 16% of each run, Pallas kernels for 0% -> 9%
where the time goes in v1:
time: 110 us
  matrix products  36.7 us (33%)
  starting transfers between devices  25.8 us (23%)
  waiting for transfers between devices  18.3 us (17%)
  Pallas kernels  10.2 us (9%)
  local copies, waits for them, and re-layouts  9.97 us (9%)
  other arithmetic  7.82 us (7%)
    dot_general x1, matrix products, on_device(): result = jnp.dot(hidden, w_out, preferred_element_type=jnp.float32) + b_out  21.1 us
    pallas_call x1, Pallas kernels, count_matrix(): pl.pallas_call(count_kernel, out_shape=jax.ShapeDtypeStruct((batch, width...  10.2 us
    all_to_all x1, waiting for transfers between devices, on_device(): parts = lax.all_to_all(chip, 'dp', split_axis=0, concat_axis=0, tiled=True)  9.81 us
    dot_general x1, matrix products, on_device(): jnp.dot(hot_feat, w_in[:width], preferred_element_type=jnp.float32)  8.71 us
    all_to_all x1, starting transfers between devices, on_device(): parts = lax.all_to_all(chip, 'dp', split_axis=0, concat_axis=0, tiled=True)  7.73 us
    all_to_all x1, waiting for transfers between devices, on_device(): lax.all_to_all(spread, 'dp', split_axis=0, concat_axis=0, tiled=True)  6.74 us
    all_to_all x1, starting transfers between devices, on_device(): lax.all_to_all(picked, 'table', split_axis=0, concat_axis=0, tiled=True)  5.86 us
    ppermute x3, starting transfers between devices, on_device(): lax.ppermute(share, 'table', [(i, (i + 2 * step) % n_table) for i in rang...  5.04 us
  transfers between devices with their start and end apart: 8, of which 3 were waited for; matrix products, arithmetic and copies ran while one was open for 16% of the time, Pallas kernels for 9%

profile of v1, /device:TPU:1, one launch (start us, length us, event | category | flops | bytes accessed | tf_op | source)
XLA Modules:
  0.0 109.7 jit_solution(6249134447865336901)
XLA Ops:
  0.6 0.0 copy-start
  0.7 2.2 %fusion.20 = bf16[16,4,8,512]{3,2,1,0:T(8,128)(2,1)} fusion(f32[16,4,2,8,512]{4,3,2,1,0:T(8,128)} %bitcast.94, s32[]{:T(128)S(6)} %select_n.104), kind=kLoop, calls=%fused_computation.23 | loop fusion | bytes 1048580 | tf_op jit(solution)/shard_map/convert_element_type | solution.py:136
  2.9 1.4 %collective-permute-start = (bf16[16,4,8,512]{3,2,1,0:T(8,128)(2,1)}, bf16[16,4,8,512]{3,2,1,0:T(8,128)(2,1)}, u32[]{:S(2)}, u32[]{:S(2)}) collective-permute-start(bf16[16,4,8,512]{3,2,1,0:T(8,128)(2,1)} %fusion.20), channel_id=1, source_target_pairs={{0,1},{1,0},{2,3},{3,2},{4,5},{5,4},{6,7},{7,6},{8,9},{9,8},{10,11... | collective-permute-start | bytes 1572872 | tf_op jit(solution)/shard_map/ppermute | solution.py:138
  4.3 0.7 fusion.43
  5.0 0.0 copy-done
  5.0 0.0 copy-start.10
  5.0 4.0 %gather_fusion = bf16[1024,512]{1,0:T(8,128)(2,1)S(1)} fusion(bf16[2048,512]{1,0:T(8,128)(2,1)S(1)} %copy-done, s32[1024]{0:T(1024)S(1)} %fusion.43), kind=kCustom, calls=%fused_computation | custom fusion | bytes 2101248 | tf_op jit(solution)/shard_map/jit(_take)/gather | solution.py:167
  9.0 0.0 copy-start.8
  9.0 0.0 copy-start.2
  9.0 0.0 collective-permute-done
  9.0 2.4 %fusion.17 = bf16[16,4,8,512]{3,2,1,0:T(8,128)(2,1)} fusion(bf16[16,4,8,512]{3,2,1,0:T(8,128)(2,1)} %collective-permute-done, f32[16,4,2,8,512]{4,3,2,1,0:T(8,128)} %bitcast.95, s32[]{:T(128)S(6)} %select_n.103), kind=kLoop, calls=%fused_computation.19 | loop fusion | flops 786432 | bytes 2097156 | tf_op jit(solution)/shard_map/convert_element_type | solution.py:139
  11.4 7.7 %all-to-all-start = ((bf16[16,4,8,512]{3,2,1,0:T(8,128)(2,1)}), bf16[16,4,8,512]{3,2,1,0:T(8,128)(2,1)}, u32[]{:S(2)}, u32[]{:S(2)}) async-start(bf16[16,4,8,512]{3,2,1,0:T(8,128)(2,1)} %fusion.17), calls=%async_computation | async-start | bytes 1048576 | tf_op jit(solution)/shard_map/all_to_all | solution.py:140
  19.1 0.0 copy-done.9
  19.2 0.1 iota_compare_fusion.4
  19.2 1.2 %select_select_fusion = bf16[8,128,512]{2,1,0:T(8,128)(2,1)} fusion(bf16[8,128,512]{2,1,0:T(8,128)(2,1)S(1)} %bitcast.91, pred[8,128]{1,0:T(8,128)(4,1)S(1)} %get-tuple-element.11, pred[8,128]{1,0:T(8,128)(4,1)S(1)} %get-tuple-element.10), kind=kLoop, calls=%fused_computation.20 | loop fusion | flops 1048576 | bytes 2099200 | tf_op jit(solution)/shard_map/jit(_where)/select_n | solution.py:170
  20.5 9.8 %all-to-all-done = bf16[16,4,8,512]{3,2,1,0:T(8,128)(2,1)} async-done(((bf16[16,4,8,512]{3,2,1,0:T(8,128)(2,1)}), bf16[16,4,8,512]{3,2,1,0:T(8,128)(2,1)}, u32[]{:S(2)}, u32[]{:S(2)}) %all-to-all-start) | async-done | bytes 524320 | tf_op jit(solution)/shard_map/all_to_all | solution.py:140
  30.3 5.9 %all-to-all-start.2 = ((bf16[8,128,512]{2,1,0:T(8,128)(2,1)}), bf16[8,128,512]{2,1,0:T(8,128)(2,1)S(1)}, u32[]{:S(2)}, u32[]{:S(2)}) async-start(bf16[8,128,512]{2,1,0:T(8,128)(2,1)} %select_select_fusion), calls=%async_computation.2 | async-start | bytes 2097152 | tf_op jit(solution)/shard_map/all_to_all | solution.py:171
  36.2 0.2 fusion.32.columns_ref
  36.4 0.0 copy-start.6
  36.4 0.0 copy-start.13
  36.4 10.2 %shard_map.165 = bf16[1024,1024]{1,0:T(8,128)(2,1)S(1)} custom-call(s32[16,1,256]{2,1,0:T(1,128)S(1)} %fusion.32.columns_ref, s32[8,1,128]{2,1,0:T(1,128)S(1)} %bitcast.90), custom_call_target="tpu_custom_call" | custom-call | flops 1610612736 | bytes 2097152 | tf_op jit(solution)/shard_map/pallas_call | solution.py:92
  46.7 0.0 copy-start.1
  46.7 1.3 %copy-done.1 = bf16[1024,1024]{1,0:T(8,128)(2,1)} copy-done((bf16[1024,1024]{1,0:T(8,128)(2,1)}, bf16[1024,1024]{1,0:T(8,128)(2,1)S(1)}, u32[]{:S(2)}) %copy-start.1) | copy-done | bytes 2097176
  48.0 1.1 %convert_reduce_fusion = f32[4,8,512]{2,1,0:T(8,128)S(1)} fusion(bf16[16,4,8,512]{3,2,1,0:T(8,128)(2,1)} %all-to-all-done), kind=kLoop, calls=%fused_computation.21 | loop fusion | flops 507904 | bytes 589824 | tf_op jit(solution)/shard_map/reduce_sum | solution.py:141
  49.1 1.5 %collective-permute-start.3 = (f32[32,512]{1,0:T(8,128)S(1)}, f32[32,512]{1,0:T(8,128)S(1)}, u32[]{:S(2)}, u32[]{:S(2)}) collective-permute-start(f32[32,512]{1,0:T(8,128)S(1)} %bitcast.97), channel_id=1, source_target_pairs={{0,2},{1,3},{2,4},{3,5},{4,6},{5,7},{6,0},{7,1},{8,10},{9,11},{10,... | collective-permute-start | bytes 196616 | tf_op jit(solution)/shard_map/ppermute | solution.py:143
  50.6 2.4 %collective-permute-start.2 = (f32[32,512]{1,0:T(8,128)S(1)}, f32[32,512]{1,0:T(8,128)S(1)}, u32[]{:S(2)}, u32[]{:S(2)}) collective-permute-start(f32[32,512]{1,0:T(8,128)S(1)} %bitcast.98), channel_id=1, source_target_pairs={{0,4},{1,5},{2,6},{3,7},{4,0},{5,1},{6,2},{7,3},{8,12},{9,13},{10,... | collective-permute-start | bytes 196616 | tf_op jit(solution)/shard_map/ppermute | solution.py:143
  53.0 1.2 %collective-permute-start.1 = (f32[32,512]{1,0:T(8,128)S(1)}, f32[32,512]{1,0:T(8,128)S(1)}, u32[]{:S(2)}, u32[]{:S(2)}) collective-permute-start(f32[32,512]{1,0:T(8,128)S(1)} %bitcast.99), channel_id=1, source_target_pairs={{0,6},{1,7},{2,0},{3,1},{4,2},{5,3},{6,4},{7,5},{8,14},{9,15},{10,... | collective-permute-start | bytes 196616 | tf_op jit(solution)/shard_map/ppermute | solution.py:143
  54.2 0.0 copy-done.4
  54.2 0.6 dynamic-slice_bitcast_fusion
  54.8 0.0 collective-permute-done.3
  54.8 1.8 %collective-permute-done.2 = f32[32,512]{1,0:T(8,128)S(1)} collective-permute-done((f32[32,512]{1,0:T(8,128)S(1)}, f32[32,512]{1,0:T(8,128)S(1)}, u32[]{:S(2)}, u32[]{:S(2)}) %collective-permute-start.2) | collective-permute-done | bytes 65568 | tf_op jit(solution)/shard_map/ppermute | solution.py:143
  56.6 0.0 collective-permute-done.1
  56.6 0.7 fusion.28
  57.2 0.1 fusion.30
  57.3 0.0 all-to-all-done.2
  57.3 0.9 broadcast_in_dim.33
  58.3 0.2 copy-done.3
  58.5 3.6 %all-to-all-start.1 = ((bf16[16,32,512]{2,1,0:T(8,128)(2,1)}), bf16[16,32,512]{2,1,0:T(8,128)(2,1)S(1)}, u32[]{:S(2)}, u32[]{:S(2)}) async-start(bf16[16,32,512]{2,1,0:T(8,128)(2,1)} %broadcast_in_dim.33), calls=%async_computation.1 | async-start | bytes 1048576 | tf_op jit(solution)/shard_map/all_to_all | solution.py:161
  62.1 0.0 copy-start.7
  62.1 3.5 %fusion.13 = bf16[1024,512]{1,0:T(8,128)(2,1)} fusion(bf16[1024,512]{1,0:T(8,128)(2,1)} %bitcast.96, s32[1024]{0:T(1024)S(1)} %bitcast.108), kind=kOutput, calls=%fused_computation.14 | convolution fusion | flops 1075314688 | bytes 2101248 | tf_op jit(solution)/shard_map/dot_general | solution.py:175
  65.6 6.7 %all-to-all-done.1 = bf16[16,32,512]{2,1,0:T(8,128)(2,1)S(1)} async-done(((bf16[16,32,512]{2,1,0:T(8,128)(2,1)}), bf16[16,32,512]{2,1,0:T(8,128)(2,1)S(1)}, u32[]{:S(2)}, u32[]{:S(2)}) %all-to-all-start.1) | async-done | bytes 524320 | tf_op jit(solution)/shard_map/all_to_all | solution.py:161
  72.3 2.2 %collective-permute-start.4 = (bf16[512,512]{1,0:T(8,128)(2,1)S(1)}, bf16[512,512]{1,0:T(8,128)(2,1)S(1)}, u32[]{:S(2)}, u32[]{:S(2)}) collective-permute-start(bf16[512,512]{1,0:T(8,128)(2,1)S(1)} %bitcast.92), channel_id=1, source_target_pairs={{0,1},{1,0},{2,3},{3,2},{4,5},{5,4},{6,7},{7,6},{8,9},{9,8},{10,11... | collective-permute-start | bytes 1572872 | tf_op jit(solution)/shard_map/ppermute | solution.py:163
  74.5 0.6 dynamic-slice_bitcast_fusion.1
  75.1 1.4 %dynamic-slice_bitcast_fusion.2 = (f32[8,512]{1,0:T(8,128)}, f32[8,512]{1,0:T(8,128)}) fusion(f32[4,8,512]{2,1,0:T(8,128)} %get-tuple-element.4, s32[]{:T(128)S(6)} %select_n.110, f32[4,8,512]{2,1,0:T(8,128)S(1)} %get-tuple-element.6, f32[4,8,512]{2,1,0:T(8,128)} %dynamic-slice_bitcast_fusion), kind=kLoop, calls=%fused_computation.69 | loop fusion | flops 28672 | bytes 81924 | tf_op jit(solution)/shard_map/jit(dynamic_index_in_dim)/squeeze | solution.py:157
  76.5 3.3 %fusion.15 = f32[1024,512]{1,0:T(8,128)} fusion(bf16[512,512]{1,0:T(8,128)(2,1)S(1)} %bitcast.93, bf16[1024,1024]{1,0:T(8,128)(2,1)} %copy-done.1), kind=kOutput, calls=%fused_computation.16 | convolution fusion | flops 536870912 | bytes 3670016 | tf_op jit(solution)/shard_map/dot_general | solution.py:186
  79.8 0.0 collective-permute-done.4
  79.8 8.7 %fusion.11 = f32[1024,2048]{1,0:T(8,128)} fusion(bf16[1024,2048]{1,0:T(8,128)(2,1)} %param.24, f32[1024,512]{1,0:T(8,128)} %fusion.15, bf16[512,512]{1,0:T(8,128)(2,1)S(1)} %collective-permute-done.4, bf16[1024,1024]{1,0:T(8,128)(2,1)} %copy-done.1), kind=kOutput, calls=%fused_computation.11 | convolution fusion | flops 2685403136 | bytes 14155776 | tf_op jit(solution)/shard_map/dot_general | solution.py:190
  88.5 21.1 %add_bitcast_fusion = f32[1,1,1024,2048]{3,2,1,0:T(8,128)} fusion(f32[2048]{0:T(1024)S(1)} %copy-done.11, bf16[2048,2048]{1,0:T(8,128)(2,1)} %param.26, f32[1024,2048]{1,0:T(8,128)} %fusion.11, f32[2048]{0:T(1024)S(1)} %copy-done.12, bf16[1024,512]{1,0:T(8,128)(2,1)} %fusion.13, bf16[1024,2048]{1,0:T(8,128)(2,1)} %param.24), kind=kOutput, calls=%fused_computation.1 | convolution fusion | flops 10747904000 | bytes 28327936 | tf_op jit(solution)/shard_map/dot_general | solution.py:192
  (16 shorter events, 0.0 us)
Async XLA Ops:
  0.6 4.4 %copy-start = (bf16[2048,512]{1,0:T(8,128)(2,1)S(1)}, bf16[2048,512]{1,0:T(8,128)(2,1)}, u32[]{:S(2)}) copy-start(bf16[2048,512]{1,0:T(8,128)(2,1)} %param.20) | copy-start | bytes 6291460
  2.9 6.1 %collective-permute-start = (bf16[16,4,8,512]{3,2,1,0:T(8,128)(2,1)}, bf16[16,4,8,512]{3,2,1,0:T(8,128)(2,1)}, u32[]{:S(2)}, u32[]{:S(2)}) collective-permute-start(bf16[16,4,8,512]{3,2,1,0:T(8,128)(2,1)} %fusion.20), channel_id=1, source_target_pairs={{0,1},{1,0},{2,3},{3,2},{4,5},{5,4},{6,7},{7,6},{8,9},{9,8},{10,11... | collective-permute-start | bytes 1572872 | tf_op jit(solution)/shard_map/ppermute | solution.py:138
  5.0 14.1 %copy-start.9 = (s32[1,1,8,128]{3,2,1,0:T(8,128)S(1)}, s32[1,1,8,128]{3,2,1,0:T(8,128)}, u32[]{:S(2)}) copy-start(s32[1,1,8,128]{3,2,1,0:T(8,128)} %param.21) | copy-start | bytes 12292
  5.0 14.1 %copy-start.10 = (s32[1,1,8]{2,1,0:T(1,128)S(1)}, s32[1,1,8]{2,1,0:T(1,128)}, u32[]{:S(2)}) copy-start(s32[1,1,8]{2,1,0:T(1,128)} %param.22) | copy-start | bytes 100
  9.0 27.1 %copy-start.8 = (s32[1,1,4096]{2,1,0:T(1,128)S(1)}, s32[1,1,4096]{2,1,0:T(1,128)}, u32[]{:S(2)}) copy-start(s32[1,1,4096]{2,1,0:T(1,128)} %param.18) | copy-start | bytes 49156
  9.0 27.4 %copy-start.2 = (s32[1,1,1024]{2,1,0:T(1,128)S(1)}, s32[1,1,1024]{2,1,0:T(1,128)}, u32[]{:S(2)}) copy-start(s32[1,1,1024]{2,1,0:T(1,128)} %param.19) | copy-start | bytes 12292
  11.4 18.9 %all-to-all-start = ((bf16[16,4,8,512]{3,2,1,0:T(8,128)(2,1)}), bf16[16,4,8,512]{3,2,1,0:T(8,128)(2,1)}, u32[]{:S(2)}, u32[]{:S(2)}) async-start(bf16[16,4,8,512]{3,2,1,0:T(8,128)(2,1)} %fusion.17), calls=%async_computation | async-start | bytes 1048576 | tf_op jit(solution)/shard_map/all_to_all | solution.py:140
  20.5 33.7 %copy-start.4 = (f32[64,512]{1,0:T(8,128)S(1)}, f32[64,512]{1,0:T(8,128)}, u32[]{:S(2)}) copy-start(f32[64,512]{1,0:T(8,128)} %param.17) | copy-start | bytes 393220
  20.5 36.1 %copy-start.5 = (f32[64,512]{1,0:T(8,128)S(1)}, f32[64,512]{1,0:T(8,128)}, u32[]{:S(2)}) copy-start(f32[64,512]{1,0:T(8,128)} %param.15) | copy-start | bytes 393220
  30.3 27.0 %all-to-all-start.2 = ((bf16[8,128,512]{2,1,0:T(8,128)(2,1)}), bf16[8,128,512]{2,1,0:T(8,128)(2,1)S(1)}, u32[]{:S(2)}, u32[]{:S(2)}) async-start(bf16[8,128,512]{2,1,0:T(8,128)(2,1)} %select_select_fusion), calls=%async_computation.2 | async-start | bytes 2097152 | tf_op jit(solution)/shard_map/all_to_all | solution.py:171
  36.4 20.8 %copy-start.6 = (f32[64,512]{1,0:T(8,128)S(1)}, f32[64,512]{1,0:T(8,128)}, u32[]{:S(2)}) copy-start(f32[64,512]{1,0:T(8,128)} %param.16) | copy-start | bytes 393220
  36.4 25.6 %copy-start.13 = (s32[1,1,8,128]{3,2,1,0:T(8,128)S(1)}, s32[1,1,8,128]{3,2,1,0:T(8,128)}, u32[]{:S(2)}) copy-start(s32[1,1,8,128]{3,2,1,0:T(8,128)} %param.23) | copy-start | bytes 12292
  46.7 1.3 %copy-start.1 = (bf16[1024,1024]{1,0:T(8,128)(2,1)}, bf16[1024,1024]{1,0:T(8,128)(2,1)S(1)}, u32[]{:S(2)}) copy-start(bf16[1024,1024]{1,0:T(8,128)(2,1)S(1)} %shard_map.165) | copy-start | bytes 6291460
  49.1 5.7 %collective-permute-start.3 = (f32[32,512]{1,0:T(8,128)S(1)}, f32[32,512]{1,0:T(8,128)S(1)}, u32[]{:S(2)}, u32[]{:S(2)}) collective-permute-start(f32[32,512]{1,0:T(8,128)S(1)} %bitcast.97), channel_id=1, source_target_pairs={{0,2},{1,3},{2,4},{3,5},{4,6},{5,7},{6,0},{7,1},{8,10},{9,11},{10,... | collective-permute-start | bytes 196616 | tf_op jit(solution)/shard_map/ppermute | solution.py:143
  50.6 6.0 %collective-permute-start.2 = (f32[32,512]{1,0:T(8,128)S(1)}, f32[32,512]{1,0:T(8,128)S(1)}, u32[]{:S(2)}, u32[]{:S(2)}) collective-permute-start(f32[32,512]{1,0:T(8,128)S(1)} %bitcast.98), channel_id=1, source_target_pairs={{0,4},{1,5},{2,6},{3,7},{4,0},{5,1},{6,2},{7,3},{8,12},{9,13},{10,... | collective-permute-start | bytes 196616 | tf_op jit(solution)/shard_map/ppermute | solution.py:143
  53.0 3.6 %collective-permute-start.1 = (f32[32,512]{1,0:T(8,128)S(1)}, f32[32,512]{1,0:T(8,128)S(1)}, u32[]{:S(2)}, u32[]{:S(2)}) collective-permute-start(f32[32,512]{1,0:T(8,128)S(1)} %bitcast.99), channel_id=1, source_target_pairs={{0,6},{1,7},{2,0},{3,1},{4,2},{5,3},{6,4},{7,5},{8,14},{9,15},{10,... | collective-permute-start | bytes 196616 | tf_op jit(solution)/shard_map/ppermute | solution.py:143
  57.3 1.2 %copy-start.3 = (bf16[8,128,512]{2,1,0:T(8,128)(2,1)}, bf16[8,128,512]{2,1,0:T(8,128)(2,1)S(1)}, u32[]{:S(2)}) copy-start(bf16[8,128,512]{2,1,0:T(8,128)(2,1)S(1)} %all-to-all-done.2) | copy-start | bytes 3145732
  58.5 13.9 %all-to-all-start.1 = ((bf16[16,32,512]{2,1,0:T(8,128)(2,1)}), bf16[16,32,512]{2,1,0:T(8,128)(2,1)S(1)}, u32[]{:S(2)}, u32[]{:S(2)}) async-start(bf16[16,32,512]{2,1,0:T(8,128)(2,1)} %broadcast_in_dim.33), calls=%async_computation.1 | async-start | bytes 1048576 | tf_op jit(solution)/shard_map/all_to_all | solution.py:161
  62.1 3.5 %copy-start.7 = (f32[64,512]{1,0:T(8,128)S(1)}, f32[64,512]{1,0:T(8,128)}, u32[]{:S(2)}) copy-start(f32[64,512]{1,0:T(8,128)} %param.16) | copy-start | bytes 393220
  72.3 7.5 %collective-permute-start.4 = (bf16[512,512]{1,0:T(8,128)(2,1)S(1)}, bf16[512,512]{1,0:T(8,128)(2,1)S(1)}, u32[]{:S(2)}, u32[]{:S(2)}) collective-permute-start(bf16[512,512]{1,0:T(8,128)(2,1)S(1)} %bitcast.92), channel_id=1, source_target_pairs={{0,1},{1,0},{2,3},{3,2},{4,5},{5,4},{6,7},{7,6},{8,9},{9,8},{10,11... | collective-permute-start | bytes 1572872 | tf_op jit(solution)/shard_map/ppermute | solution.py:163
  79.8 8.7 %copy-start.11 = (f32[2048]{0:T(1024)S(1)}, f32[2048]{0:T(1024)}, u32[]{:S(2)}) copy-start(f32[2048]{0:T(1024)} %param.27) | copy-start | bytes 24580
  79.8 8.7 %copy-start.12 = (f32[2048]{0:T(1024)S(1)}, f32[2048]{0:T(1024)}, u32[]{:S(2)}) copy-start(f32[2048]{0:T(1024)} %param.25) | copy-start | bytes 24580

commit v2 on v0

v2 whole, which is shorter than its diff:
```python
import functools

import jax
import jax.numpy as jnp
from jax import lax
from jax.experimental import pallas as pl
from jax.experimental.pallas import tpu as pltpu
from jax.sharding import PartitionSpec as P

beta_first = 0.9
beta_second = 0.999
adam_count = 10
learning_rate = 0.05
weight_decay = 0.01
epsilon = 1e-08

BF16 = jnp.bfloat16
F32 = jnp.float32
I32 = jnp.int32
I16 = jnp.int16
VMEM = pl.BlockSpec(memory_space=pltpu.VMEM)
HBM = pl.BlockSpec(memory_space=pltpu.HBM)
MIB = 1 << 20
CHUNK = 512
BAGS = 256
LANES = 128
TILE = 256
ROWS = 512
PIECE = 512
LAST = (((1,), (1,)), ((), ()))
FIRST = (((0,), (0,)), ((), ()))


def adamw(master, first, second, grad):
    first_new = beta_first * first + (1.0 - beta_first) * grad
    second_new = beta_second * second + (1.0 - beta_second) * grad * grad
    corrected = first_new / (1.0 - beta_first**adam_count)
    scaled = second_new / (1.0 - beta_second**adam_count)
    master_new = master - learning_rate * (
        corrected / (jnp.sqrt(scaled) + epsilon) + weight_decay * master
    )
    return (master_new, first_new, second_new)


def dot(a, b):
    return jnp.dot(a, b, preferred_element_type=F32)


def dot_on(a, b, dims):
    return lax.dot_general(a, b, dims, preferred_element_type=F32)


def params(mib):
    return pltpu.CompilerParams(vmem_limit_bytes=mib * MIB)


def cost(flops, moved):
    return pl.CostEstimate(flops=flops, bytes_accessed=moved, transcendentals=0)


def in_hbm(array):
    return pltpu.with_memory_space_constraint(array, pltpu.HBM)


def my_place():
    place = lax.axis_index("table")
    return lax.rem(place, 2), lax.div(place, 2)


def after(first, *others):
    return lax.optimization_barrier((first, *others))[1:]


def load_half(grad_ref, side, held_ref, sems):
    steps = sems.shape[0]
    part = grad_ref.shape[0] // steps
    copies = []
    for i in range(steps):
        here = pl.ds(i * part, part)
        copy = pltpu.make_async_copy(
            grad_ref.at[here, :, side], held_ref.at[here], sems.at[i]
        )
        copy.start()
        copies.append(copy)
    return copies


def half_kernel(grad_ref, out_ref, held_ref, sems):
    core, _ = my_place()
    copies = load_half(grad_ref, 1 - core, held_ref, sems)
    rows, part = out_ref.shape[0] // len(copies), held_ref.shape[0] // len(copies)
    for i, copy in enumerate(copies):
        copy.wait()
        mine = held_ref[i * part : (i + 1) * part].reshape(rows, out_ref.shape[1])
        out_ref[i * rows : (i + 1) * rows, :] = mine.astype(BF16)


def chip_kernel(grad_ref, other_ref, out_ref, held_ref, sems):
    core, _ = my_place()
    copies = load_half(grad_ref, core, held_ref, sems)
    rows, part = out_ref.shape[0] // len(copies), held_ref.shape[0] // len(copies)
    for i, copy in enumerate(copies):
        copy.wait()
        here = slice(i * rows, (i + 1) * rows)
        mine = held_ref[i * part : (i + 1) * part].reshape(rows, out_ref.shape[1])
        out_ref[here, :] = (mine + other_ref[here, :].astype(F32)).astype(BF16)


def half_rows(grad, other=None):
    n_dp, lines, _, own, width = grad.shape
    total = n_dp * lines * own
    return pl.pallas_call(
        half_kernel if other is None else chip_kernel,
        out_shape=jax.ShapeDtypeStruct((total, width), BF16),
        in_specs=[HBM] if other is None else [HBM, VMEM],
        out_specs=VMEM,
        scratch_shapes=[
            pltpu.VMEM((n_dp, lines, own, width), F32), pltpu.SemaphoreType.DMA((4,))
        ],
        compiler_params=params(16),
        cost_estimate=cost(0, total * width * 6),
    )(in_hbm(grad), *(() if other is None else (other,)))


def sum_kernel(parts_ref, out_ref):
    total = parts_ref[0].astype(F32)
    for i in range(1, parts_ref.shape[0]):
        total = total + parts_ref[i].astype(F32)
    out_ref[...] = total


def sum_parts(parts):
    return pl.pallas_call(
        sum_kernel,
        out_shape=jax.ShapeDtypeStruct(parts.shape[1:], F32),
        in_specs=[VMEM],
        out_specs=VMEM,
        compiler_params=params(16),
        cost_estimate=cost(parts.size, parts.size * 2),
    )(parts)


def update_kernel(
    share_ref, in1_ref, in2_ref, in3_ref, master_ref, first_ref, second_ref,
    spread_ref, new_master_ref, new_first_ref, new_second_ref,
):
    core, line = my_place()
    lines, _, own, width = master_ref.shape
    grad = (share_ref[...] + in1_ref[...]) + (in2_ref[...] + in3_ref[...])
    rows = lines * own
    master, first, second = adamw(
        master_ref[:, core].reshape(rows, width),
        first_ref[:, core].reshape(rows, width),
        second_ref[:, core].reshape(rows, width),
        grad,
    )
    fresh = master.astype(BF16)
    for i in range(spread_ref.shape[0]):
        spread_ref[i] = fresh
    for whole, out_ref in (
        (master, new_master_ref), (first, new_first_ref), (second, new_second_ref)
    ):
        picked = whole[:own]
        for i in range(1, lines):
            picked = jnp.where(line == i, whole[i * own : (i + 1) * own], picked)
        out_ref[...] = picked


def update(share, shares_in, master, first, second, n_dp, lines, own):
    width = master.shape[1]
    rows = [a.reshape(lines, 2, own, width) for a in (master, first, second)]
    mine = jax.ShapeDtypeStruct((own, width), F32)
    return pl.pallas_call(
        update_kernel,
        out_shape=(
            jax.ShapeDtypeStruct((n_dp, lines * own, width), BF16), mine, mine, mine,
        ),
        in_specs=[VMEM] * 7,
        out_specs=(VMEM,) * 4,
        compiler_params=params(16),
        cost_estimate=cost(20 * share.size, 60 * share.size),
    )(share, *shares_in, *rows)


def pick_kernel(
    other_side, index_hbm, count_hbm, table_hbm, out_ref, index_ref, count_ref, table_ref, sems
):
    copies = [
        pltpu.make_async_copy(source, target, sems.at[i])
        for i, (source, target) in enumerate(
            ((index_hbm, index_ref), (count_hbm, count_ref), (table_hbm, table_ref))
        )
    ]
    for copy in copies:
        copy.start()
    core, line = my_place()
    side = 1 - core if other_side else core
    askers, slots = index_ref.shape
    lines = askers // 2
    rows = lax.broadcasted_iota(I16, (table_ref.shape[0], slots), 0)
    slot = lax.broadcasted_iota(I32, (1, slots), 1)
    each = lax.broadcasted_iota(I32, (1, askers), 1)
    copies[0].wait()
    copies[1].wait()
    for s in range(lines):
        asker = lax.rem(line + s, lines) * 2 + side
        used = jnp.sum(jnp.where(each == asker, count_ref[...], 0), axis=1, keepdims=True)
        wanted = index_ref[pl.ds(asker, 1), :]
        wanted = jnp.where(slot < used, wanted, -1).astype(I16)
        hit = jnp.where(rows == wanted, BF16(1), BF16(0))
        if s == 0:
            copies[2].wait()
        found = dot_on(hit, table_ref[...], FIRST)
        out_ref[s * slots : (s + 1) * slots, :] = found.astype(BF16)


def pick(index, counts, table, other_side):
    width = table.shape[1]
    rows = index.size // 2
    return pl.pallas_call(
        functools.partial(pick_kernel, other_side),
        out_shape=jax.ShapeDtypeStruct((rows, width), BF16),
        in_specs=[HBM, HBM, HBM],
        out_specs=VMEM,
        scratch_shapes=[
            pltpu.VMEM(index.shape, I32),
            pltpu.VMEM(counts.shape, I32),
            pltpu.VMEM(table.shape, BF16),
            pltpu.SemaphoreType.DMA((3,)),
        ],
        compiler_params=params(24),
        cost_estimate=cost(index.size * table.size, table.size * 2),
    )(in_hbm(index), in_hbm(counts), in_hbm(table))


def merge_kernel(near_ref, far_ref, *out_refs):
    slots = near_ref.shape[0] // len(out_refs)
    for s, out_ref in enumerate(out_refs):
        out_ref[:slots, :] = near_ref[s * slots : (s + 1) * slots, :]
        out_ref[slots:, :] = far_ref[s * slots : (s + 1) * slots, :]


def merge(near, far, lines):
    out = jax.ShapeDtypeStruct((2 * near.shape[0] // lines, near.shape[1]), BF16)
    return pl.pallas_call(
        merge_kernel,
        out_shape=(out,) * lines,
        in_specs=[VMEM, VMEM],
        out_specs=(VMEM,) * lines,
        compiler_params=params(16),
        cost_estimate=cost(0, near.size * 8),
    )(near, far)


def cold_kernel(sample_ref, *refs):
    rows_in, (w_hbm, b_ref, pre_hbm, w_ref, held_ref, sem, out_sems) = refs[:-7], refs[-7:]
    core, line = my_place()
    lines = len(rows_in)
    batch, width = held_ref.shape[0], rows_in[0].shape[1]
    copy = pltpu.make_async_copy(w_hbm.at[pl.ds(width, width)], w_ref, sem)
    copy.start()
    samples = []
    for s in range(lines):
        owner = lax.rem(line + lines - s, lines) * 2
        samples.append(
            jnp.concatenate(
                [sample_ref[pl.ds(owner + side, 1), :] for side in (core, 1 - core)], axis=1
            )
        )
    bag = lax.broadcasted_iota(I16, (TILE, samples[0].shape[1]), 0)

    def leave(i):
        here = pl.ds(pl.multiple_of(i * TILE, TILE), TILE)
        return pltpu.make_async_copy(held_ref.at[here], pre_hbm.at[here], out_sems.at[i])

    def step(i, _):
        pool = None
        for sample, rows_ref in zip(samples, rows_in, strict=True):
            hit = bag == (sample - i * TILE).astype(I16)
            part = dot(jnp.where(hit, BF16(1), BF16(0)), rows_ref[...])
            pool = part if pool is None else pool + part

        @pl.when(i == 0)
        def _():
            copy.wait()

        here = pl.ds(pl.multiple_of(i * TILE, TILE), TILE)
        held_ref[here, :] = (dot(pool.astype(BF16), w_ref[...]) + b_ref[...]).astype(BF16)
        leave(i).start()
        return 0

    lax.fori_loop(0, batch // TILE, step, 0)
    for i in range(batch // TILE):
        leave(i).wait()


def cold_half(samples, rows_in, w_in, b_in, batch):
    hidden = w_in.shape[1]
    width = rows_in[0].shape[1]
    return pl.pallas_call(
        cold_kernel,
        out_shape=pltpu.HBM((batch, hidden), BF16),
        in_specs=[VMEM] * (len(rows_in) + 1) + [HBM, VMEM],
        out_specs=HBM,
        scratch_shapes=[
            pltpu.VMEM((width, hidden), BF16),
            pltpu.VMEM((batch, hidden), BF16),
            pltpu.SemaphoreType.DMA(()),
            pltpu.SemaphoreType.DMA((batch // TILE,)),
        ],
        compiler_params=params(24),
        cost_estimate=cost(2 * batch * width * (hidden + samples.size), batch * hidden * 2),
    )(samples, *rows_in, in_hbm(w_in), b_in.reshape(1, hidden))


def count_kernel(low_block, own, ids_ref, lengths_ref, out_ref, total_ref):
    core, _ = my_place()
    bags, width = out_ref.shape
    row = lax.broadcasted_iota(I32, (BAGS, BAGS), 0)
    col = lax.broadcasted_iota(I32, (BAGS, BAGS), 1)
    upto = (col <= row).astype(BF16)
    before = (col < row).astype(BF16)
    rows = lax.broadcasted_iota(I16, (width, CHUNK), 0)
    offset = F32(0.0)
    if low_block:
        offset = jnp.sum(lengths_ref[:, : low_block * BAGS].astype(F32))
    for k in range(bags // BAGS):
        at = (low_block + k) * BAGS
        lengths = lengths_ref[:, at : at + BAGS].astype(F32)
        spread = jnp.broadcast_to(lengths, (LANES, BAGS)).astype(BF16)
        end = offset + dot_on(upto, spread, LAST)
        start = offset + dot_on(before, spread, LAST)
        following = offset + jnp.sum(lengths)
        lowest, highest = offset.astype(I32), following.astype(I32)
        offset = following
        total_ref[...] = jnp.zeros_like(total_ref)

        def step(j, _, start=start, end=end):
            here = pl.multiple_of(j * CHUNK, CHUNK)
            ids = ids_ref[:, pl.ds(here, CHUNK)]
            far = lax.div(ids, own) % 2 != core
            places = lax.div(ids, 2 * own) * own + lax.rem(ids, own)
            places = jnp.where(far, places + width // 2, places).astype(I16)
            hits = jnp.where(rows == places, BF16(1), BF16(0))
            lane = (here + lax.broadcasted_iota(I32, (BAGS, LANES), 1)).astype(F32)
            member = jnp.concatenate(
                [
                    jnp.where((start <= lane + o) & (lane + o < end), 1.0, 0.0)
                    for o in range(0, CHUNK, LANES)
                ],
                axis=1,
            ).astype(BF16)
            total_ref[...] += dot_on(member, hits, LAST)
            return 0

        lax.fori_loop(lowest // CHUNK, (highest + CHUNK - 1) // CHUNK, step, 0)
        out_ref[k * BAGS : (k + 1) * BAGS, :] = total_ref[...].astype(BF16)


def count_matrix(ids, lengths, width, own, low_block, blocks):
    return pl.pallas_call(
        functools.partial(count_kernel, low_block, own),
        out_shape=pltpu.HBM((blocks * BAGS, width), BF16),
        grid=(1,),
        in_specs=[VMEM, VMEM],
        out_specs=pl.BlockSpec((blocks * BAGS, width), lambda i: (0, 0)),
        scratch_shapes=[pltpu.VMEM((BAGS, width), F32)],
        compiler_params=params(24),
        cost_estimate=cost(3 * blocks * 2 * BAGS * CHUNK * width, 2 * blocks * BAGS * width),
    )(ids, lengths)


def own_kernel(
    low_hbm, high_hbm, own_ref, w_in_hbm, pool_ref, count_ref, w_hot_ref, held_ref, sems
):
    half, width = own_ref.shape
    low, high = low_hbm.shape[0], high_hbm.shape[0]
    mine, rest = pl.ds(0, half), pl.ds(half, half)
    copies = [
        pltpu.make_async_copy(source, target, sems.at[i])
        for i, (source, target) in enumerate(
            (
                (low_hbm.at[:, mine], held_ref.at[pl.ds(0, low)]),
                (high_hbm.at[:, mine], held_ref.at[pl.ds(low, high)]),
                (low_hbm.at[:, rest], count_ref.at[pl.ds(0, low)]),
                (high_hbm.at[:, rest], count_ref.at[pl.ds(low, high)]),
                (w_in_hbm.at[pl.ds(0, width)], w_hot_ref),
            )
        )
    ]
    for copy in copies:
        copy.start()
    copies[0].wait()
    copies[1].wait()

    def step(i, _):
        here = pl.ds(pl.multiple_of(i * TILE, TILE), TILE)
        pool_ref[here, :] = dot(held_ref[here, :], own_ref[...])
        return 0

    lax.fori_loop(0, (low + high) // TILE, step, 0)
    for copy in copies[2:]:
        copy.wait()


def own_pool(low, high, fresh_own, w_in):
    half, width = fresh_own.shape
    batch, hidden = low.shape[0] + high.shape[0], w_in.shape[1]
    return pl.pallas_call(
        own_kernel,
        out_shape=(
            pltpu.VMEM((batch, width), F32),
            pltpu.VMEM((batch, half), BF16),
            pltpu.VMEM((width, hidden), BF16),
        ),
        in_specs=[HBM, HBM, VMEM, HBM],
        out_specs=(VMEM, VMEM, VMEM),
        scratch_shapes=[pltpu.VMEM((batch, half), BF16), pltpu.SemaphoreType.DMA((5,))],
        compiler_params=params(16),
        cost_estimate=cost(2 * batch * half * width, 3 * batch * width * 4),
    )(in_hbm(low), in_hbm(high), fresh_own, in_hbm(w_in))


def mlp_kernel(
    pool_ref, count_ref, other_ref, w_hot_ref, pre_hbm, w_out_hbm, b_ref, out_hbm,
    hidden_ref, w_out_ref, pre_ref, out_ref, pre_sems, w_sems, out_sems,
):
    tiles, rows, _ = pre_ref.shape
    pieces, _, wide = w_out_ref.shape

    def load_pre(i):
        here = pl.ds(pl.multiple_of(i * rows, rows), rows)
        return pltpu.make_async_copy(pre_hbm.at[here], pre_ref.at[i], pre_sems.at[i])

    def load_w(n):
        here = pl.ds(pl.multiple_of(n * wide, wide), wide)
        return pltpu.make_async_copy(w_out_hbm.at[:, here], w_out_ref.at[n], w_sems.at[n])

    def leave(n):
        here = pl.ds(pl.multiple_of(n * wide, wide), wide)
        slot = lax.rem(n, 2)
        return pltpu.make_async_copy(out_ref.at[slot], out_hbm.at[:, here], out_sems.at[slot])

    for i in range(tiles):
        load_pre(i).start()
    for n in range(pieces):
        load_w(n).start()

    def first_layer(i, _):
        here = pl.ds(pl.multiple_of(i * rows, rows), rows)
        pool = pool_ref[here, :] + dot(count_ref[here, :], other_ref[...])
        load_pre(i).wait()
        pre = dot(pool.astype(BF16), w_hot_ref[...]) + pre_ref[i].astype(F32)
        hidden_ref[here, :] = jnp.maximum(pre, 0.0).astype(BF16)
        return 0

    lax.fori_loop(0, tiles, first_layer, 0)

    def second_layer(n, _):
        load_w(n).wait()

        @pl.when(n >= 2)
        def _():
            leave(n - 2).wait()

        here = pl.ds(pl.multiple_of(n * wide, wide), wide)
        out_ref[lax.rem(n, 2)] = dot(hidden_ref[...], w_out_ref[n]) + b_ref[:, here]
        leave(n).start()
        return 0

    lax.fori_loop(0, pieces, second_layer, 0)
    leave(pieces - 2).wait()
    leave(pieces - 1).wait()


def mlp(pool, counts, fresh_other, w_hot, pre, w_out, b_out):
    batch, hidden = pre.shape
    wide = w_out.shape[1]
    half, width = fresh_other.shape
    tiles, pieces = batch // ROWS, wide // PIECE
    return pl.pallas_call(
        mlp_kernel,
        out_shape=jax.ShapeDtypeStruct((batch, wide), F32),
        in_specs=[VMEM] * 4 + [HBM, HBM, VMEM],
        out_specs=HBM,
        scratch_shapes=[
            pltpu.VMEM((batch, hidden), BF16),
            pltpu.VMEM((pieces, hidden, PIECE), BF16),
            pltpu.VMEM((tiles, ROWS, hidden), BF16),
            pltpu.VMEM((2, batch, PIECE), F32),
            pltpu.SemaphoreType.DMA((tiles,)),
            pltpu.SemaphoreType.DMA((pieces,)),
            pltpu.SemaphoreType.DMA((2,)),
        ],
        compiler_params=params(36),
        cost_estimate=cost(
            2 * batch * (half * width + width * hidden + hidden * wide), batch * wide * 4
        ),
    )(
        pool, counts, fresh_other, w_hot, in_hbm(pre), in_hbm(w_out), b_out.reshape(1, wide)
    )


def on_device(
    hot_grad,
    first_moment,
    second_moment,
    hot_master,
    hot_ids,
    hot_lengths,
    cold_table,
    cold_index,
    cold_count,
    cold_sample,
    w_in,
    b_in,
    w_out,
    b_out,
):
    width = cold_table.shape[1]
    batch = hot_lengths.shape[2]
    hot = hot_grad.shape[2]
    n_dp, n_table = lax.axis_size("dp"), lax.axis_size("table")
    lines = n_table // 2
    own = hot // (n_dp * n_table)
    swap = [(i, i ^ 1) for i in range(n_table)]

    def along(array, step):
        pairs = [(i, (i + 2 * step) % n_table) for i in range(n_table)]
        return lax.ppermute(array, "table", pairs)

    grad = hot_grad[0, 0].reshape(n_dp, lines, 2, own, width)
    send = half_rows(grad)
    other = lax.ppermute(send, "table", swap)
    index, counts = cold_index[0, 0], cold_count[0]
    (index_far,) = after(send, index)
    far = pick(index_far, counts, cold_table, True)
    other, far = lax.optimization_barrier((other, far))
    chip = half_rows(grad, other)

    parts = lax.all_to_all(
        chip.reshape(n_dp, lines * own, width), "dp", split_axis=0, concat_axis=0, tiled=True
    )
    far_in = lax.ppermute(far, "table", swap)
    (index_near,) = after(chip, index)
    near = pick(index_near, counts, cold_table, False)
    blocks = merge(near, far_in, lines)
    rows_in = [along(blocks[s], s) if s in (1, lines - 1) else blocks[s] for s in range(lines)]

    ids, lengths = hot_ids[0], hot_lengths[0]
    early = batch // BAGS * 3 // 4
    (ids_now,) = after(blocks[0], ids)
    count_low = count_matrix(ids_now, lengths, hot, own, 0, early)
    parts, *_ = lax.optimization_barrier((parts, count_low, rows_in[1], rows_in[-1]))
    share = sum_parts(parts)
    shares_in = [along(share, s) for s in range(1, lines)]
    spread, new_master, new_first, new_second = update(
        share, shares_in, hot_master, first_moment, second_moment, n_dp, lines, own
    )
    fresh_own = lax.all_to_all(spread, "dp", split_axis=0, concat_axis=0, tiled=True)
    samples, ids_late, *middle = after(spread, cold_sample[0, 0], ids, *rows_in[2:-1])
    for s, block in enumerate(middle):
        rows_in[2 + s] = along(block, 2 + s)
    count_high = count_matrix(ids_late, lengths, hot, own, early, batch // BAGS - early)
    pre = cold_half(samples, rows_in, w_in, b_in, batch)
    fresh_own, *_ = lax.optimization_barrier((fresh_own, pre, count_high))
    fresh_own = fresh_own.reshape(hot // 2, width)
    fresh_other = lax.ppermute(fresh_own, "table", swap)
    pool, counts_other, w_hot = own_pool(count_low, count_high, fresh_own, w_in)
    fresh_other, pool = lax.optimization_barrier((fresh_other, pool))
    result = mlp(pool, counts_other, fresh_other, w_hot, pre, w_out, b_out)
    return (result[None, None], new_master, new_first, new_second)


def solution(mesh):
    return jax.shard_map(
        on_device,
        mesh=mesh,
        in_specs=(
            P("dp", "table", None, None),
            P("dp", None),
            P("dp", None),
            P("dp", None),
            P("dp", "table", None),
            P("dp", "table", None),
            P("table", None),
            P("dp", "table", None, None),
            P("dp", "table", None),
            P("dp", "table", None, None),
            P(),
            P(),
            P(),
            P(),
        ),
        out_specs=(
            P("dp", "table", None, None),
            P(("dp", "table"), None),
            P(("dp", "table"), None),
            P(("dp", "table"), None),
        ),
        check_vma=False,
    )
```

time: 305 us -> 77.9 us (0.26)
  waiting for transfers between devices: 179 us -> 4.38 us
  other arithmetic: 77.7 us -> 0 us
  Pallas kernels: 0 us -> 44.8 us
  matrix products: 21.5 us -> 0 us
  starting transfers between devices: 6.67 us -> 27.3 us
  between operations: 13.9 us -> 0.97 us
  local copies, waits for them, and re-layouts: 5.61 us -> 0.04 us
    reduce_scatter x1 -> x0, waiting for transfers between devices: 74.5 us -> none  [on_device(): shard_grad = lax.psum_scatter(grad, 'dp', scatter_dimension=0, tiled=True)]
    scatter-add x2 -> x0, other arithmetic: 65.4 us -> none  [the longest x1 57.2 us: on_device(): jax.ops.segment_sum(looked.astype(jnp.float32), segment, num_segments=bat...]
    psum x1 -> x0, waiting for transfers between devices: 52.4 us -> none  [on_device(): shard_grad = lax.psum(shard_grad, 'table')]
    all_gather x1 -> x0, waiting for transfers between devices: 51.5 us -> none  [on_device(): fresh_all = lax.all_gather(fresh, ('dp', 'table'), axis=0, tiled=True)]
    pallas_call x0 -> x12, Pallas kernels: none -> 44.8 us  [the longest x1 16.5 us: mlp(): pl.pallas_call(mlp_kernel, out_shape=jax.ShapeDtypeStruct((batch, wide),...]
    dot_general x1 -> x0, matrix products: 21.5 us -> none  [on_device(): result = jnp.dot(hidden, w_out, preferred_element_type=jnp.float32) + b_out]
    ppermute x0 -> x9, starting transfers between devices: none -> 13.1 us  [the longest x6 6.62 us: along(): return lax.ppermute(array, 'table', pairs)]
    all_to_all x1 -> x2, starting transfers between devices: 6.59 us -> 14.3 us  [the longest x1 7.69 us: on_device(): lax.all_to_all(chip.reshape(n_dp, lines * own, width), 'dp', split_axis=0...]
  transfers between devices with their start and end apart: 4 -> 11, of which waited for: 3 -> 3; matrix products, arithmetic and copies ran while one was open for 8% -> 0% of each run, Pallas kernels for 0% -> 34%
where the time goes in v2:
time: 77.9 us; the launch traced here: 77.5 us
  Pallas kernels  44.8 us (58%)
  starting transfers between devices  27.3 us (35%)
  waiting for transfers between devices  4.38 us (6%)
  between operations  0.97 us (1%)
    pallas_call x1, Pallas kernels, mlp(): pl.pallas_call(mlp_kernel, out_shape=jax.ShapeDtypeStruct((batch, wide),...  16.5 us
    pallas_call x2, Pallas kernels, count_matrix(): pl.pallas_call(functools.partial(count_kernel, low_block, own), out_shape...  8.76 us
    all_to_all x1, starting transfers between devices, on_device(): lax.all_to_all(chip.reshape(n_dp, lines * own, width), 'dp', split_axis=0...  7.69 us
    pallas_call x1, Pallas kernels, cold_half(): pl.pallas_call(cold_kernel, out_shape=pltpu.HBM((batch, hidden), BF16), i...  6.79 us
    ppermute x6, starting transfers between devices, along(): return lax.ppermute(array, 'table', pairs)  6.62 us
    all_to_all x1, starting transfers between devices, on_device(): lax.all_to_all(spread, 'dp', split_axis=0, concat_axis=0, tiled=True)  6.59 us
    pallas_call x2, Pallas kernels, pick(): pl.pallas_call(functools.partial(pick_kernel, other_side), out_shape=jax....  5.87 us
    ppermute x1, starting transfers between devices, on_device(): fresh_other = lax.ppermute(fresh_own, 'table', swap)  4.83 us
  transfers between devices with their start and end apart: 11, of which 3 were waited for; matrix products, arithmetic and copies ran while one was open for 0% of the time, Pallas kernels for 34%

profile of v2, /device:TPU:1, one launch (start us, length us, event | category | flops | bytes accessed | tf_op | source)
XLA Modules:
  0.0 77.5 jit_solution(12994131698477800749)
XLA Ops:
  0.6 1.2 %shard_map.165 = bf16[512,512]{1,0:T(8,128)(2,1)S(1)} custom-call(f32[16,4,2,8,512]{4,3,2,1,0:T(8,128)} %bitcast.26), custom_call_target="tpu_custom_call" | custom-call | bytes 1572864 | tf_op jit(solution)/shard_map/pallas_call | solution.py:112
  1.9 1.5 %collective-permute-start = (bf16[512,512]{1,0:T(8,128)(2,1)S(1)}, bf16[512,512]{1,0:T(8,128)(2,1)S(1)}, u32[]{:S(2)}, u32[]{:S(2)}) collective-permute-start(bf16[512,512]{1,0:T(8,128)(2,1)S(1)} %shard_map.165), channel_id=1, source_target_pairs={{0,1},{1,0},{2,3},{3,2},{4,5},{5,4},{6,7},{7,6},{8,9},{9,8},{10,11... | collective-permute-start | bytes 1572872 | tf_op jit(solution)/shard_map/ppermute | solution.py:534
  3.4 2.9 %shard_map.166 = bf16[512,512]{1,0:T(8,128)(2,1)S(1)} custom-call(s32[8,128]{1,0:T(8,128)} %bitcast.28, s32[1,8]{1,0:T(1,128)} %bitcast.30, bf16[2048,512]{1,0:T(8,128)(2,1)} %table_hbm.3), custom_call_target="tpu_custom_call" | custom-call | flops 1073741824 | bytes 2097152 | tf_op jit(solution)/shard_map/pallas_call | solution.py:220
  6.3 0.0 collective-permute-done.other_ref
  6.3 0.1 collective-permute-start.1
  6.4 2.1 %shard_map.167 = bf16[512,512]{1,0:T(8,128)(2,1)} custom-call(f32[16,4,2,8,512]{4,3,2,1,0:T(8,128)} %bitcast.27, bf16[512,512]{1,0:T(8,128)(2,1)S(1)} %collective-permute-done.other_ref), custom_call_target="tpu_custom_call" | custom-call | bytes 1572864 | tf_op jit(solution)/shard_map/pallas_call | solution.py:112
  8.5 7.7 %all-to-all-start = ((bf16[16,32,512]{2,1,0:T(8,128)(2,1)}), bf16[16,32,512]{2,1,0:T(8,128)(2,1)S(1)}, u32[]{:S(2)}, u32[]{:S(2)}) async-start(bf16[16,32,512]{2,1,0:T(8,128)(2,1)} %bitcast.3), calls=%async_computation | async-start | bytes 1048576 | tf_op jit(solution)/shard_map/all_to_all | solution.py:541
  16.2 0.0 copy-start.3
  16.2 0.0 copy-start.6
  16.2 2.9 %shard_map.168.near_ref = bf16[512,512]{1,0:T(8,128)(2,1)S(1)} custom-call(s32[8,128]{1,0:T(8,128)} %bitcast.29, s32[1,8]{1,0:T(1,128)} %bitcast.31, bf16[2048,512]{1,0:T(8,128)(2,1)} %table_hbm.3), custom_call_target="tpu_custom_call" | custom-call | flops 1073741824 | bytes 2097152 | tf_op jit(solution)/shard_map/pallas_call | solution.py:220
  19.2 0.0 collective-permute-done.1.far_ref
  19.2 0.1 shard_map.169
  19.3 1.4 %collective-permute-start.2 = (bf16[256,512]{1,0:T(8,128)(2,1)S(1)}, bf16[256,512]{1,0:T(8,128)(2,1)S(1)}, u32[]{:S(2)}, u32[]{:S(2)}) collective-permute-start(bf16[256,512]{1,0:T(8,128)(2,1)S(1)} %get-tuple-element.33), channel_id=1, source_target_pairs={{0,2},{1,3},{2,4},{3,5},{4,6},{5,7},{6,0},{7,1},{8,10},{9,11},{10,... | collective-permute-start | bytes 786440 | tf_op jit(solution)/shard_map/ppermute | solution.py:530
  20.6 1.5 %collective-permute-start.3 = (bf16[256,512]{1,0:T(8,128)(2,1)S(1)}, bf16[256,512]{1,0:T(8,128)(2,1)S(1)}, u32[]{:S(2)}, u32[]{:S(2)}) collective-permute-start(bf16[256,512]{1,0:T(8,128)(2,1)S(1)} %get-tuple-element.34), channel_id=1, source_target_pairs={{0,6},{1,7},{2,0},{3,1},{4,2},{5,3},{6,4},{7,5},{8,14},{9,15},{10,... | collective-permute-start | bytes 786440 | tf_op jit(solution)/shard_map/ppermute | solution.py:530
  22.1 0.0 copy-done.3
  22.1 0.0 copy-done.6
  22.1 0.0 copy-start
  22.2 0.0 copy-start.1
  22.2 0.0 copy-start.2
  22.2 6.1 %shard_map.170.low_hbm = bf16[768,1024]{1,0:T(8,128)(2,1)} custom-call(s32[1,4096]{1,0:T(1,128)S(1)} %bitcast.19, s32[1,1024]{1,0:T(1,128)S(1)} %bitcast.23), custom_call_target="tpu_custom_call" | custom-call | flops 2415919104 | bytes 1572864 | tf_op jit(solution)/shard_map/pallas_call | solution.py:361
  28.3 0.0 all-to-all-done.parts_ref
  28.3 0.0 collective-permute-done.2.refs_1_
  28.3 0.0 collective-permute-done.3.refs_3_
  28.3 0.1 shard_map.171.share_ref
  28.4 2.0 %collective-permute-start.6 = (f32[32,512]{1,0:T(8,128)S(1)}, f32[32,512]{1,0:T(8,128)S(1)}, u32[]{:S(2)}, u32[]{:S(2)}) collective-permute-start(f32[32,512]{1,0:T(8,128)S(1)} %shard_map.171.share_ref), channel_id=1, source_target_pairs={{0,6},{1,7},{2,0},{3,1},{4,2},{5,3},{6,4},{7,5},{8,14},{9,15},{10,... | collective-permute-start | bytes 196616 | tf_op jit(solution)/shard_map/ppermute | solution.py:530
  30.4 0.3 collective-permute-start.5
  30.7 0.7 collective-permute-start.4
  31.4 0.4 collective-permute-done.6.in3_ref
  31.7 3.4 %collective-permute-done.5.in2_ref = f32[32,512]{1,0:T(8,128)S(1)} collective-permute-done((f32[32,512]{1,0:T(8,128)S(1)}, f32[32,512]{1,0:T(8,128)S(1)}, u32[]{:S(2)}, u32[]{:S(2)}) %collective-permute-start.5) | collective-permute-done | bytes 65568 | tf_op jit(solution)/shard_map/ppermute | solution.py:530
  35.1 0.6 collective-permute-done.4.in1_ref
  35.7 0.0 copy-done
  35.7 0.0 copy-done.1
  35.7 0.0 copy-done.2
  35.7 0.9 %shard_map.172 = (bf16[16,32,512]{2,1,0:T(8,128)(2,1)}, f32[8,512]{1,0:T(8,128)}, f32[8,512]{1,0:T(8,128)}, f32[8,512]{1,0:T(8,128)}) custom-call(f32[32,512]{1,0:T(8,128)S(1)} %shard_map.171.share_ref, f32[32,512]{1,0:T(8,128)S(1)} %collective-permute-done.4.in1_ref, f32[32,512]{1,0:T(8,128)S(1)} %collective-permute-done.5.in2_ref, ...), custom_call_target="tpu_custom_call" | custom-call | flops 327680 | bytes 983040 | tf_op jit(solution)/shard_map/pallas_call | solution.py:173
  36.7 0.8 collective-permute-start.7
  37.4 6.6 %all-to-all-start.1 = ((bf16[16,32,512]{2,1,0:T(8,128)(2,1)}), bf16[16,32,512]{2,1,0:T(8,128)(2,1)S(1)}, u32[]{:S(2)}, u32[]{:S(2)}) async-start(bf16[16,32,512]{2,1,0:T(8,128)(2,1)} %get-tuple-element.36), calls=%async_computation.1 | async-start | bytes 1048576 | tf_op jit(solution)/shard_map/all_to_all | solution.py:560
  44.0 2.6 %shard_map.174.high_hbm = bf16[256,1024]{1,0:T(8,128)(2,1)} custom-call(s32[1,4096]{1,0:T(1,128)S(1)} %bitcast.20, s32[1,1024]{1,0:T(1,128)S(1)} %bitcast.24), custom_call_target="tpu_custom_call" | custom-call | flops 805306368 | bytes 524288 | tf_op jit(solution)/shard_map/pallas_call | solution.py:361
  46.6 0.0 collective-permute-done.7.refs_2_
  46.7 0.0 copy-done.4
  46.7 0.0 copy-done.7
  46.7 6.8 %shard_map.173.pre_hbm = bf16[1024,2048]{1,0:T(8,128)(2,1)} custom-call(s32[8,128]{1,0:T(8,128)S(1)} %bitcast.25, bf16[256,512]{1,0:T(8,128)(2,1)S(1)} %get-tuple-element.31.refs_0_, bf16[256,512]{1,0:T(8,128)(2,1)S(1)} %collective-permute-done.2.refs_1_, bf16[256,512]{1,0:T(8,128)(2,1)S(1)} %collective-permute-done.7.refs_2_, ...), custom_call_target="tpu_custom_call" | custom-call | flops 3221225472 | bytes 4194304 | tf_op jit(solution)/shard_map/pallas_call | solution.py:300
  53.5 0.0 all-to-all-done.1
  53.5 0.0 copy-start.5
  53.5 4.8 %collective-permute-start.8 = (bf16[512,512]{1,0:T(8,128)(2,1)S(1)}, bf16[512,512]{1,0:T(8,128)(2,1)S(1)}, u32[]{:S(2)}, u32[]{:S(2)}) collective-permute-start(bf16[512,512]{1,0:T(8,128)(2,1)S(1)} %bitcast.14), channel_id=1, source_target_pairs={{0,1},{1,0},{2,3},{3,2},{4,5},{5,4},{6,7},{7,6},{8,9},{9,8},{10,11... | collective-permute-start | bytes 1572872 | tf_op jit(solution)/shard_map/ppermute | solution.py:568
  58.3 2.4 %shard_map.175 = (f32[1024,512]{1,0:T(8,128)S(1)}, bf16[1024,512]{1,0:T(8,128)(2,1)S(1)}, bf16[512,2048]{1,0:T(8,128)(2,1)S(1)}) custom-call(bf16[768,1024]{1,0:T(8,128)(2,1)} %shard_map.170.low_hbm, bf16[256,1024]{1,0:T(8,128)(2,1)} %shard_map.174.high_hbm, bf16[512,512]{1,0:T(8,128)(2,1)S(1)} %bitcast.15, bf16[1024,2048]{1,0:T(8,128)(2,1)} %w_in_hbm.1), custom_call_target="tpu_custom_call" | custom-call | flops 536870912 | bytes 6291456 | tf_op jit(solution)/shard_map/pallas_call | solution.py:409
  60.8 0.0 collective-permute-done.8.other_ref
  60.8 0.0 copy-done.5
  60.8 16.5 %shard_map.176 = f32[1024,2048]{1,0:T(8,128)} custom-call(f32[1024,512]{1,0:T(8,128)S(1)} %get-tuple-element.43.pool_ref, bf16[1024,512]{1,0:T(8,128)(2,1)S(1)} %get-tuple-element.44.count_ref, bf16[512,512]{1,0:T(8,128)(2,1)S(1)} %collective-permute-done.8.other_ref, bf16[512,2048]{1,0:T(8,128)(2,1)S(1)} %get-tuple-element.46.w_hot_ref, ...), custom_call_target="tpu_custom_call" | custom-call | flops 11274289152 | bytes 8388608 | tf_op jit(solution)/shard_map/pallas_call | solution.py:481
  (2 shorter events, 0.0 us)
Async XLA Ops:
  1.9 4.4 %collective-permute-start = (bf16[512,512]{1,0:T(8,128)(2,1)S(1)}, bf16[512,512]{1,0:T(8,128)(2,1)S(1)}, u32[]{:S(2)}, u32[]{:S(2)}) collective-permute-start(bf16[512,512]{1,0:T(8,128)(2,1)S(1)} %shard_map.165), channel_id=1, source_target_pairs={{0,1},{1,0},{2,3},{3,2},{4,5},{5,4},{6,7},{7,6},{8,9},{9,8},{10,11... | collective-permute-start | bytes 1572872 | tf_op jit(solution)/shard_map/ppermute | solution.py:534
  6.3 12.8 %collective-permute-start.1 = (bf16[512,512]{1,0:T(8,128)(2,1)S(1)}, bf16[512,512]{1,0:T(8,128)(2,1)S(1)}, u32[]{:S(2)}, u32[]{:S(2)}) collective-permute-start(bf16[512,512]{1,0:T(8,128)(2,1)S(1)} %shard_map.166), channel_id=1, source_target_pairs={{0,1},{1,0},{2,3},{3,2},{4,5},{5,4},{6,7},{7,6},{8,9},{9,8},{10,11... | collective-permute-start | bytes 1572872 | tf_op jit(solution)/shard_map/ppermute | solution.py:544
  8.5 19.8 %all-to-all-start = ((bf16[16,32,512]{2,1,0:T(8,128)(2,1)}), bf16[16,32,512]{2,1,0:T(8,128)(2,1)S(1)}, u32[]{:S(2)}, u32[]{:S(2)}) async-start(bf16[16,32,512]{2,1,0:T(8,128)(2,1)} %bitcast.3), calls=%async_computation | async-start | bytes 1048576 | tf_op jit(solution)/shard_map/all_to_all | solution.py:541
  16.2 6.0 %copy-start.3 = (s32[1,1,4096]{2,1,0:T(1,128)S(1)}, s32[1,1,4096]{2,1,0:T(1,128)}, u32[]{:S(2)}) copy-start(s32[1,1,4096]{2,1,0:T(1,128)} %param.18) | copy-start | bytes 49156
  16.2 5.9 %copy-start.6 = (s32[1,1,1024]{2,1,0:T(1,128)S(1)}, s32[1,1,1024]{2,1,0:T(1,128)}, u32[]{:S(2)}) copy-start(s32[1,1,1024]{2,1,0:T(1,128)} %param.19) | copy-start | bytes 12292
  19.3 9.1 %collective-permute-start.2 = (bf16[256,512]{1,0:T(8,128)(2,1)S(1)}, bf16[256,512]{1,0:T(8,128)(2,1)S(1)}, u32[]{:S(2)}, u32[]{:S(2)}) collective-permute-start(bf16[256,512]{1,0:T(8,128)(2,1)S(1)} %get-tuple-element.33), channel_id=1, source_target_pairs={{0,2},{1,3},{2,4},{3,5},{4,6},{5,7},{6,0},{7,1},{8,10},{9,11},{10,... | collective-permute-start | bytes 786440 | tf_op jit(solution)/shard_map/ppermute | solution.py:530
  20.6 7.7 %collective-permute-start.3 = (bf16[256,512]{1,0:T(8,128)(2,1)S(1)}, bf16[256,512]{1,0:T(8,128)(2,1)S(1)}, u32[]{:S(2)}, u32[]{:S(2)}) collective-permute-start(bf16[256,512]{1,0:T(8,128)(2,1)S(1)} %get-tuple-element.34), channel_id=1, source_target_pairs={{0,6},{1,7},{2,0},{3,1},{4,2},{5,3},{6,4},{7,5},{8,14},{9,15},{10,... | collective-permute-start | bytes 786440 | tf_op jit(solution)/shard_map/ppermute | solution.py:530
  22.1 13.6 %copy-start = (f32[64,512]{1,0:T(8,128)S(1)}, f32[64,512]{1,0:T(8,128)}, u32[]{:S(2)}) copy-start(f32[64,512]{1,0:T(8,128)} %param.17) | copy-start | bytes 393220
  22.2 13.6 %copy-start.1 = (f32[64,512]{1,0:T(8,128)S(1)}, f32[64,512]{1,0:T(8,128)}, u32[]{:S(2)}) copy-start(f32[64,512]{1,0:T(8,128)} %param.15) | copy-start | bytes 393220
  22.2 13.6 %copy-start.2 = (f32[64,512]{1,0:T(8,128)S(1)}, f32[64,512]{1,0:T(8,128)}, u32[]{:S(2)}) copy-start(f32[64,512]{1,0:T(8,128)} %param.16) | copy-start | bytes 393220
  28.4 3.3 %collective-permute-start.6 = (f32[32,512]{1,0:T(8,128)S(1)}, f32[32,512]{1,0:T(8,128)S(1)}, u32[]{:S(2)}, u32[]{:S(2)}) collective-permute-start(f32[32,512]{1,0:T(8,128)S(1)} %shard_map.171.share_ref), channel_id=1, source_target_pairs={{0,6},{1,7},{2,0},{3,1},{4,2},{5,3},{6,4},{7,5},{8,14},{9,15},{10,... | collective-permute-start | bytes 196616 | tf_op jit(solution)/shard_map/ppermute | solution.py:530
  30.4 4.7 %collective-permute-start.5 = (f32[32,512]{1,0:T(8,128)S(1)}, f32[32,512]{1,0:T(8,128)S(1)}, u32[]{:S(2)}, u32[]{:S(2)}) collective-permute-start(f32[32,512]{1,0:T(8,128)S(1)} %shard_map.171.share_ref), channel_id=1, source_target_pairs={{0,4},{1,5},{2,6},{3,7},{4,0},{5,1},{6,2},{7,3},{8,12},{9,13},{10,... | collective-permute-start | bytes 196616 | tf_op jit(solution)/shard_map/ppermute | solution.py:530
  30.7 5.0 %collective-permute-start.4 = (f32[32,512]{1,0:T(8,128)S(1)}, f32[32,512]{1,0:T(8,128)S(1)}, u32[]{:S(2)}, u32[]{:S(2)}) collective-permute-start(f32[32,512]{1,0:T(8,128)S(1)} %shard_map.171.share_ref), channel_id=1, source_target_pairs={{0,2},{1,3},{2,4},{3,5},{4,6},{5,7},{6,0},{7,1},{8,10},{9,11},{10,... | collective-permute-start | bytes 196616 | tf_op jit(solution)/shard_map/ppermute | solution.py:530
  36.7 10.0 %copy-start.4 = (f32[2048]{0:T(1024)S(1)}, f32[2048]{0:T(1024)}, u32[]{:S(2)}) copy-start(f32[2048]{0:T(1024)} %param.25) | copy-start | bytes 24580
  36.7 10.0 %copy-start.7 = (s32[1,1,8,128]{3,2,1,0:T(8,128)S(1)}, s32[1,1,8,128]{3,2,1,0:T(8,128)}, u32[]{:S(2)}) copy-start(s32[1,1,8,128]{3,2,1,0:T(8,128)} %param.23) | copy-start | bytes 12292
  36.7 10.0 %collective-permute-start.7 = (bf16[256,512]{1,0:T(8,128)(2,1)S(1)}, bf16[256,512]{1,0:T(8,128)(2,1)S(1)}, u32[]{:S(2)}, u32[]{:S(2)}) collective-permute-start(bf16[256,512]{1,0:T(8,128)(2,1)S(1)} %get-tuple-element.39), channel_id=1, source_target_pairs={{0,4},{1,5},{2,6},{3,7},{4,0},{5,1},{6,2},{7,3},{8,12},{9,13},{10,... | collective-permute-start | bytes 786440 | tf_op jit(solution)/shard_map/ppermute | solution.py:530
  37.4 16.0 %all-to-all-start.1 = ((bf16[16,32,512]{2,1,0:T(8,128)(2,1)}), bf16[16,32,512]{2,1,0:T(8,128)(2,1)S(1)}, u32[]{:S(2)}, u32[]{:S(2)}) async-start(bf16[16,32,512]{2,1,0:T(8,128)(2,1)} %get-tuple-element.36), calls=%async_computation.1 | async-start | bytes 1048576 | tf_op jit(solution)/shard_map/all_to_all | solution.py:560
  53.5 7.3 %copy-start.5 = (f32[2048]{0:T(1024)S(1)}, f32[2048]{0:T(1024)}, u32[]{:S(2)}) copy-start(f32[2048]{0:T(1024)} %param.27) | copy-start | bytes 24580
  53.5 7.3 %collective-permute-start.8 = (bf16[512,512]{1,0:T(8,128)(2,1)S(1)}, bf16[512,512]{1,0:T(8,128)(2,1)S(1)}, u32[]{:S(2)}, u32[]{:S(2)}) collective-permute-start(bf16[512,512]{1,0:T(8,128)(2,1)S(1)} %bitcast.14), channel_id=1, source_target_pairs={{0,1},{1,0},{2,3},{3,2},{4,5},{5,4},{6,7},{7,6},{8,9},{9,8},{10,11... | collective-permute-start | bytes 1572872 | tf_op jit(solution)/shard_map/ppermute | solution.py:568

commit v3 on v2

--- a/solution.py
+++ b/solution.py
@@ -95,31 +95,48 @@
         out_ref[i * rows : (i + 1) * rows, :] = mine.astype(BF16)
 
 
-def chip_kernel(grad_ref, other_ref, out_ref, held_ref, sems):
-    core, _ = my_place()
-    copies = load_half(grad_ref, core, held_ref, sems)
-    rows, part = out_ref.shape[0] // len(copies), held_ref.shape[0] // len(copies)
-    for i, copy in enumerate(copies):
-        copy.wait()
-        here = slice(i * rows, (i + 1) * rows)
-        mine = held_ref[i * part : (i + 1) * part].reshape(rows, out_ref.shape[1])
-        out_ref[here, :] = (mine + other_ref[here, :].astype(F32)).astype(BF16)
-
-
-def half_rows(grad, other=None):
+def other_half(grad):
     n_dp, lines, _, own, width = grad.shape
     total = n_dp * lines * own
     return pl.pallas_call(
-        half_kernel if other is None else chip_kernel,
+        half_kernel,
         out_shape=jax.ShapeDtypeStruct((total, width), BF16),
-        in_specs=[HBM] if other is None else [HBM, VMEM],
+        in_specs=[HBM],
         out_specs=VMEM,
         scratch_shapes=[
             pltpu.VMEM((n_dp, lines, own, width), F32), pltpu.SemaphoreType.DMA((4,))
         ],
         compiler_params=params(16),
         cost_estimate=cost(0, total * width * 6),
-    )(in_hbm(grad), *(() if other is None else (other,)))
+    )(in_hbm(grad))
+
+
+def chip_kernel(mine_ref, other_ref, out_hbm, out_ref, sems):
+    steps = sems.shape[0]
+    rows, part = other_ref.shape[0] // steps, mine_ref.shape[0] // steps
+    copies = []
+    for i in range(steps):
+        here = slice(i * rows, (i + 1) * rows)
+        mine = mine_ref[i * part : (i + 1) * part].reshape(rows, out_ref.shape[1])
+        out_ref[here, :] = (mine + other_ref[here, :].astype(F32)).astype(BF16)
+        block = pl.ds(i * rows, rows)
+        copy = pltpu.make_async_copy(out_ref.at[block], out_hbm.at[block], sems.at[i])
+        copy.start()
+        copies.append(copy)
+    for copy in copies:
+        copy.wait()
+
+
+def chip_rows(mine, other):
+    return pl.pallas_call(
+        chip_kernel,
+        out_shape=pltpu.HBM(other.shape, BF16),
+        in_specs=[VMEM, VMEM],
+        out_specs=HBM,
+        scratch_shapes=[pltpu.VMEM(other.shape, BF16), pltpu.SemaphoreType.DMA((4,))],
+        compiler_params=params(16),
+        cost_estimate=cost(0, other.size * 8),
+    )(mine, other)
 
 
 def sum_kernel(parts_ref, out_ref):
@@ -182,55 +199,82 @@
     )(share, *shares_in, *rows)
 
 
-def pick_kernel(
-    other_side, index_hbm, count_hbm, table_hbm, out_ref, index_ref, count_ref, table_ref, sems
-):
+def pick_kernel(other_side, index_hbm, count_hbm, table_hbm, *refs):
+    if other_side:
+        grad_hbm, out_ref, mine_ref, *scratch, grad_sems = refs
+    else:
+        out_ref, *scratch = refs
+    index_ref, count_ref, table_ref, total_ref, sems = scratch
+    asked = [
+        pltpu.make_async_copy(index_hbm, index_ref, sems.at[0]),
+        pltpu.make_async_copy(count_hbm, count_ref, sems.at[1]),
+    ]
+    pieces = sems.shape[0] - 2
+    part = table_ref.shape[0] // pieces
     copies = [
-        pltpu.make_async_copy(source, target, sems.at[i])
-        for i, (source, target) in enumerate(
-            ((index_hbm, index_ref), (count_hbm, count_ref), (table_hbm, table_ref))
+        pltpu.make_async_copy(
+            table_hbm.at[pl.ds(i * part, part)], table_ref.at[pl.ds(i * part, part)], sems.at[2 + i]
         )
+        for i in range(pieces)
     ]
-    for copy in copies:
+    for copy in asked + copies:
         copy.start()
     core, line = my_place()
+    grads = load_half(grad_hbm, core, mine_ref, grad_sems) if other_side else []
     side = 1 - core if other_side else core
     askers, slots = index_ref.shape
     lines = askers // 2
-    rows = lax.broadcasted_iota(I16, (table_ref.shape[0], slots), 0)
     slot = lax.broadcasted_iota(I32, (1, slots), 1)
     each = lax.broadcasted_iota(I32, (1, askers), 1)
-    copies[0].wait()
-    copies[1].wait()
+    for copy in asked:
+        copy.wait()
+    wanted = []
     for s in range(lines):
         asker = lax.rem(line + s, lines) * 2 + side
         used = jnp.sum(jnp.where(each == asker, count_ref[...], 0), axis=1, keepdims=True)
-        wanted = index_ref[pl.ds(asker, 1), :]
-        wanted = jnp.where(slot < used, wanted, -1).astype(I16)
-        hit = jnp.where(rows == wanted, BF16(1), BF16(0))
-        if s == 0:
-            copies[2].wait()
-        found = dot_on(hit, table_ref[...], FIRST)
-        out_ref[s * slots : (s + 1) * slots, :] = found.astype(BF16)
-
-
-def pick(index, counts, table, other_side):
+        wanted.append(jnp.where(slot < used, index_ref[pl.ds(asker, 1), :], -1).astype(I16))
+    wanted = jnp.concatenate(wanted, axis=1)
+    rows = lax.broadcasted_iota(I16, (part, lines * slots), 0)
+    for i, copy in enumerate(copies):
+        hit = jnp.where(rows + I16(i * part) == wanted, BF16(1), BF16(0))
+        copy.wait()
+        found = dot_on(hit, table_ref[i * part : (i + 1) * part, :], FIRST)
+        if i > 0:
+            found = found + total_ref[...]
+        if i < pieces - 1:
+            total_ref[...] = found
+        else:
+            out_ref[...] = found.astype(BF16)
+    for copy in grads:
+        copy.wait()
+
+
+def pick(index, counts, table, grad=None):
     width = table.shape[1]
     rows = index.size // 2
-    return pl.pallas_call(
-        functools.partial(pick_kernel, other_side),
-        out_shape=jax.ShapeDtypeStruct((rows, width), BF16),
-        in_specs=[HBM, HBM, HBM],
-        out_specs=VMEM,
-        scratch_shapes=[
-            pltpu.VMEM(index.shape, I32),
-            pltpu.VMEM(counts.shape, I32),
-            pltpu.VMEM(table.shape, BF16),
-            pltpu.SemaphoreType.DMA((3,)),
-        ],
+    out = [jax.ShapeDtypeStruct((rows, width), BF16)]
+    scratch = [
+        pltpu.VMEM(index.shape, I32),
+        pltpu.VMEM(counts.shape, I32),
+        pltpu.VMEM(table.shape, BF16),
+        pltpu.VMEM((rows, width), F32),
+        pltpu.SemaphoreType.DMA((6,)),
+    ]
+    operands = [index, counts, table]
+    if grad is not None:
+        n_dp, lines, _, own, _ = grad.shape
+        out.append(jax.ShapeDtypeStruct((n_dp, lines, own, width), F32))
+        scratch.append(pltpu.SemaphoreType.DMA((4,)))
+        operands.append(grad)
+    return pl.pallas_call(
+        functools.partial(pick_kernel, grad is not None),
+        out_shape=tuple(out),
+        in_specs=[HBM] * len(operands),
+        out_specs=(VMEM,) * len(out),
+        scratch_shapes=scratch,
         compiler_params=params(24),
         cost_estimate=cost(index.size * table.size, table.size * 2),
-    )(in_hbm(index), in_hbm(counts), in_hbm(table))
+    )(*(in_hbm(a) for a in operands))
 
 
 def merge_kernel(near_ref, far_ref, *out_refs):
@@ -253,10 +297,11 @@
 
 
 def cold_kernel(sample_ref, *refs):
-    rows_in, (w_hbm, b_ref, pre_hbm, w_ref, held_ref, sem, out_sems) = refs[:-7], refs[-7:]
+    rows_in, rest = refs[:-8], refs[-8:]
+    w_hbm, b_ref, pre_hbm, w_ref, feature_ref, held_ref, sem, out_sems = rest
     core, line = my_place()
     lines = len(rows_in)
-    batch, width = held_ref.shape[0], rows_in[0].shape[1]
+    batch, width = feature_ref.shape
     copy = pltpu.make_async_copy(w_hbm.at[pl.ds(width, width)], w_ref, sem)
     copy.start()
     samples = []
@@ -267,25 +312,27 @@
                 [sample_ref[pl.ds(owner + side, 1), :] for side in (core, 1 - core)], axis=1
             )
         )
-    bag = lax.broadcasted_iota(I16, (TILE, samples[0].shape[1]), 0)
+    bag = lax.broadcasted_iota(I16, (ROWS, samples[0].shape[1]), 0)
+
+    def pool_step(i, _):
+        pool = None
+        for sample, rows_ref in zip(samples, rows_in, strict=True):
+            hit = bag == (sample - i * ROWS).astype(I16)
+            part = dot(jnp.where(hit, BF16(1), BF16(0)), rows_ref[...])
+            pool = part if pool is None else pool + part
+        feature_ref[pl.ds(pl.multiple_of(i * ROWS, ROWS), ROWS), :] = pool.astype(BF16)
+        return 0
+
+    lax.fori_loop(0, batch // ROWS, pool_step, 0)
+    copy.wait()
 
     def leave(i):
         here = pl.ds(pl.multiple_of(i * TILE, TILE), TILE)
         return pltpu.make_async_copy(held_ref.at[here], pre_hbm.at[here], out_sems.at[i])
 
     def step(i, _):
-        pool = None
-        for sample, rows_ref in zip(samples, rows_in, strict=True):
-            hit = bag == (sample - i * TILE).astype(I16)
-            part = dot(jnp.where(hit, BF16(1), BF16(0)), rows_ref[...])
-            pool = part if pool is None else pool + part
-
-        @pl.when(i == 0)
-        def _():
-            copy.wait()
-
         here = pl.ds(pl.multiple_of(i * TILE, TILE), TILE)
-        held_ref[here, :] = (dot(pool.astype(BF16), w_ref[...]) + b_ref[...]).astype(BF16)
+        held_ref[here, :] = (dot(feature_ref[here, :], w_ref[...]) + b_ref[...]).astype(BF16)
         leave(i).start()
         return 0
 
@@ -304,6 +351,7 @@
         out_specs=HBM,
         scratch_shapes=[
             pltpu.VMEM((width, hidden), BF16),
+            pltpu.VMEM((batch, width), BF16),
             pltpu.VMEM((batch, hidden), BF16),
             pltpu.SemaphoreType.DMA(()),
             pltpu.SemaphoreType.DMA((batch // TILE,)),
@@ -313,7 +361,7 @@
     )(samples, *rows_in, in_hbm(w_in), b_in.reshape(1, hidden))
 
 
-def count_kernel(low_block, own, ids_ref, lengths_ref, out_ref, total_ref):
+def count_kernel(low_block, own, ids_ref, lengths_ref, out_hbm, total_ref, out_ref, sems):
     core, _ = my_place()
     bags, width = out_ref.shape
     row = lax.broadcasted_iota(I32, (BAGS, BAGS), 0)
@@ -324,12 +372,17 @@
     offset = F32(0.0)
     if low_block:
         offset = jnp.sum(lengths_ref[:, : low_block * BAGS].astype(F32))
+
+    def leave(k):
+        here = pl.ds(k * BAGS, BAGS)
+        return pltpu.make_async_copy(out_ref.at[here], out_hbm.at[here], sems.at[k])
+
     for k in range(bags // BAGS):
         at = (low_block + k) * BAGS
         lengths = lengths_ref[:, at : at + BAGS].astype(F32)
         spread = jnp.broadcast_to(lengths, (LANES, BAGS)).astype(BF16)
-        end = offset + dot_on(upto, spread, LAST)
-        start = offset + dot_on(before, spread, LAST)
+        end = (offset + dot_on(upto, spread, LAST)).astype(I32).astype(I16)
+        start = (offset + dot_on(before, spread, LAST)).astype(I32).astype(I16)
         following = offset + jnp.sum(lengths)
         lowest, highest = offset.astype(I32), following.astype(I32)
         offset = following
@@ -342,114 +395,127 @@
             places = lax.div(ids, 2 * own) * own + lax.rem(ids, own)
             places = jnp.where(far, places + width // 2, places).astype(I16)
             hits = jnp.where(rows == places, BF16(1), BF16(0))
-            lane = (here + lax.broadcasted_iota(I32, (BAGS, LANES), 1)).astype(F32)
-            member = jnp.concatenate(
-                [
-                    jnp.where((start <= lane + o) & (lane + o < end), 1.0, 0.0)
-                    for o in range(0, CHUNK, LANES)
-                ],
-                axis=1,
-            ).astype(BF16)
-            total_ref[...] += dot_on(member, hits, LAST)
+            lane = (here + lax.broadcasted_iota(I32, (1, CHUNK), 1)).astype(I16)
+            parts = []
+            for o in range(0, CHUNK, LANES):
+                at_lane = lane[:, o : o + LANES]
+                inside = (start <= at_lane) & (at_lane < end)
+                parts.append(jnp.where(inside, BF16(1), BF16(0)))
+            total_ref[...] += dot_on(jnp.concatenate(parts, axis=1), hits, LAST)
             return 0
 
         lax.fori_loop(lowest // CHUNK, (highest + CHUNK - 1) // CHUNK, step, 0)
         out_ref[k * BAGS : (k + 1) * BAGS, :] = total_ref[...].astype(BF16)
+        leave(k).start()
+    for k in range(bags // BAGS):
+        leave(k).wait()
 
 
 def count_matrix(ids, lengths, width, own, low_block, blocks):
     return pl.pallas_call(
         functools.partial(count_kernel, low_block, own),
         out_shape=pltpu.HBM((blocks * BAGS, width), BF16),
-        grid=(1,),
         in_specs=[VMEM, VMEM],
-        out_specs=pl.BlockSpec((blocks * BAGS, width), lambda i: (0, 0)),
-        scratch_shapes=[pltpu.VMEM((BAGS, width), F32)],
+        out_specs=HBM,
+        scratch_shapes=[
+            pltpu.VMEM((BAGS, width), F32),
+            pltpu.VMEM((blocks * BAGS, width), BF16),
+            pltpu.SemaphoreType.DMA((blocks,)),
+        ],
         compiler_params=params(24),
         cost_estimate=cost(3 * blocks * 2 * BAGS * CHUNK * width, 2 * blocks * BAGS * width),
     )(ids, lengths)
 
 
-def own_kernel(
-    low_hbm, high_hbm, own_ref, w_in_hbm, pool_ref, count_ref, w_hot_ref, held_ref, sems
-):
-    half, width = own_ref.shape
-    low, high = low_hbm.shape[0], high_hbm.shape[0]
-    mine, rest = pl.ds(0, half), pl.ds(half, half)
+def own_kernel(own_ref, pre_hbm, w_in_hbm, *refs):
+    counts, rest = refs[:-6], refs[-6:]
+    pool_ref, count_ref, pre_ref, w_hot_ref, held_ref, sems = rest
+    half = own_ref.shape[0]
+    needed, later, low = [], [], 0
+    for part in counts:
+        here = pl.ds(low, part.shape[0])
+        needed.append((part.at[:, pl.ds(0, half)], held_ref.at[here]))
+        later.append((part.at[:, pl.ds(half, half)], count_ref.at[here]))
+        low += part.shape[0]
+    later.append((w_in_hbm.at[pl.ds(0, w_hot_ref.shape[0])], w_hot_ref))
+    later.append((pre_hbm.at[pl.ds(0, pre_ref.shape[0])], pre_ref))
     copies = [
         pltpu.make_async_copy(source, target, sems.at[i])
-        for i, (source, target) in enumerate(
-            (
-                (low_hbm.at[:, mine], held_ref.at[pl.ds(0, low)]),
-                (high_hbm.at[:, mine], held_ref.at[pl.ds(low, high)]),
-                (low_hbm.at[:, rest], count_ref.at[pl.ds(0, low)]),
-                (high_hbm.at[:, rest], count_ref.at[pl.ds(low, high)]),
-                (w_in_hbm.at[pl.ds(0, width)], w_hot_ref),
-            )
-        )
+        for i, (source, target) in enumerate(needed + later)
     ]
     for copy in copies:
         copy.start()
-    copies[0].wait()
-    copies[1].wait()
+    for copy in copies[: len(counts)]:
+        copy.wait()
 
     def step(i, _):
         here = pl.ds(pl.multiple_of(i * TILE, TILE), TILE)
         pool_ref[here, :] = dot(held_ref[here, :], own_ref[...])
         return 0
 
-    lax.fori_loop(0, (low + high) // TILE, step, 0)
-    for copy in copies[2:]:
+    lax.fori_loop(0, low // TILE, step, 0)
+    for copy in copies[len(counts) :]:
         copy.wait()
 
 
-def own_pool(low, high, fresh_own, w_in):
+def own_pool(counts, fresh_own, pre, w_in):
     half, width = fresh_own.shape
-    batch, hidden = low.shape[0] + high.shape[0], w_in.shape[1]
+    batch, hidden = pre.shape
     return pl.pallas_call(
         own_kernel,
         out_shape=(
             pltpu.VMEM((batch, width), F32),
             pltpu.VMEM((batch, half), BF16),
+            pltpu.VMEM((TILE, hidden), BF16),
             pltpu.VMEM((width, hidden), BF16),
         ),
-        in_specs=[HBM, HBM, VMEM, HBM],
-        out_specs=(VMEM, VMEM, VMEM),
-        scratch_shapes=[pltpu.VMEM((batch, half), BF16), pltpu.SemaphoreType.DMA((5,))],
+        in_specs=[VMEM] + [HBM] * (2 + len(counts)),
+        out_specs=(VMEM, VMEM, VMEM, VMEM),
+        scratch_shapes=[
+            pltpu.VMEM((batch, half), BF16), pltpu.SemaphoreType.DMA((2 * len(counts) + 2,))
+        ],
         compiler_params=params(16),
         cost_estimate=cost(2 * batch * half * width, 3 * batch * width * 4),
-    )(in_hbm(low), in_hbm(high), fresh_own, in_hbm(w_in))
+    )(fresh_own, in_hbm(pre), in_hbm(w_in), *(in_hbm(c) for c in counts))
 
 
 def mlp_kernel(
-    pool_ref, count_ref, other_ref, w_hot_ref, pre_hbm, w_out_hbm, b_ref, out_hbm,
+    pool_ref, count_ref, other_ref, w_hot_ref, first_pre_ref, pre_hbm, w_out_hbm, b_ref, out_hbm,
     hidden_ref, w_out_ref, pre_ref, out_ref, pre_sems, w_sems, out_sems,
 ):
-    tiles, rows, _ = pre_ref.shape
-    pieces, _, wide = w_out_ref.shape
+    tiles = hidden_ref.shape[0] // TILE
+    pieces, _, columns = w_out_ref.shape
 
     def load_pre(i):
-        here = pl.ds(pl.multiple_of(i * rows, rows), rows)
+        here = pl.ds(pl.multiple_of(i * TILE, TILE), TILE)
         return pltpu.make_async_copy(pre_hbm.at[here], pre_ref.at[i], pre_sems.at[i])
 
     def load_w(n):
-        here = pl.ds(pl.multiple_of(n * wide, wide), wide)
+        here = pl.ds(pl.multiple_of(n * columns, columns), columns)
         return pltpu.make_async_copy(w_out_hbm.at[:, here], w_out_ref.at[n], w_sems.at[n])
 
     def leave(n):
-        here = pl.ds(pl.multiple_of(n * wide, wide), wide)
+        here = pl.ds(pl.multiple_of(n * columns, columns), columns)
         slot = lax.rem(n, 2)
         return pltpu.make_async_copy(out_ref.at[slot], out_hbm.at[:, here], out_sems.at[slot])
 
-    for i in range(tiles):
+    for i in range(1, tiles):
         load_pre(i).start()
-    for n in range(pieces):
-        load_w(n).start()
+    load_w(0).start()
+    pre_ref[0] = first_pre_ref[...]
 
     def first_layer(i, _):
-        here = pl.ds(pl.multiple_of(i * rows, rows), rows)
+        here = pl.ds(pl.multiple_of(i * TILE, TILE), TILE)
         pool = pool_ref[here, :] + dot(count_ref[here, :], other_ref[...])
-        load_pre(i).wait()
+
+        @pl.when(i > 0)
+        def _():
+            load_pre(i).wait()
+
+            @pl.when(i < pieces)
+            def _():
+                load_w(i).start()
+
         pre = dot(pool.astype(BF16), w_hot_ref[...]) + pre_ref[i].astype(F32)
         hidden_ref[here, :] = jnp.maximum(pre, 0.0).astype(BF16)
         return 0
@@ -463,7 +529,7 @@
         def _():
             leave(n - 2).wait()
 
-        here = pl.ds(pl.multiple_of(n * wide, wide), wide)
+        here = pl.ds(pl.multiple_of(n * columns, columns), columns)
         out_ref[lax.rem(n, 2)] = dot(hidden_ref[...], w_out_ref[n]) + b_ref[:, here]
         leave(n).start()
         return 0
@@ -473,22 +539,22 @@
     leave(pieces - 1).wait()
 
 
-def mlp(pool, counts, fresh_other, w_hot, pre, w_out, b_out):
+def mlp(pool, counts, fresh_other, w_hot, first_pre, pre, w_out, b_out):
     batch, hidden = pre.shape
     wide = w_out.shape[1]
     half, width = fresh_other.shape
-    tiles, pieces = batch // ROWS, wide // PIECE
+    pieces = wide // PIECE
     return pl.pallas_call(
         mlp_kernel,
         out_shape=jax.ShapeDtypeStruct((batch, wide), F32),
-        in_specs=[VMEM] * 4 + [HBM, HBM, VMEM],
+        in_specs=[VMEM] * 5 + [HBM, HBM, VMEM],
         out_specs=HBM,
         scratch_shapes=[
             pltpu.VMEM((batch, hidden), BF16),
             pltpu.VMEM((pieces, hidden, PIECE), BF16),
-            pltpu.VMEM((tiles, ROWS, hidden), BF16),
+            pltpu.VMEM((batch // TILE, TILE, hidden), BF16),
             pltpu.VMEM((2, batch, PIECE), F32),
-            pltpu.SemaphoreType.DMA((tiles,)),
+            pltpu.SemaphoreType.DMA((batch // TILE,)),
             pltpu.SemaphoreType.DMA((pieces,)),
             pltpu.SemaphoreType.DMA((2,)),
         ],
@@ -497,7 +563,8 @@
             2 * batch * (half * width + width * hidden + hidden * wide), batch * wide * 4
         ),
     )(
-        pool, counts, fresh_other, w_hot, in_hbm(pre), in_hbm(w_out), b_out.reshape(1, wide)
+        pool, counts, fresh_other, w_hot, first_pre, in_hbm(pre), in_hbm(w_out),
+        b_out.reshape(1, wide),
     )
 
 
@@ -530,25 +597,25 @@
         return lax.ppermute(array, "table", pairs)
 
     grad = hot_grad[0, 0].reshape(n_dp, lines, 2, own, width)
-    send = half_rows(grad)
+    send = other_half(grad)
     other = lax.ppermute(send, "table", swap)
     index, counts = cold_index[0, 0], cold_count[0]
     (index_far,) = after(send, index)
-    far = pick(index_far, counts, cold_table, True)
-    other, far = lax.optimization_barrier((other, far))
-    chip = half_rows(grad, other)
+    far, mine = pick(index_far, counts, cold_table, grad)
+    chip = chip_rows(mine, other)
 
     parts = lax.all_to_all(
         chip.reshape(n_dp, lines * own, width), "dp", split_axis=0, concat_axis=0, tiled=True
     )
     far_in = lax.ppermute(far, "table", swap)
     (index_near,) = after(chip, index)
-    near = pick(index_near, counts, cold_table, False)
+    (near,) = pick(index_near, counts, cold_table)
     blocks = merge(near, far_in, lines)
     rows_in = [along(blocks[s], s) if s in (1, lines - 1) else blocks[s] for s in range(lines)]
 
     ids, lengths = hot_ids[0], hot_lengths[0]
-    early = batch // BAGS * 3 // 4
+    blocks_in_all = batch // BAGS
+    early = blocks_in_all * 3 // 4
     (ids_now,) = after(blocks[0], ids)
     count_low = count_matrix(ids_now, lengths, hot, own, 0, early)
     parts, *_ = lax.optimization_barrier((parts, count_low, rows_in[1], rows_in[-1]))
@@ -558,17 +625,18 @@
         share, shares_in, hot_master, first_moment, second_moment, n_dp, lines, own
     )
     fresh_own = lax.all_to_all(spread, "dp", split_axis=0, concat_axis=0, tiled=True)
-    samples, ids_late, *middle = after(spread, cold_sample[0, 0], ids, *rows_in[2:-1])
-    for s, block in enumerate(middle):
-        rows_in[2 + s] = along(block, 2 + s)
-    count_high = count_matrix(ids_late, lengths, hot, own, early, batch // BAGS - early)
+    samples, ids_late, *further = after(spread, cold_sample[0, 0], ids, *rows_in[2:-1])
+    rows_in[2:-1] = [along(block, 2 + s) for s, block in enumerate(further)]
+    count_high = count_matrix(ids_late, lengths, hot, own, early, blocks_in_all - early)
     pre = cold_half(samples, rows_in, w_in, b_in, batch)
     fresh_own, *_ = lax.optimization_barrier((fresh_own, pre, count_high))
     fresh_own = fresh_own.reshape(hot // 2, width)
     fresh_other = lax.ppermute(fresh_own, "table", swap)
-    pool, counts_other, w_hot = own_pool(count_low, count_high, fresh_own, w_in)
+    pool, counts_other, first_pre, w_hot = own_pool(
+        [count_low, count_high], fresh_own, pre, w_in
+    )
     fresh_other, pool = lax.optimization_barrier((fresh_other, pool))
-    result = mlp(pool, counts_other, fresh_other, w_hot, pre, w_out, b_out)
+    result = mlp(pool, counts_other, fresh_other, w_hot, first_pre, pre, w_out, b_out)
     return (result[None, None], new_master, new_first, new_second)
 
 

time: 77.9 us -> 74.5 us (0.956)
  Pallas kernels: 44.8 us -> 39.6 us
  waiting for transfers between devices: 4.38 us -> 6.05 us
    pallas_call x4, Pallas kernels: 9.17 us -> 7.44 us  [the longest x2 5.32 us: pick(): pl.pallas_call(functools.partial(pick_kernel, grad is not None), out_shap...]
    pallas_call x1, Pallas kernels: 16.5 us -> 14.9 us  [mlp(): pl.pallas_call(mlp_kernel, out_shape=jax.ShapeDtypeStruct((batch, wide),...]
    all_to_all x1, waiting for transfers between devices: 0.01 us -> 1.47 us  [on_device(): lax.all_to_all(spread, 'dp', split_axis=0, concat_axis=0, tiled=True)]
    pallas_call x1, Pallas kernels: 6.79 us -> 5.48 us  [cold_half(): pl.pallas_call(cold_kernel, out_shape=pltpu.HBM((batch, hidden), BF16), i...]
  transfers between devices with their start and end apart: 11 -> 11, of which waited for: 3 -> 4; matrix products, arithmetic and copies ran while one was open for 0% -> 0% of each run, Pallas kernels for 34% -> 30%
where the time goes in v3:
time: 74.5 us; the launch traced here: 74.1 us
  Pallas kernels  39.6 us (53%)
  starting transfers between devices  27.5 us (37%)
  waiting for transfers between devices  6.05 us (8%)
  between operations  0.84 us (1%)
    pallas_call x1, Pallas kernels, mlp(): pl.pallas_call(mlp_kernel, out_shape=jax.ShapeDtypeStruct((batch, wide),...  14.9 us
    pallas_call x2, Pallas kernels, count_matrix(): pl.pallas_call(functools.partial(count_kernel, low_block, own), out_shape...  8.18 us
    all_to_all x1, starting transfers between devices, on_device(): lax.all_to_all(chip.reshape(n_dp, lines * own, width), 'dp', split_axis=0...  7.7 us
    ppermute x6, starting transfers between devices, along(): return lax.ppermute(array, 'table', pairs)  6.45 us
    all_to_all x1, starting transfers between devices, on_device(): lax.all_to_all(spread, 'dp', split_axis=0, concat_axis=0, tiled=True)  6.35 us
    pallas_call x1, Pallas kernels, cold_half(): pl.pallas_call(cold_kernel, out_shape=pltpu.HBM((batch, hidden), BF16), i...  5.48 us
    ppermute x1, starting transfers between devices, on_device(): fresh_other = lax.ppermute(fresh_own, 'table', swap)  5.43 us
    pallas_call x2, Pallas kernels, pick(): pl.pallas_call(functools.partial(pick_kernel, grad is not None), out_shap...  5.32 us
  transfers between devices with their start and end apart: 11, of which 4 were waited for; matrix products, arithmetic and copies ran while one was open for 0% of the time, Pallas kernels for 30%

profile of v3, /device:TPU:1, one launch (start us, length us, event | category | flops | bytes accessed | tf_op | source)
XLA Modules:
  0.0 74.1 jit_solution(13600868259335449486)
XLA Ops:
  0.6 1.2 %shard_map.165 = bf16[512,512]{1,0:T(8,128)(2,1)S(1)} custom-call(f32[16,4,2,8,512]{4,3,2,1,0:T(8,128)} %bitcast.26), custom_call_target="tpu_custom_call" | custom-call | bytes 1572864 | tf_op jit(solution)/shard_map/pallas_call | solution.py:101
  1.9 1.5 %collective-permute-start = (bf16[512,512]{1,0:T(8,128)(2,1)S(1)}, bf16[512,512]{1,0:T(8,128)(2,1)S(1)}, u32[]{:S(2)}, u32[]{:S(2)}) collective-permute-start(bf16[512,512]{1,0:T(8,128)(2,1)S(1)} %shard_map.165), channel_id=1, source_target_pairs={{0,1},{1,0},{2,3},{3,2},{4,5},{5,4},{6,7},{7,6},{8,9},{9,8},{10,11... | collective-permute-start | bytes 1572872 | tf_op jit(solution)/shard_map/ppermute | solution.py:601
  3.4 2.7 %shard_map.166 = (bf16[512,512]{1,0:T(8,128)(2,1)S(1)}, f32[16,4,8,512]{3,2,1,0:T(8,128)S(1)}) custom-call(s32[8,128]{1,0:T(8,128)} %bitcast.29, s32[1,8]{1,0:T(1,128)} %bitcast.31, bf16[2048,512]{1,0:T(8,128)(2,1)} %table_hbm.3, f32[16,4,2,8,512]{4,3,2,1,0:T(8,128)} %bitcast.27), custom_call_target="tpu_custom_call" | custom-call | flops 1073741824 | bytes 2097152 | tf_op jit(solution)/shard_map/pallas_call | solution.py:269
  6.1 0.1 collective-permute-start.1
  6.2 0.0 collective-permute-done.other_ref
  6.2 0.9 %shard_map.167 = bf16[512,512]{1,0:T(8,128)(2,1)} custom-call(f32[16,4,8,512]{3,2,1,0:T(8,128)S(1)} %get-tuple-element.29.mine_ref, bf16[512,512]{1,0:T(8,128)(2,1)S(1)} %collective-permute-done.other_ref), custom_call_target="tpu_custom_call" | custom-call | bytes 2097152 | tf_op jit(solution)/shard_map/pallas_call | solution.py:131
  7.1 7.7 %all-to-all-start = ((bf16[16,32,512]{2,1,0:T(8,128)(2,1)}), bf16[16,32,512]{2,1,0:T(8,128)(2,1)S(1)}, u32[]{:S(2)}, u32[]{:S(2)}) async-start(bf16[16,32,512]{2,1,0:T(8,128)(2,1)} %bitcast.28), calls=%async_computation | async-start | bytes 1048576 | tf_op jit(solution)/shard_map/all_to_all | solution.py:607
  14.8 0.0 copy-start.3
  14.8 0.0 copy-start.6
  14.8 2.6 %shard_map.168.near_ref = bf16[512,512]{1,0:T(8,128)(2,1)S(1)} custom-call(s32[8,128]{1,0:T(8,128)} %bitcast.30, s32[1,8]{1,0:T(1,128)} %bitcast.32, bf16[2048,512]{1,0:T(8,128)(2,1)} %table_hbm.3), custom_call_target="tpu_custom_call" | custom-call | flops 1073741824 | bytes 2097152 | tf_op jit(solution)/shard_map/pallas_call | solution.py:269
  17.4 0.0 collective-permute-done.1.far_ref
  17.4 0.1 shard_map.169
  17.5 1.4 %collective-permute-start.2 = (bf16[256,512]{1,0:T(8,128)(2,1)S(1)}, bf16[256,512]{1,0:T(8,128)(2,1)S(1)}, u32[]{:S(2)}, u32[]{:S(2)}) collective-permute-start(bf16[256,512]{1,0:T(8,128)(2,1)S(1)} %get-tuple-element.34), channel_id=1, source_target_pairs={{0,2},{1,3},{2,4},{3,5},{4,6},{5,7},{6,0},{7,1},{8,10},{9,11},{10,... | collective-permute-start | bytes 786440 | tf_op jit(solution)/shard_map/ppermute | solution.py:597
  18.9 1.5 %collective-permute-start.3 = (bf16[256,512]{1,0:T(8,128)(2,1)S(1)}, bf16[256,512]{1,0:T(8,128)(2,1)S(1)}, u32[]{:S(2)}, u32[]{:S(2)}) collective-permute-start(bf16[256,512]{1,0:T(8,128)(2,1)S(1)} %get-tuple-element.35), channel_id=1, source_target_pairs={{0,6},{1,7},{2,0},{3,1},{4,2},{5,3},{6,4},{7,5},{8,14},{9,15},{10,... | collective-permute-start | bytes 786440 | tf_op jit(solution)/shard_map/ppermute | solution.py:597
  20.4 0.0 copy-done.3
  20.4 0.0 copy-done.6
  20.4 0.0 copy-start
  20.4 0.0 copy-start.1
  20.4 0.0 copy-start.2
  20.4 6.1 %shard_map.170.refs_0_ = bf16[768,1024]{1,0:T(8,128)(2,1)} custom-call(s32[1,4096]{1,0:T(1,128)S(1)} %bitcast.19, s32[1,1024]{1,0:T(1,128)S(1)} %bitcast.23), custom_call_target="tpu_custom_call" | custom-call | flops 2415919104 | bytes 1572864 | tf_op jit(solution)/shard_map/pallas_call | solution.py:415
  26.5 0.0 collective-permute-done.2.refs_1_
  26.5 0.0 collective-permute-done.3.refs_3_
  26.5 0.0 all-to-all-done.parts_ref
  26.5 0.1 shard_map.171.share_ref
  26.6 2.0 %collective-permute-start.6 = (f32[32,512]{1,0:T(8,128)S(1)}, f32[32,512]{1,0:T(8,128)S(1)}, u32[]{:S(2)}, u32[]{:S(2)}) collective-permute-start(f32[32,512]{1,0:T(8,128)S(1)} %shard_map.171.share_ref), channel_id=1, source_target_pairs={{0,6},{1,7},{2,0},{3,1},{4,2},{5,3},{6,4},{7,5},{8,14},{9,15},{10,... | collective-permute-start | bytes 196616 | tf_op jit(solution)/shard_map/ppermute | solution.py:597
  28.7 0.2 collective-permute-start.5
  28.9 0.5 collective-permute-start.4
  29.3 1.1 %collective-permute-done.6.in3_ref = f32[32,512]{1,0:T(8,128)S(1)} collective-permute-done((f32[32,512]{1,0:T(8,128)S(1)}, f32[32,512]{1,0:T(8,128)S(1)}, u32[]{:S(2)}, u32[]{:S(2)}) %collective-permute-start.6) | collective-permute-done | bytes 65568 | tf_op jit(solution)/shard_map/ppermute | solution.py:597
  30.4 3.0 %collective-permute-done.5.in2_ref = f32[32,512]{1,0:T(8,128)S(1)} collective-permute-done((f32[32,512]{1,0:T(8,128)S(1)}, f32[32,512]{1,0:T(8,128)S(1)}, u32[]{:S(2)}, u32[]{:S(2)}) %collective-permute-start.5) | collective-permute-done | bytes 65568 | tf_op jit(solution)/shard_map/ppermute | solution.py:597
  33.4 0.5 collective-permute-done.4.in1_ref
  33.9 0.0 copy-done
  33.9 0.0 copy-done.1
  33.9 0.0 copy-done.2
  33.9 0.9 %shard_map.172 = (bf16[16,32,512]{2,1,0:T(8,128)(2,1)}, f32[8,512]{1,0:T(8,128)}, f32[8,512]{1,0:T(8,128)}, f32[8,512]{1,0:T(8,128)}) custom-call(f32[32,512]{1,0:T(8,128)S(1)} %shard_map.171.share_ref, f32[32,512]{1,0:T(8,128)S(1)} %collective-permute-done.4.in1_ref, f32[32,512]{1,0:T(8,128)S(1)} %collective-permute-done.5.in2_ref, ...), custom_call_target="tpu_custom_call" | custom-call | flops 327680 | bytes 983040 | tf_op jit(solution)/shard_map/pallas_call | solution.py:190
  34.8 0.0 copy-start.4
  34.9 0.9 %collective-permute-start.7 = (bf16[256,512]{1,0:T(8,128)(2,1)S(1)}, bf16[256,512]{1,0:T(8,128)(2,1)S(1)}, u32[]{:S(2)}, u32[]{:S(2)}) collective-permute-start(bf16[256,512]{1,0:T(8,128)(2,1)S(1)} %get-tuple-element.40), channel_id=1, source_target_pairs={{0,4},{1,5},{2,6},{3,7},{4,0},{5,1},{6,2},{7,3},{8,12},{9,13},{10,... | collective-permute-start | bytes 786440 | tf_op jit(solution)/shard_map/ppermute | solution.py:597
  35.7 6.4 %all-to-all-start.1 = ((bf16[16,32,512]{2,1,0:T(8,128)(2,1)}), bf16[16,32,512]{2,1,0:T(8,128)(2,1)S(1)}, u32[]{:S(2)}, u32[]{:S(2)}) async-start(bf16[16,32,512]{2,1,0:T(8,128)(2,1)} %get-tuple-element.37), calls=%async_computation.1 | async-start | bytes 1048576 | tf_op jit(solution)/shard_map/all_to_all | solution.py:627
  42.1 2.1 %shard_map.174.refs_1_ = bf16[256,1024]{1,0:T(8,128)(2,1)} custom-call(s32[1,4096]{1,0:T(1,128)S(1)} %bitcast.20, s32[1,1024]{1,0:T(1,128)S(1)} %bitcast.24), custom_call_target="tpu_custom_call" | custom-call | flops 805306368 | bytes 524288 | tf_op jit(solution)/shard_map/pallas_call | solution.py:415
  44.2 0.0 collective-permute-done.7.refs_2_
  44.2 0.0 copy-done.4
  44.2 0.0 copy-done.7
  44.2 5.5 %shard_map.173.pre_hbm = bf16[1024,2048]{1,0:T(8,128)(2,1)} custom-call(s32[8,128]{1,0:T(8,128)S(1)} %bitcast.25, bf16[256,512]{1,0:T(8,128)(2,1)S(1)} %get-tuple-element.32.refs_0_, bf16[256,512]{1,0:T(8,128)(2,1)S(1)} %collective-permute-done.2.refs_1_, bf16[256,512]{1,0:T(8,128)(2,1)S(1)} %collective-permute-done.7.refs_2_, ...), custom_call_target="tpu_custom_call" | custom-call | flops 3221225472 | bytes 4194304 | tf_op jit(solution)/shard_map/pallas_call | solution.py:347
  49.7 1.5 %all-to-all-done.1 = bf16[16,32,512]{2,1,0:T(8,128)(2,1)S(1)} async-done(((bf16[16,32,512]{2,1,0:T(8,128)(2,1)}), bf16[16,32,512]{2,1,0:T(8,128)(2,1)S(1)}, u32[]{:S(2)}, u32[]{:S(2)}) %all-to-all-start.1) | async-done | bytes 524320 | tf_op jit(solution)/shard_map/all_to_all | solution.py:627
  51.2 5.4 %collective-permute-start.8 = (bf16[512,512]{1,0:T(8,128)(2,1)S(1)}, bf16[512,512]{1,0:T(8,128)(2,1)S(1)}, u32[]{:S(2)}, u32[]{:S(2)}) collective-permute-start(bf16[512,512]{1,0:T(8,128)(2,1)S(1)} %bitcast.14), channel_id=1, source_target_pairs={{0,1},{1,0},{2,3},{3,2},{4,5},{5,4},{6,7},{7,6},{8,9},{9,8},{10,11... | collective-permute-start | bytes 1572872 | tf_op jit(solution)/shard_map/ppermute | solution.py:634
  56.6 2.5 %shard_map.175 = (f32[1024,512]{1,0:T(8,128)S(1)}, bf16[1024,512]{1,0:T(8,128)(2,1)S(1)}, bf16[256,2048]{1,0:T(8,128)(2,1)S(1)}, bf16[512,2048]{1,0:T(8,128)(2,1)S(1)}) custom-call(bf16[512,512]{1,0:T(8,128)(2,1)S(1)} %bitcast.15, bf16[1024,2048]{1,0:T(8,128)(2,1)} %shard_map.173.pre_hbm, bf16[1024,2048]{1,0:T(8,128)(2,1)} %w_in_hbm.1, ...), custom_call_target="tpu_custom_call" | custom-call | flops 536870912 | bytes 6291456 | tf_op jit(solution)/shard_map/pallas_call | solution.py:464
  59.1 0.0 collective-permute-done.8.other_ref
  59.2 0.0 copy-done.5
  59.2 14.9 %shard_map.176 = f32[1024,2048]{1,0:T(8,128)} custom-call(f32[1024,512]{1,0:T(8,128)S(1)} %get-tuple-element.44.pool_ref, bf16[1024,512]{1,0:T(8,128)(2,1)S(1)} %get-tuple-element.45.count_ref, bf16[512,512]{1,0:T(8,128)(2,1)S(1)} %collective-permute-done.8.other_ref, bf16[512,2048]{1,0:T(8,128)(2,1)S(1)} %get-tuple-element.47.w_hot_ref, ...), custom_call_target="tpu_custom_call" | custom-call | flops 11274289152 | bytes 8388608 | tf_op jit(solution)/shard_map/pallas_call | solution.py:547
  (2 shorter events, 0.0 us)
Async XLA Ops:
  1.9 4.3 %collective-permute-start = (bf16[512,512]{1,0:T(8,128)(2,1)S(1)}, bf16[512,512]{1,0:T(8,128)(2,1)S(1)}, u32[]{:S(2)}, u32[]{:S(2)}) collective-permute-start(bf16[512,512]{1,0:T(8,128)(2,1)S(1)} %shard_map.165), channel_id=1, source_target_pairs={{0,1},{1,0},{2,3},{3,2},{4,5},{5,4},{6,7},{7,6},{8,9},{9,8},{10,11... | collective-permute-start | bytes 1572872 | tf_op jit(solution)/shard_map/ppermute | solution.py:601
  6.1 11.4 %collective-permute-start.1 = (bf16[512,512]{1,0:T(8,128)(2,1)S(1)}, bf16[512,512]{1,0:T(8,128)(2,1)S(1)}, u32[]{:S(2)}, u32[]{:S(2)}) collective-permute-start(bf16[512,512]{1,0:T(8,128)(2,1)S(1)} %get-tuple-element.31), channel_id=1, source_target_pairs={{0,1},{1,0},{2,3},{3,2},{4,5},{5,4},{6,7},{7,6},{8,9},{9,8},{10,11... | collective-permute-start | bytes 1572872 | tf_op jit(solution)/shard_map/ppermute | solution.py:610
  7.1 19.5 %all-to-all-start = ((bf16[16,32,512]{2,1,0:T(8,128)(2,1)}), bf16[16,32,512]{2,1,0:T(8,128)(2,1)S(1)}, u32[]{:S(2)}, u32[]{:S(2)}) async-start(bf16[16,32,512]{2,1,0:T(8,128)(2,1)} %bitcast.28), calls=%async_computation | async-start | bytes 1048576 | tf_op jit(solution)/shard_map/all_to_all | solution.py:607
  14.8 5.6 %copy-start.3 = (s32[1,1,4096]{2,1,0:T(1,128)S(1)}, s32[1,1,4096]{2,1,0:T(1,128)}, u32[]{:S(2)}) copy-start(s32[1,1,4096]{2,1,0:T(1,128)} %param.18) | copy-start | bytes 49156
  14.8 5.6 %copy-start.6 = (s32[1,1,1024]{2,1,0:T(1,128)S(1)}, s32[1,1,1024]{2,1,0:T(1,128)}, u32[]{:S(2)}) copy-start(s32[1,1,1024]{2,1,0:T(1,128)} %param.19) | copy-start | bytes 12292
  17.5 9.0 %collective-permute-start.2 = (bf16[256,512]{1,0:T(8,128)(2,1)S(1)}, bf16[256,512]{1,0:T(8,128)(2,1)S(1)}, u32[]{:S(2)}, u32[]{:S(2)}) collective-permute-start(bf16[256,512]{1,0:T(8,128)(2,1)S(1)} %get-tuple-element.34), channel_id=1, source_target_pairs={{0,2},{1,3},{2,4},{3,5},{4,6},{5,7},{6,0},{7,1},{8,10},{9,11},{10,... | collective-permute-start | bytes 786440 | tf_op jit(solution)/shard_map/ppermute | solution.py:597
  18.9 7.6 %collective-permute-start.3 = (bf16[256,512]{1,0:T(8,128)(2,1)S(1)}, bf16[256,512]{1,0:T(8,128)(2,1)S(1)}, u32[]{:S(2)}, u32[]{:S(2)}) collective-permute-start(bf16[256,512]{1,0:T(8,128)(2,1)S(1)} %get-tuple-element.35), channel_id=1, source_target_pairs={{0,6},{1,7},{2,0},{3,1},{4,2},{5,3},{6,4},{7,5},{8,14},{9,15},{10,... | collective-permute-start | bytes 786440 | tf_op jit(solution)/shard_map/ppermute | solution.py:597
  20.4 13.5 %copy-start = (f32[64,512]{1,0:T(8,128)S(1)}, f32[64,512]{1,0:T(8,128)}, u32[]{:S(2)}) copy-start(f32[64,512]{1,0:T(8,128)} %param.17) | copy-start | bytes 393220
  20.4 13.5 %copy-start.1 = (f32[64,512]{1,0:T(8,128)S(1)}, f32[64,512]{1,0:T(8,128)}, u32[]{:S(2)}) copy-start(f32[64,512]{1,0:T(8,128)} %param.15) | copy-start | bytes 393220
  20.4 13.5 %copy-start.2 = (f32[64,512]{1,0:T(8,128)S(1)}, f32[64,512]{1,0:T(8,128)}, u32[]{:S(2)}) copy-start(f32[64,512]{1,0:T(8,128)} %param.16) | copy-start | bytes 393220
  26.6 3.8 %collective-permute-start.6 = (f32[32,512]{1,0:T(8,128)S(1)}, f32[32,512]{1,0:T(8,128)S(1)}, u32[]{:S(2)}, u32[]{:S(2)}) collective-permute-start(f32[32,512]{1,0:T(8,128)S(1)} %shard_map.171.share_ref), channel_id=1, source_target_pairs={{0,6},{1,7},{2,0},{3,1},{4,2},{5,3},{6,4},{7,5},{8,14},{9,15},{10,... | collective-permute-start | bytes 196616 | tf_op jit(solution)/shard_map/ppermute | solution.py:597
  28.7 4.7 %collective-permute-start.5 = (f32[32,512]{1,0:T(8,128)S(1)}, f32[32,512]{1,0:T(8,128)S(1)}, u32[]{:S(2)}, u32[]{:S(2)}) collective-permute-start(f32[32,512]{1,0:T(8,128)S(1)} %shard_map.171.share_ref), channel_id=1, source_target_pairs={{0,4},{1,5},{2,6},{3,7},{4,0},{5,1},{6,2},{7,3},{8,12},{9,13},{10,... | collective-permute-start | bytes 196616 | tf_op jit(solution)/shard_map/ppermute | solution.py:597
  28.9 5.0 %collective-permute-start.4 = (f32[32,512]{1,0:T(8,128)S(1)}, f32[32,512]{1,0:T(8,128)S(1)}, u32[]{:S(2)}, u32[]{:S(2)}) collective-permute-start(f32[32,512]{1,0:T(8,128)S(1)} %shard_map.171.share_ref), channel_id=1, source_target_pairs={{0,2},{1,3},{2,4},{3,5},{4,6},{5,7},{6,0},{7,1},{8,10},{9,11},{10,... | collective-permute-start | bytes 196616 | tf_op jit(solution)/shard_map/ppermute | solution.py:597
  34.8 9.3 %copy-start.4 = (f32[2048]{0:T(1024)S(1)}, f32[2048]{0:T(1024)}, u32[]{:S(2)}) copy-start(f32[2048]{0:T(1024)} %param.25) | copy-start | bytes 24580
  34.9 9.4 %copy-start.7 = (s32[1,1,8,128]{3,2,1,0:T(8,128)S(1)}, s32[1,1,8,128]{3,2,1,0:T(8,128)}, u32[]{:S(2)}) copy-start(s32[1,1,8,128]{3,2,1,0:T(8,128)} %param.23) | copy-start | bytes 12292
  34.9 9.3 %collective-permute-start.7 = (bf16[256,512]{1,0:T(8,128)(2,1)S(1)}, bf16[256,512]{1,0:T(8,128)(2,1)S(1)}, u32[]{:S(2)}, u32[]{:S(2)}) collective-permute-start(bf16[256,512]{1,0:T(8,128)(2,1)S(1)} %get-tuple-element.40), channel_id=1, source_target_pairs={{0,4},{1,5},{2,6},{3,7},{4,0},{5,1},{6,2},{7,3},{8,12},{9,13},{10,... | collective-permute-start | bytes 786440 | tf_op jit(solution)/shard_map/ppermute | solution.py:597
  35.7 15.5 %all-to-all-start.1 = ((bf16[16,32,512]{2,1,0:T(8,128)(2,1)}), bf16[16,32,512]{2,1,0:T(8,128)(2,1)S(1)}, u32[]{:S(2)}, u32[]{:S(2)}) async-start(bf16[16,32,512]{2,1,0:T(8,128)(2,1)} %get-tuple-element.37), calls=%async_computation.1 | async-start | bytes 1048576 | tf_op jit(solution)/shard_map/all_to_all | solution.py:627
  51.2 8.0 %copy-start.5 = (f32[2048]{0:T(1024)S(1)}, f32[2048]{0:T(1024)}, u32[]{:S(2)}) copy-start(f32[2048]{0:T(1024)} %param.27) | copy-start | bytes 24580
  51.2 8.0 %collective-permute-start.8 = (bf16[512,512]{1,0:T(8,128)(2,1)S(1)}, bf16[512,512]{1,0:T(8,128)(2,1)S(1)}, u32[]{:S(2)}, u32[]{:S(2)}) collective-permute-start(bf16[512,512]{1,0:T(8,128)(2,1)S(1)} %bitcast.14), channel_id=1, source_target_pairs={{0,1},{1,0},{2,3},{3,2},{4,5},{5,4},{6,7},{7,6},{8,9},{9,8},{10,11... | collective-permute-start | bytes 1572872 | tf_op jit(solution)/shard_map/ppermute | solution.py:634

commit v4 on v3

--- a/solution.py
+++ b/solution.py
@@ -618,9 +618,9 @@
     early = blocks_in_all * 3 // 4
     (ids_now,) = after(blocks[0], ids)
     count_low = count_matrix(ids_now, lengths, hot, own, 0, early)
-    parts, *_ = lax.optimization_barrier((parts, count_low, rows_in[1], rows_in[-1]))
+    (parts,) = after(count_low, parts)
     share = sum_parts(parts)
-    shares_in = [along(share, s) for s in range(1, lines)]
+    shares_in = [along(share, s) for s in (1, 3, 2)]
     spread, new_master, new_first, new_second = update(
         share, shares_in, hot_master, first_moment, second_moment, n_dp, lines, own
     )

time: 74.5 us -> 71.4 us (0.958)
  waiting for transfers between devices: 6.05 us -> 4.36 us
  starting transfers between devices: 27.5 us -> 26.1 us
    ppermute x6, waiting for transfers between devices: 4.57 us -> 1.93 us  [along(): return lax.ppermute(array, 'table', pairs)]
    all_to_all x1, waiting for transfers between devices: 0.01 us -> 2.18 us  [on_device(): lax.all_to_all(chip.reshape(n_dp, lines * own, width), 'dp', split_axis=0...]
    all_to_all x1, starting transfers between devices: 6.35 us -> 4.98 us  [on_device(): lax.all_to_all(spread, 'dp', split_axis=0, concat_axis=0, tiled=True)]
    all_to_all x1, waiting for transfers between devices: 1.47 us -> 0.25 us  [on_device(): lax.all_to_all(spread, 'dp', split_axis=0, concat_axis=0, tiled=True)]
    ppermute x1, starting transfers between devices: 5.43 us -> 4.6 us  [on_device(): fresh_other = lax.ppermute(fresh_own, 'table', swap)]
    ppermute x6, starting transfers between devices: 6.45 us -> 7.21 us  [along(): return lax.ppermute(array, 'table', pairs)]
  transfers between devices with their start and end apart: 11 -> 11, of which waited for: 4 -> 4; matrix products, arithmetic and copies ran while one was open for 0% -> 0% of each run, Pallas kernels for 30% -> 33%
where the time goes in v4:
time: 71.4 us; the launch traced here: 70.9 us
  Pallas kernels  39.6 us (55%)
  starting transfers between devices  26.1 us (37%)
  waiting for transfers between devices  4.36 us (6%)
  between operations  0.83 us (1%)
    pallas_call x1, Pallas kernels, mlp(): pl.pallas_call(mlp_kernel, out_shape=jax.ShapeDtypeStruct((batch, wide),...  14.9 us
    pallas_call x2, Pallas kernels, count_matrix(): pl.pallas_call(functools.partial(count_kernel, low_block, own), out_shape...  8.18 us
    all_to_all x1, starting transfers between devices, on_device(): lax.all_to_all(chip.reshape(n_dp, lines * own, width), 'dp', split_axis=0...  7.7 us
    ppermute x6, starting transfers between devices, along(): return lax.ppermute(array, 'table', pairs)  7.21 us
    pallas_call x1, Pallas kernels, cold_half(): pl.pallas_call(cold_kernel, out_shape=pltpu.HBM((batch, hidden), BF16), i...  5.47 us
    pallas_call x2, Pallas kernels, pick(): pl.pallas_call(functools.partial(pick_kernel, grad is not None), out_shap...  5.32 us
    all_to_all x1, starting transfers between devices, on_device(): lax.all_to_all(spread, 'dp', split_axis=0, concat_axis=0, tiled=True)  4.98 us
    ppermute x1, starting transfers between devices, on_device(): fresh_other = lax.ppermute(fresh_own, 'table', swap)  4.6 us
  transfers between devices with their start and end apart: 11, of which 4 were waited for; matrix products, arithmetic and copies ran while one was open for 0% of the time, Pallas kernels for 33%

profile of v4, /device:TPU:1, one launch (start us, length us, event | category | flops | bytes accessed | tf_op | source)
XLA Modules:
  0.0 70.9 jit_solution(1977069777187566766)
XLA Ops:
  0.6 1.2 %shard_map.165 = bf16[512,512]{1,0:T(8,128)(2,1)S(1)} custom-call(f32[16,4,2,8,512]{4,3,2,1,0:T(8,128)} %bitcast.26), custom_call_target="tpu_custom_call" | custom-call | bytes 1572864 | tf_op jit(solution)/shard_map/pallas_call | solution.py:101
  1.9 1.5 %collective-permute-start = (bf16[512,512]{1,0:T(8,128)(2,1)S(1)}, bf16[512,512]{1,0:T(8,128)(2,1)S(1)}, u32[]{:S(2)}, u32[]{:S(2)}) collective-permute-start(bf16[512,512]{1,0:T(8,128)(2,1)S(1)} %shard_map.165), channel_id=1, source_target_pairs={{0,1},{1,0},{2,3},{3,2},{4,5},{5,4},{6,7},{7,6},{8,9},{9,8},{10,11... | collective-permute-start | bytes 1572872 | tf_op jit(solution)/shard_map/ppermute | solution.py:601
  3.4 2.7 %shard_map.166 = (bf16[512,512]{1,0:T(8,128)(2,1)S(1)}, f32[16,4,8,512]{3,2,1,0:T(8,128)S(1)}) custom-call(s32[8,128]{1,0:T(8,128)} %bitcast.29, s32[1,8]{1,0:T(1,128)} %bitcast.31, bf16[2048,512]{1,0:T(8,128)(2,1)} %table_hbm.3, f32[16,4,2,8,512]{4,3,2,1,0:T(8,128)} %bitcast.27), custom_call_target="tpu_custom_call" | custom-call | flops 1073741824 | bytes 2097152 | tf_op jit(solution)/shard_map/pallas_call | solution.py:269
  6.1 0.1 collective-permute-start.1
  6.2 0.0 collective-permute-done.other_ref
  6.2 0.9 %shard_map.167 = bf16[512,512]{1,0:T(8,128)(2,1)} custom-call(f32[16,4,8,512]{3,2,1,0:T(8,128)S(1)} %get-tuple-element.29.mine_ref, bf16[512,512]{1,0:T(8,128)(2,1)S(1)} %collective-permute-done.other_ref), custom_call_target="tpu_custom_call" | custom-call | bytes 2097152 | tf_op jit(solution)/shard_map/pallas_call | solution.py:131
  7.0 7.7 %all-to-all-start = ((bf16[16,32,512]{2,1,0:T(8,128)(2,1)}), bf16[16,32,512]{2,1,0:T(8,128)(2,1)S(1)}, u32[]{:S(2)}, u32[]{:S(2)}) async-start(bf16[16,32,512]{2,1,0:T(8,128)(2,1)} %bitcast.28), calls=%async_computation | async-start | bytes 1048576 | tf_op jit(solution)/shard_map/all_to_all | solution.py:607
  14.8 0.0 copy-start.3
  14.8 0.0 copy-start.6
  14.8 2.6 %shard_map.168.near_ref = bf16[512,512]{1,0:T(8,128)(2,1)S(1)} custom-call(s32[8,128]{1,0:T(8,128)} %bitcast.30, s32[1,8]{1,0:T(1,128)} %bitcast.32, bf16[2048,512]{1,0:T(8,128)(2,1)} %table_hbm.3), custom_call_target="tpu_custom_call" | custom-call | flops 1073741824 | bytes 2097152 | tf_op jit(solution)/shard_map/pallas_call | solution.py:269
  17.4 0.0 collective-permute-done.1.far_ref
  17.4 0.1 shard_map.169
  17.5 0.0 copy-done.3
  17.5 0.0 copy-done.6
  17.5 0.0 copy-start
  17.5 0.0 copy-start.1
  17.6 0.0 copy-start.2
  17.6 5.6 %shard_map.170.refs_0_ = bf16[768,1024]{1,0:T(8,128)(2,1)} custom-call(s32[1,4096]{1,0:T(1,128)S(1)} %bitcast.19, s32[1,1024]{1,0:T(1,128)S(1)} %bitcast.23), custom_call_target="tpu_custom_call" | custom-call | flops 2415919104 | bytes 1572864 | tf_op jit(solution)/shard_map/pallas_call | solution.py:415
  23.2 2.2 %all-to-all-done.parts_ref = bf16[16,32,512]{2,1,0:T(8,128)(2,1)S(1)} async-done(((bf16[16,32,512]{2,1,0:T(8,128)(2,1)}), bf16[16,32,512]{2,1,0:T(8,128)(2,1)S(1)}, u32[]{:S(2)}, u32[]{:S(2)}) %all-to-all-start) | async-done | bytes 524320 | tf_op jit(solution)/shard_map/all_to_all | solution.py:607
  25.3 0.1 shard_map.171.share_ref
  25.4 3.0 %collective-permute-start.4 = (f32[32,512]{1,0:T(8,128)S(1)}, f32[32,512]{1,0:T(8,128)S(1)}, u32[]{:S(2)}, u32[]{:S(2)}) collective-permute-start(f32[32,512]{1,0:T(8,128)S(1)} %shard_map.171.share_ref), channel_id=1, source_target_pairs={{0,4},{1,5},{2,6},{3,7},{4,0},{5,1},{6,2},{7,3},{8,12},{9,13},{10,... | collective-permute-start | bytes 196616 | tf_op jit(solution)/shard_map/ppermute | solution.py:597
  28.4 0.8 %collective-permute-start.3 = (f32[32,512]{1,0:T(8,128)S(1)}, f32[32,512]{1,0:T(8,128)S(1)}, u32[]{:S(2)}, u32[]{:S(2)}) collective-permute-start(f32[32,512]{1,0:T(8,128)S(1)} %shard_map.171.share_ref), channel_id=1, source_target_pairs={{0,6},{1,7},{2,0},{3,1},{4,2},{5,3},{6,4},{7,5},{8,14},{9,15},{10,... | collective-permute-start | bytes 196616 | tf_op jit(solution)/shard_map/ppermute | solution.py:597
  29.2 0.7 collective-permute-start.2
  29.9 0.4 collective-permute-start.5
  30.3 2.3 %collective-permute-start.7 = (bf16[256,512]{1,0:T(8,128)(2,1)S(1)}, bf16[256,512]{1,0:T(8,128)(2,1)S(1)}, u32[]{:S(2)}, u32[]{:S(2)}) collective-permute-start(bf16[256,512]{1,0:T(8,128)(2,1)S(1)} %get-tuple-element.40), channel_id=1, source_target_pairs={{0,6},{1,7},{2,0},{3,1},{4,2},{5,3},{6,4},{7,5},{8,14},{9,15},{10,... | collective-permute-start | bytes 786440 | tf_op jit(solution)/shard_map/ppermute | solution.py:597
  32.5 0.0 collective-permute-done.4.in3_ref
  32.5 0.0 collective-permute-done.3.in2_ref
  32.5 1.1 %collective-permute-done.2.in1_ref = f32[32,512]{1,0:T(8,128)S(1)} collective-permute-done((f32[32,512]{1,0:T(8,128)S(1)}, f32[32,512]{1,0:T(8,128)S(1)}, u32[]{:S(2)}, u32[]{:S(2)}) %collective-permute-start.2) | collective-permute-done | bytes 65568 | tf_op jit(solution)/shard_map/ppermute | solution.py:597
  33.6 0.0 copy-done
  33.6 0.0 copy-done.1
  33.6 0.0 copy-done.2
  33.7 0.9 %shard_map.172 = (bf16[16,32,512]{2,1,0:T(8,128)(2,1)}, f32[8,512]{1,0:T(8,128)}, f32[8,512]{1,0:T(8,128)}, f32[8,512]{1,0:T(8,128)}) custom-call(f32[32,512]{1,0:T(8,128)S(1)} %shard_map.171.share_ref, f32[32,512]{1,0:T(8,128)S(1)} %collective-permute-done.2.in1_ref, f32[32,512]{1,0:T(8,128)S(1)} %collective-permute-done.3.in2_ref, ...), custom_call_target="tpu_custom_call" | custom-call | flops 327680 | bytes 983040 | tf_op jit(solution)/shard_map/pallas_call | solution.py:190
  34.6 0.0 copy-start.4
  34.6 0.1 collective-permute-start.6
  34.7 5.0 %all-to-all-start.1 = ((bf16[16,32,512]{2,1,0:T(8,128)(2,1)}), bf16[16,32,512]{2,1,0:T(8,128)(2,1)S(1)}, u32[]{:S(2)}, u32[]{:S(2)}) async-start(bf16[16,32,512]{2,1,0:T(8,128)(2,1)} %get-tuple-element.35), calls=%async_computation.1 | async-start | bytes 1048576 | tf_op jit(solution)/shard_map/all_to_all | solution.py:627
  39.7 2.6 %shard_map.174.refs_1_ = bf16[256,1024]{1,0:T(8,128)(2,1)} custom-call(s32[1,4096]{1,0:T(1,128)S(1)} %bitcast.20, s32[1,1024]{1,0:T(1,128)S(1)} %bitcast.24), custom_call_target="tpu_custom_call" | custom-call | flops 805306368 | bytes 524288 | tf_op jit(solution)/shard_map/pallas_call | solution.py:415
  42.3 0.0 collective-permute-done.5.refs_1_
  42.3 0.0 collective-permute-done.7.refs_3_
  42.3 0.8 %collective-permute-done.6.refs_2_ = bf16[256,512]{1,0:T(8,128)(2,1)S(1)} collective-permute-done((bf16[256,512]{1,0:T(8,128)(2,1)S(1)}, bf16[256,512]{1,0:T(8,128)(2,1)S(1)}, u32[]{:S(2)}, u32[]{:S(2)}) %collective-permute-start.6) | collective-permute-done | bytes 262176 | tf_op jit(solution)/shard_map/ppermute | solution.py:597
  43.1 0.0 copy-done.4
  43.1 0.0 copy-done.7
  43.1 5.5 %shard_map.173.pre_hbm = bf16[1024,2048]{1,0:T(8,128)(2,1)} custom-call(s32[8,128]{1,0:T(8,128)S(1)} %bitcast.25, bf16[256,512]{1,0:T(8,128)(2,1)S(1)} %get-tuple-element.32.refs_0_, bf16[256,512]{1,0:T(8,128)(2,1)S(1)} %collective-permute-done.5.refs_1_, bf16[256,512]{1,0:T(8,128)(2,1)S(1)} %collective-permute-done.6.refs_2_, ...), custom_call_target="tpu_custom_call" | custom-call | flops 3221225472 | bytes 4194304 | tf_op jit(solution)/shard_map/pallas_call | solution.py:347
  48.6 0.3 all-to-all-done.1
  48.9 4.6 %collective-permute-start.8 = (bf16[512,512]{1,0:T(8,128)(2,1)S(1)}, bf16[512,512]{1,0:T(8,128)(2,1)S(1)}, u32[]{:S(2)}, u32[]{:S(2)}) collective-permute-start(bf16[512,512]{1,0:T(8,128)(2,1)S(1)} %bitcast.14), channel_id=1, source_target_pairs={{0,1},{1,0},{2,3},{3,2},{4,5},{5,4},{6,7},{7,6},{8,9},{9,8},{10,11... | collective-permute-start | bytes 1572872 | tf_op jit(solution)/shard_map/ppermute | solution.py:634
  53.5 2.5 %shard_map.175 = (f32[1024,512]{1,0:T(8,128)S(1)}, bf16[1024,512]{1,0:T(8,128)(2,1)S(1)}, bf16[256,2048]{1,0:T(8,128)(2,1)S(1)}, bf16[512,2048]{1,0:T(8,128)(2,1)S(1)}) custom-call(bf16[512,512]{1,0:T(8,128)(2,1)S(1)} %bitcast.15, bf16[1024,2048]{1,0:T(8,128)(2,1)} %shard_map.173.pre_hbm, bf16[1024,2048]{1,0:T(8,128)(2,1)} %w_in_hbm.1, ...), custom_call_target="tpu_custom_call" | custom-call | flops 536870912 | bytes 6291456 | tf_op jit(solution)/shard_map/pallas_call | solution.py:464
  56.0 0.0 collective-permute-done.8.other_ref
  56.0 0.0 copy-done.5
  56.0 14.9 %shard_map.176 = f32[1024,2048]{1,0:T(8,128)} custom-call(f32[1024,512]{1,0:T(8,128)S(1)} %get-tuple-element.44.pool_ref, bf16[1024,512]{1,0:T(8,128)(2,1)S(1)} %get-tuple-element.45.count_ref, bf16[512,512]{1,0:T(8,128)(2,1)S(1)} %collective-permute-done.8.other_ref, bf16[512,2048]{1,0:T(8,128)(2,1)S(1)} %get-tuple-element.47.w_hot_ref, ...), custom_call_target="tpu_custom_call" | custom-call | flops 11274289152 | bytes 8388608 | tf_op jit(solution)/shard_map/pallas_call | solution.py:547
  (2 shorter events, 0.0 us)
Async XLA Ops:
  1.9 4.3 %collective-permute-start = (bf16[512,512]{1,0:T(8,128)(2,1)S(1)}, bf16[512,512]{1,0:T(8,128)(2,1)S(1)}, u32[]{:S(2)}, u32[]{:S(2)}) collective-permute-start(bf16[512,512]{1,0:T(8,128)(2,1)S(1)} %shard_map.165), channel_id=1, source_target_pairs={{0,1},{1,0},{2,3},{3,2},{4,5},{5,4},{6,7},{7,6},{8,9},{9,8},{10,11... | collective-permute-start | bytes 1572872 | tf_op jit(solution)/shard_map/ppermute | solution.py:601
  6.1 11.4 %collective-permute-start.1 = (bf16[512,512]{1,0:T(8,128)(2,1)S(1)}, bf16[512,512]{1,0:T(8,128)(2,1)S(1)}, u32[]{:S(2)}, u32[]{:S(2)}) collective-permute-start(bf16[512,512]{1,0:T(8,128)(2,1)S(1)} %get-tuple-element.31), channel_id=1, source_target_pairs={{0,1},{1,0},{2,3},{3,2},{4,5},{5,4},{6,7},{7,6},{8,9},{9,8},{10,11... | collective-permute-start | bytes 1572872 | tf_op jit(solution)/shard_map/ppermute | solution.py:610
  7.0 18.3 %all-to-all-start = ((bf16[16,32,512]{2,1,0:T(8,128)(2,1)}), bf16[16,32,512]{2,1,0:T(8,128)(2,1)S(1)}, u32[]{:S(2)}, u32[]{:S(2)}) async-start(bf16[16,32,512]{2,1,0:T(8,128)(2,1)} %bitcast.28), calls=%async_computation | async-start | bytes 1048576 | tf_op jit(solution)/shard_map/all_to_all | solution.py:607
  14.8 2.8 %copy-start.3 = (s32[1,1,4096]{2,1,0:T(1,128)S(1)}, s32[1,1,4096]{2,1,0:T(1,128)}, u32[]{:S(2)}) copy-start(s32[1,1,4096]{2,1,0:T(1,128)} %param.18) | copy-start | bytes 49156
  14.8 2.8 %copy-start.6 = (s32[1,1,1024]{2,1,0:T(1,128)S(1)}, s32[1,1,1024]{2,1,0:T(1,128)}, u32[]{:S(2)}) copy-start(s32[1,1,1024]{2,1,0:T(1,128)} %param.19) | copy-start | bytes 12292
  17.5 16.1 %copy-start = (f32[64,512]{1,0:T(8,128)S(1)}, f32[64,512]{1,0:T(8,128)}, u32[]{:S(2)}) copy-start(f32[64,512]{1,0:T(8,128)} %param.17) | copy-start | bytes 393220
  17.5 16.1 %copy-start.1 = (f32[64,512]{1,0:T(8,128)S(1)}, f32[64,512]{1,0:T(8,128)}, u32[]{:S(2)}) copy-start(f32[64,512]{1,0:T(8,128)} %param.15) | copy-start | bytes 393220
  17.6 16.1 %copy-start.2 = (f32[64,512]{1,0:T(8,128)S(1)}, f32[64,512]{1,0:T(8,128)}, u32[]{:S(2)}) copy-start(f32[64,512]{1,0:T(8,128)} %param.16) | copy-start | bytes 393220
  25.4 7.1 %collective-permute-start.4 = (f32[32,512]{1,0:T(8,128)S(1)}, f32[32,512]{1,0:T(8,128)S(1)}, u32[]{:S(2)}, u32[]{:S(2)}) collective-permute-start(f32[32,512]{1,0:T(8,128)S(1)} %shard_map.171.share_ref), channel_id=1, source_target_pairs={{0,4},{1,5},{2,6},{3,7},{4,0},{5,1},{6,2},{7,3},{8,12},{9,13},{10,... | collective-permute-start | bytes 196616 | tf_op jit(solution)/shard_map/ppermute | solution.py:597
  28.4 4.2 %collective-permute-start.3 = (f32[32,512]{1,0:T(8,128)S(1)}, f32[32,512]{1,0:T(8,128)S(1)}, u32[]{:S(2)}, u32[]{:S(2)}) collective-permute-start(f32[32,512]{1,0:T(8,128)S(1)} %shard_map.171.share_ref), channel_id=1, source_target_pairs={{0,6},{1,7},{2,0},{3,1},{4,2},{5,3},{6,4},{7,5},{8,14},{9,15},{10,... | collective-permute-start | bytes 196616 | tf_op jit(solution)/shard_map/ppermute | solution.py:597
  29.2 4.5 %collective-permute-start.2 = (f32[32,512]{1,0:T(8,128)S(1)}, f32[32,512]{1,0:T(8,128)S(1)}, u32[]{:S(2)}, u32[]{:S(2)}) collective-permute-start(f32[32,512]{1,0:T(8,128)S(1)} %shard_map.171.share_ref), channel_id=1, source_target_pairs={{0,2},{1,3},{2,4},{3,5},{4,6},{5,7},{6,0},{7,1},{8,10},{9,11},{10,... | collective-permute-start | bytes 196616 | tf_op jit(solution)/shard_map/ppermute | solution.py:597
  29.9 12.4 %collective-permute-start.5 = (bf16[256,512]{1,0:T(8,128)(2,1)S(1)}, bf16[256,512]{1,0:T(8,128)(2,1)S(1)}, u32[]{:S(2)}, u32[]{:S(2)}) collective-permute-start(bf16[256,512]{1,0:T(8,128)(2,1)S(1)} %get-tuple-element.38), channel_id=1, source_target_pairs={{0,2},{1,3},{2,4},{3,5},{4,6},{5,7},{6,0},{7,1},{8,10},{9,11},{10,... | collective-permute-start | bytes 786440 | tf_op jit(solution)/shard_map/ppermute | solution.py:597
  30.3 12.0 %collective-permute-start.7 = (bf16[256,512]{1,0:T(8,128)(2,1)S(1)}, bf16[256,512]{1,0:T(8,128)(2,1)S(1)}, u32[]{:S(2)}, u32[]{:S(2)}) collective-permute-start(bf16[256,512]{1,0:T(8,128)(2,1)S(1)} %get-tuple-element.40), channel_id=1, source_target_pairs={{0,6},{1,7},{2,0},{3,1},{4,2},{5,3},{6,4},{7,5},{8,14},{9,15},{10,... | collective-permute-start | bytes 786440 | tf_op jit(solution)/shard_map/ppermute | solution.py:597
  34.6 8.5 %copy-start.4 = (f32[2048]{0:T(1024)S(1)}, f32[2048]{0:T(1024)}, u32[]{:S(2)}) copy-start(f32[2048]{0:T(1024)} %param.25) | copy-start | bytes 24580
  34.6 8.5 %copy-start.7 = (s32[1,1,8,128]{3,2,1,0:T(8,128)S(1)}, s32[1,1,8,128]{3,2,1,0:T(8,128)}, u32[]{:S(2)}) copy-start(s32[1,1,8,128]{3,2,1,0:T(8,128)} %param.23) | copy-start | bytes 12292
  34.6 8.5 %collective-permute-start.6 = (bf16[256,512]{1,0:T(8,128)(2,1)S(1)}, bf16[256,512]{1,0:T(8,128)(2,1)S(1)}, u32[]{:S(2)}, u32[]{:S(2)}) collective-permute-start(bf16[256,512]{1,0:T(8,128)(2,1)S(1)} %get-tuple-element.39), channel_id=1, source_target_pairs={{0,4},{1,5},{2,6},{3,7},{4,0},{5,1},{6,2},{7,3},{8,12},{9,13},{10,... | collective-permute-start | bytes 786440 | tf_op jit(solution)/shard_map/ppermute | solution.py:597
  34.7 14.2 %all-to-all-start.1 = ((bf16[16,32,512]{2,1,0:T(8,128)(2,1)}), bf16[16,32,512]{2,1,0:T(8,128)(2,1)S(1)}, u32[]{:S(2)}, u32[]{:S(2)}) async-start(bf16[16,32,512]{2,1,0:T(8,128)(2,1)} %get-tuple-element.35), calls=%async_computation.1 | async-start | bytes 1048576 | tf_op jit(solution)/shard_map/all_to_all | solution.py:627
  48.9 7.2 %copy-start.5 = (f32[2048]{0:T(1024)S(1)}, f32[2048]{0:T(1024)}, u32[]{:S(2)}) copy-start(f32[2048]{0:T(1024)} %param.27) | copy-start | bytes 24580
  48.9 7.2 %collective-permute-start.8 = (bf16[512,512]{1,0:T(8,128)(2,1)S(1)}, bf16[512,512]{1,0:T(8,128)(2,1)S(1)}, u32[]{:S(2)}, u32[]{:S(2)}) collective-permute-start(bf16[512,512]{1,0:T(8,128)(2,1)S(1)} %bitcast.14), channel_id=1, source_target_pairs={{0,1},{1,0},{2,3},{3,2},{4,5},{5,4},{6,7},{7,6},{8,9},{9,8},{10,11... | collective-permute-start | bytes 1572872 | tf_op jit(solution)/shard_map/ppermute | solution.py:634

commit v5 on v4

--- a/solution.py
+++ b/solution.py
@@ -615,7 +615,7 @@
 
     ids, lengths = hot_ids[0], hot_lengths[0]
     blocks_in_all = batch // BAGS
-    early = blocks_in_all * 3 // 4
+    early = blocks_in_all // 2
     (ids_now,) = after(blocks[0], ids)
     count_low = count_matrix(ids_now, lengths, hot, own, 0, early)
     (parts,) = after(count_low, parts)

time: 71.4 us -> 71 us (level)
  starting transfers between devices: 26.1 us -> 24.4 us
  waiting for transfers between devices: 4.36 us -> 5.53 us
    all_to_all x1, starting transfers between devices: 4.98 us -> 3.57 us  [on_device(): lax.all_to_all(spread, 'dp', split_axis=0, concat_axis=0, tiled=True)]
    all_to_all x1, waiting for transfers between devices: 2.18 us -> 3.43 us  [on_device(): lax.all_to_all(chip.reshape(n_dp, lines * own, width), 'dp', split_axis=0...]
  transfers between devices with their start and end apart: 11 -> 11, of which waited for: 4 -> 3; matrix products, arithmetic and copies ran while one was open for 0% -> 0% of each run, Pallas kernels for 33% -> 33%
where the time goes in v5:
time: 71 us; the launch traced here: 70.6 us
  Pallas kernels  39.8 us (56%)
  starting transfers between devices  24.4 us (34%)
  waiting for transfers between devices  5.53 us (8%)
  between operations  0.86 us (1%)
    pallas_call x1, Pallas kernels, mlp(): pl.pallas_call(mlp_kernel, out_shape=jax.ShapeDtypeStruct((batch, wide),...  15 us
    pallas_call x2, Pallas kernels, count_matrix(): pl.pallas_call(functools.partial(count_kernel, low_block, own), out_shape...  8.19 us
    all_to_all x1, starting transfers between devices, on_device(): lax.all_to_all(chip.reshape(n_dp, lines * own, width), 'dp', split_axis=0...  7.7 us
    ppermute x6, starting transfers between devices, along(): return lax.ppermute(array, 'table', pairs)  7.21 us
    pallas_call x1, Pallas kernels, cold_half(): pl.pallas_call(cold_kernel, out_shape=pltpu.HBM((batch, hidden), BF16), i...  5.6 us
    pallas_call x2, Pallas kernels, pick(): pl.pallas_call(functools.partial(pick_kernel, grad is not None), out_shap...  5.31 us
    ppermute x1, starting transfers between devices, on_device(): fresh_other = lax.ppermute(fresh_own, 'table', swap)  4.32 us
    all_to_all x1, starting transfers between devices, on_device(): lax.all_to_all(spread, 'dp', split_axis=0, concat_axis=0, tiled=True)  3.57 us
  transfers between devices with their start and end apart: 11, of which 3 were waited for; matrix products, arithmetic and copies ran while one was open for 0% of the time, Pallas kernels for 33%

profile of v5, /device:TPU:1, one launch (start us, length us, event | category | flops | bytes accessed | tf_op | source)
XLA Modules:
  0.0 70.6 jit_solution(10251791847086049812)
XLA Ops:
  0.6 1.2 %shard_map.165 = bf16[512,512]{1,0:T(8,128)(2,1)S(1)} custom-call(f32[16,4,2,8,512]{4,3,2,1,0:T(8,128)} %bitcast.26), custom_call_target="tpu_custom_call" | custom-call | bytes 1572864 | tf_op jit(solution)/shard_map/pallas_call | solution.py:101
  1.9 1.5 %collective-permute-start = (bf16[512,512]{1,0:T(8,128)(2,1)S(1)}, bf16[512,512]{1,0:T(8,128)(2,1)S(1)}, u32[]{:S(2)}, u32[]{:S(2)}) collective-permute-start(bf16[512,512]{1,0:T(8,128)(2,1)S(1)} %shard_map.165), channel_id=1, source_target_pairs={{0,1},{1,0},{2,3},{3,2},{4,5},{5,4},{6,7},{7,6},{8,9},{9,8},{10,11... | collective-permute-start | bytes 1572872 | tf_op jit(solution)/shard_map/ppermute | solution.py:601
  3.4 2.7 %shard_map.166 = (bf16[512,512]{1,0:T(8,128)(2,1)S(1)}, f32[16,4,8,512]{3,2,1,0:T(8,128)S(1)}) custom-call(s32[8,128]{1,0:T(8,128)} %bitcast.29, s32[1,8]{1,0:T(1,128)} %bitcast.31, bf16[2048,512]{1,0:T(8,128)(2,1)} %table_hbm.3, f32[16,4,2,8,512]{4,3,2,1,0:T(8,128)} %bitcast.27), custom_call_target="tpu_custom_call" | custom-call | flops 1073741824 | bytes 2097152 | tf_op jit(solution)/shard_map/pallas_call | solution.py:269
  6.1 0.0 copy-start.3
  6.1 0.0 copy-start.6
  6.1 0.1 collective-permute-start.1
  6.2 0.0 collective-permute-done.other_ref
  6.2 0.9 %shard_map.167 = bf16[512,512]{1,0:T(8,128)(2,1)} custom-call(f32[16,4,8,512]{3,2,1,0:T(8,128)S(1)} %get-tuple-element.29.mine_ref, bf16[512,512]{1,0:T(8,128)(2,1)S(1)} %collective-permute-done.other_ref), custom_call_target="tpu_custom_call" | custom-call | bytes 2097152 | tf_op jit(solution)/shard_map/pallas_call | solution.py:131
  7.1 7.7 %all-to-all-start = ((bf16[16,32,512]{2,1,0:T(8,128)(2,1)}), bf16[16,32,512]{2,1,0:T(8,128)(2,1)S(1)}, u32[]{:S(2)}, u32[]{:S(2)}) async-start(bf16[16,32,512]{2,1,0:T(8,128)(2,1)} %bitcast.28), calls=%async_computation | async-start | bytes 1048576 | tf_op jit(solution)/shard_map/all_to_all | solution.py:607
  14.8 2.6 %shard_map.168.near_ref = bf16[512,512]{1,0:T(8,128)(2,1)S(1)} custom-call(s32[8,128]{1,0:T(8,128)} %bitcast.30, s32[1,8]{1,0:T(1,128)} %bitcast.32, bf16[2048,512]{1,0:T(8,128)(2,1)} %table_hbm.3), custom_call_target="tpu_custom_call" | custom-call | flops 1073741824 | bytes 2097152 | tf_op jit(solution)/shard_map/pallas_call | solution.py:269
  17.4 0.0 copy-start
  17.4 0.0 copy-start.1
  17.4 0.0 copy-start.2
  17.5 0.0 collective-permute-done.1.far_ref
  17.5 0.1 shard_map.169
  17.5 0.0 copy-done.3
  17.6 0.0 copy-done.6
  17.6 4.3 %shard_map.170.refs_0_ = bf16[512,1024]{1,0:T(8,128)(2,1)} custom-call(s32[1,4096]{1,0:T(1,128)S(1)} %bitcast.19, s32[1,1024]{1,0:T(1,128)S(1)} %bitcast.23), custom_call_target="tpu_custom_call" | custom-call | flops 1610612736 | bytes 1048576 | tf_op jit(solution)/shard_map/pallas_call | solution.py:415
  21.9 0.0 copy-start.4
  21.9 0.0 copy-start.7
  21.9 3.4 %all-to-all-done.parts_ref = bf16[16,32,512]{2,1,0:T(8,128)(2,1)S(1)} async-done(((bf16[16,32,512]{2,1,0:T(8,128)(2,1)}), bf16[16,32,512]{2,1,0:T(8,128)(2,1)S(1)}, u32[]{:S(2)}, u32[]{:S(2)}) %all-to-all-start) | async-done | bytes 524320 | tf_op jit(solution)/shard_map/all_to_all | solution.py:607
  25.4 0.1 shard_map.171.share_ref
  25.4 3.0 %collective-permute-start.4 = (f32[32,512]{1,0:T(8,128)S(1)}, f32[32,512]{1,0:T(8,128)S(1)}, u32[]{:S(2)}, u32[]{:S(2)}) collective-permute-start(f32[32,512]{1,0:T(8,128)S(1)} %shard_map.171.share_ref), channel_id=1, source_target_pairs={{0,4},{1,5},{2,6},{3,7},{4,0},{5,1},{6,2},{7,3},{8,12},{9,13},{10,... | collective-permute-start | bytes 196616 | tf_op jit(solution)/shard_map/ppermute | solution.py:597
  28.4 0.8 %collective-permute-start.3 = (f32[32,512]{1,0:T(8,128)S(1)}, f32[32,512]{1,0:T(8,128)S(1)}, u32[]{:S(2)}, u32[]{:S(2)}) collective-permute-start(f32[32,512]{1,0:T(8,128)S(1)} %shard_map.171.share_ref), channel_id=1, source_target_pairs={{0,6},{1,7},{2,0},{3,1},{4,2},{5,3},{6,4},{7,5},{8,14},{9,15},{10,... | collective-permute-start | bytes 196616 | tf_op jit(solution)/shard_map/ppermute | solution.py:597
  29.2 0.7 collective-permute-start.2
  29.9 0.4 collective-permute-start.5
  30.3 2.3 %collective-permute-start.7 = (bf16[256,512]{1,0:T(8,128)(2,1)S(1)}, bf16[256,512]{1,0:T(8,128)(2,1)S(1)}, u32[]{:S(2)}, u32[]{:S(2)}) collective-permute-start(bf16[256,512]{1,0:T(8,128)(2,1)S(1)} %get-tuple-element.40), channel_id=1, source_target_pairs={{0,6},{1,7},{2,0},{3,1},{4,2},{5,3},{6,4},{7,5},{8,14},{9,15},{10,... | collective-permute-start | bytes 786440 | tf_op jit(solution)/shard_map/ppermute | solution.py:597
  32.6 0.0 collective-permute-done.4.in3_ref
  32.6 0.0 collective-permute-done.3.in2_ref
  32.6 1.1 %collective-permute-done.2.in1_ref = f32[32,512]{1,0:T(8,128)S(1)} collective-permute-done((f32[32,512]{1,0:T(8,128)S(1)}, f32[32,512]{1,0:T(8,128)S(1)}, u32[]{:S(2)}, u32[]{:S(2)}) %collective-permute-start.2) | collective-permute-done | bytes 65568 | tf_op jit(solution)/shard_map/ppermute | solution.py:597
  33.7 0.0 copy-done
  33.7 0.0 copy-done.1
  33.7 0.9 %shard_map.172 = (bf16[16,32,512]{2,1,0:T(8,128)(2,1)}, f32[8,512]{1,0:T(8,128)}, f32[8,512]{1,0:T(8,128)}, f32[8,512]{1,0:T(8,128)}) custom-call(f32[32,512]{1,0:T(8,128)S(1)} %shard_map.171.share_ref, f32[32,512]{1,0:T(8,128)S(1)} %collective-permute-done.2.in1_ref, f32[32,512]{1,0:T(8,128)S(1)} %collective-permute-done.3.in2_ref, ...), custom_call_target="tpu_custom_call" | custom-call | flops 327680 | bytes 983040 | tf_op jit(solution)/shard_map/pallas_call | solution.py:190
  34.6 0.1 collective-permute-start.6
  34.7 3.6 %all-to-all-start.1 = ((bf16[16,32,512]{2,1,0:T(8,128)(2,1)}), bf16[16,32,512]{2,1,0:T(8,128)(2,1)S(1)}, u32[]{:S(2)}, u32[]{:S(2)}) async-start(bf16[16,32,512]{2,1,0:T(8,128)(2,1)} %get-tuple-element.35), calls=%async_computation.1 | async-start | bytes 1048576 | tf_op jit(solution)/shard_map/all_to_all | solution.py:627
  38.3 3.9 %shard_map.174.refs_1_ = bf16[512,1024]{1,0:T(8,128)(2,1)} custom-call(s32[1,4096]{1,0:T(1,128)S(1)} %bitcast.20, s32[1,1024]{1,0:T(1,128)S(1)} %bitcast.24), custom_call_target="tpu_custom_call" | custom-call | flops 1610612736 | bytes 1048576 | tf_op jit(solution)/shard_map/pallas_call | solution.py:415
  42.1 0.0 collective-permute-done.5.refs_1_
  42.1 0.0 collective-permute-done.7.refs_3_
  42.2 1.0 %collective-permute-done.6.refs_2_ = bf16[256,512]{1,0:T(8,128)(2,1)S(1)} collective-permute-done((bf16[256,512]{1,0:T(8,128)(2,1)S(1)}, bf16[256,512]{1,0:T(8,128)(2,1)S(1)}, u32[]{:S(2)}, u32[]{:S(2)}) %collective-permute-start.6) | collective-permute-done | bytes 262176 | tf_op jit(solution)/shard_map/ppermute | solution.py:597
  43.1 0.0 copy-done.4
  43.1 5.6 %shard_map.173.pre_hbm = bf16[1024,2048]{1,0:T(8,128)(2,1)} custom-call(s32[8,128]{1,0:T(8,128)S(1)} %bitcast.25, bf16[256,512]{1,0:T(8,128)(2,1)S(1)} %get-tuple-element.32.refs_0_, bf16[256,512]{1,0:T(8,128)(2,1)S(1)} %collective-permute-done.5.refs_1_, bf16[256,512]{1,0:T(8,128)(2,1)S(1)} %collective-permute-done.6.refs_2_, ...), custom_call_target="tpu_custom_call" | custom-call | flops 3221225472 | bytes 4194304 | tf_op jit(solution)/shard_map/pallas_call | solution.py:347
  48.7 0.0 all-to-all-done.1
  48.8 0.0 copy-start.5
  48.8 4.3 %collective-permute-start.8 = (bf16[512,512]{1,0:T(8,128)(2,1)S(1)}, bf16[512,512]{1,0:T(8,128)(2,1)S(1)}, u32[]{:S(2)}, u32[]{:S(2)}) collective-permute-start(bf16[512,512]{1,0:T(8,128)(2,1)S(1)} %bitcast.14), channel_id=1, source_target_pairs={{0,1},{1,0},{2,3},{3,2},{4,5},{5,4},{6,7},{7,6},{8,9},{9,8},{10,11... | collective-permute-start | bytes 1572872 | tf_op jit(solution)/shard_map/ppermute | solution.py:634
  53.1 2.5 %shard_map.175 = (f32[1024,512]{1,0:T(8,128)S(1)}, bf16[1024,512]{1,0:T(8,128)(2,1)S(1)}, bf16[256,2048]{1,0:T(8,128)(2,1)S(1)}, bf16[512,2048]{1,0:T(8,128)(2,1)S(1)}) custom-call(bf16[512,512]{1,0:T(8,128)(2,1)S(1)} %bitcast.15, bf16[1024,2048]{1,0:T(8,128)(2,1)} %shard_map.173.pre_hbm, bf16[1024,2048]{1,0:T(8,128)(2,1)} %w_in_hbm.1, ...), custom_call_target="tpu_custom_call" | custom-call | flops 536870912 | bytes 6291456 | tf_op jit(solution)/shard_map/pallas_call | solution.py:464
  55.6 0.0 collective-permute-done.8.other_ref
  55.6 0.0 copy-done.5
  55.7 15.0 %shard_map.176 = f32[1024,2048]{1,0:T(8,128)} custom-call(f32[1024,512]{1,0:T(8,128)S(1)} %get-tuple-element.44.pool_ref, bf16[1024,512]{1,0:T(8,128)(2,1)S(1)} %get-tuple-element.45.count_ref, bf16[512,512]{1,0:T(8,128)(2,1)S(1)} %collective-permute-done.8.other_ref, bf16[512,2048]{1,0:T(8,128)(2,1)S(1)} %get-tuple-element.47.w_hot_ref, ...), custom_call_target="tpu_custom_call" | custom-call | flops 11274289152 | bytes 8388608 | tf_op jit(solution)/shard_map/pallas_call | solution.py:547
  (2 shorter events, 0.0 us)
Async XLA Ops:
  1.9 4.3 %collective-permute-start = (bf16[512,512]{1,0:T(8,128)(2,1)S(1)}, bf16[512,512]{1,0:T(8,128)(2,1)S(1)}, u32[]{:S(2)}, u32[]{:S(2)}) collective-permute-start(bf16[512,512]{1,0:T(8,128)(2,1)S(1)} %shard_map.165), channel_id=1, source_target_pairs={{0,1},{1,0},{2,3},{3,2},{4,5},{5,4},{6,7},{7,6},{8,9},{9,8},{10,11... | collective-permute-start | bytes 1572872 | tf_op jit(solution)/shard_map/ppermute | solution.py:601
  6.1 11.5 %copy-start.3 = (s32[1,1,4096]{2,1,0:T(1,128)S(1)}, s32[1,1,4096]{2,1,0:T(1,128)}, u32[]{:S(2)}) copy-start(s32[1,1,4096]{2,1,0:T(1,128)} %param.18) | copy-start | bytes 49156
  6.1 11.5 %copy-start.6 = (s32[1,1,1024]{2,1,0:T(1,128)S(1)}, s32[1,1,1024]{2,1,0:T(1,128)}, u32[]{:S(2)}) copy-start(s32[1,1,1024]{2,1,0:T(1,128)} %param.19) | copy-start | bytes 12292
  6.1 11.4 %collective-permute-start.1 = (bf16[512,512]{1,0:T(8,128)(2,1)S(1)}, bf16[512,512]{1,0:T(8,128)(2,1)S(1)}, u32[]{:S(2)}, u32[]{:S(2)}) collective-permute-start(bf16[512,512]{1,0:T(8,128)(2,1)S(1)} %get-tuple-element.31), channel_id=1, source_target_pairs={{0,1},{1,0},{2,3},{3,2},{4,5},{5,4},{6,7},{7,6},{8,9},{9,8},{10,11... | collective-permute-start | bytes 1572872 | tf_op jit(solution)/shard_map/ppermute | solution.py:610
  7.1 18.3 %all-to-all-start = ((bf16[16,32,512]{2,1,0:T(8,128)(2,1)}), bf16[16,32,512]{2,1,0:T(8,128)(2,1)S(1)}, u32[]{:S(2)}, u32[]{:S(2)}) async-start(bf16[16,32,512]{2,1,0:T(8,128)(2,1)} %bitcast.28), calls=%async_computation | async-start | bytes 1048576 | tf_op jit(solution)/shard_map/all_to_all | solution.py:607
  17.4 16.2 %copy-start = (f32[64,512]{1,0:T(8,128)S(1)}, f32[64,512]{1,0:T(8,128)}, u32[]{:S(2)}) copy-start(f32[64,512]{1,0:T(8,128)} %param.17) | copy-start | bytes 393220
  17.4 16.2 %copy-start.1 = (f32[64,512]{1,0:T(8,128)S(1)}, f32[64,512]{1,0:T(8,128)}, u32[]{:S(2)}) copy-start(f32[64,512]{1,0:T(8,128)} %param.15) | copy-start | bytes 393220
  17.4 16.2 %copy-start.2 = (f32[64,512]{1,0:T(8,128)S(1)}, f32[64,512]{1,0:T(8,128)}, u32[]{:S(2)}) copy-start(f32[64,512]{1,0:T(8,128)} %param.16) | copy-start | bytes 393220
  21.9 21.2 %copy-start.4 = (f32[2048]{0:T(1024)S(1)}, f32[2048]{0:T(1024)}, u32[]{:S(2)}) copy-start(f32[2048]{0:T(1024)} %param.25) | copy-start | bytes 24580
  21.9 21.2 %copy-start.7 = (s32[1,1,8,128]{3,2,1,0:T(8,128)S(1)}, s32[1,1,8,128]{3,2,1,0:T(8,128)}, u32[]{:S(2)}) copy-start(s32[1,1,8,128]{3,2,1,0:T(8,128)} %param.23) | copy-start | bytes 12292
  25.4 7.1 %collective-permute-start.4 = (f32[32,512]{1,0:T(8,128)S(1)}, f32[32,512]{1,0:T(8,128)S(1)}, u32[]{:S(2)}, u32[]{:S(2)}) collective-permute-start(f32[32,512]{1,0:T(8,128)S(1)} %shard_map.171.share_ref), channel_id=1, source_target_pairs={{0,4},{1,5},{2,6},{3,7},{4,0},{5,1},{6,2},{7,3},{8,12},{9,13},{10,... | collective-permute-start | bytes 196616 | tf_op jit(solution)/shard_map/ppermute | solution.py:597
  28.4 4.2 %collective-permute-start.3 = (f32[32,512]{1,0:T(8,128)S(1)}, f32[32,512]{1,0:T(8,128)S(1)}, u32[]{:S(2)}, u32[]{:S(2)}) collective-permute-start(f32[32,512]{1,0:T(8,128)S(1)} %shard_map.171.share_ref), channel_id=1, source_target_pairs={{0,6},{1,7},{2,0},{3,1},{4,2},{5,3},{6,4},{7,5},{8,14},{9,15},{10,... | collective-permute-start | bytes 196616 | tf_op jit(solution)/shard_map/ppermute | solution.py:597
  29.2 4.5 %collective-permute-start.2 = (f32[32,512]{1,0:T(8,128)S(1)}, f32[32,512]{1,0:T(8,128)S(1)}, u32[]{:S(2)}, u32[]{:S(2)}) collective-permute-start(f32[32,512]{1,0:T(8,128)S(1)} %shard_map.171.share_ref), channel_id=1, source_target_pairs={{0,2},{1,3},{2,4},{3,5},{4,6},{5,7},{6,0},{7,1},{8,10},{9,11},{10,... | collective-permute-start | bytes 196616 | tf_op jit(solution)/shard_map/ppermute | solution.py:597
  29.9 12.2 %collective-permute-start.5 = (bf16[256,512]{1,0:T(8,128)(2,1)S(1)}, bf16[256,512]{1,0:T(8,128)(2,1)S(1)}, u32[]{:S(2)}, u32[]{:S(2)}) collective-permute-start(bf16[256,512]{1,0:T(8,128)(2,1)S(1)} %get-tuple-element.38), channel_id=1, source_target_pairs={{0,2},{1,3},{2,4},{3,5},{4,6},{5,7},{6,0},{7,1},{8,10},{9,11},{10,... | collective-permute-start | bytes 786440 | tf_op jit(solution)/shard_map/ppermute | solution.py:597
  30.3 11.9 %collective-permute-start.7 = (bf16[256,512]{1,0:T(8,128)(2,1)S(1)}, bf16[256,512]{1,0:T(8,128)(2,1)S(1)}, u32[]{:S(2)}, u32[]{:S(2)}) collective-permute-start(bf16[256,512]{1,0:T(8,128)(2,1)S(1)} %get-tuple-element.40), channel_id=1, source_target_pairs={{0,6},{1,7},{2,0},{3,1},{4,2},{5,3},{6,4},{7,5},{8,14},{9,15},{10,... | collective-permute-start | bytes 786440 | tf_op jit(solution)/shard_map/ppermute | solution.py:597
  34.6 8.5 %collective-permute-start.6 = (bf16[256,512]{1,0:T(8,128)(2,1)S(1)}, bf16[256,512]{1,0:T(8,128)(2,1)S(1)}, u32[]{:S(2)}, u32[]{:S(2)}) collective-permute-start(bf16[256,512]{1,0:T(8,128)(2,1)S(1)} %get-tuple-element.39), channel_id=1, source_target_pairs={{0,4},{1,5},{2,6},{3,7},{4,0},{5,1},{6,2},{7,3},{8,12},{9,13},{10,... | collective-permute-start | bytes 786440 | tf_op jit(solution)/shard_map/ppermute | solution.py:597
  34.7 14.1 %all-to-all-start.1 = ((bf16[16,32,512]{2,1,0:T(8,128)(2,1)}), bf16[16,32,512]{2,1,0:T(8,128)(2,1)S(1)}, u32[]{:S(2)}, u32[]{:S(2)}) async-start(bf16[16,32,512]{2,1,0:T(8,128)(2,1)} %get-tuple-element.35), calls=%async_computation.1 | async-start | bytes 1048576 | tf_op jit(solution)/shard_map/all_to_all | solution.py:627
  48.8 6.9 %copy-start.5 = (f32[2048]{0:T(1024)S(1)}, f32[2048]{0:T(1024)}, u32[]{:S(2)}) copy-start(f32[2048]{0:T(1024)} %param.27) | copy-start | bytes 24580
  48.8 6.9 %collective-permute-start.8 = (bf16[512,512]{1,0:T(8,128)(2,1)S(1)}, bf16[512,512]{1,0:T(8,128)(2,1)S(1)}, u32[]{:S(2)}, u32[]{:S(2)}) collective-permute-start(bf16[512,512]{1,0:T(8,128)(2,1)S(1)} %bitcast.14), channel_id=1, source_target_pairs={{0,1},{1,0},{2,3},{3,2},{4,5},{5,4},{6,7},{7,6},{8,9},{9,8},{10,11... | collective-permute-start | bytes 1572872 | tf_op jit(solution)/shard_map/ppermute | solution.py:634

commit v6 on v5

--- a/solution.py
+++ b/solution.py
@@ -297,8 +297,8 @@
 
 
 def cold_kernel(sample_ref, *refs):
-    rows_in, rest = refs[:-8], refs[-8:]
-    w_hbm, b_ref, pre_hbm, w_ref, feature_ref, held_ref, sem, out_sems = rest
+    rows_in, rest = refs[:-9], refs[-9:]
+    w_hbm, b_ref, pre_hbm, first_ref, w_ref, feature_ref, held_ref, sem, out_sems = rest
     core, line = my_place()
     lines = len(rows_in)
     batch, width = feature_ref.shape
@@ -337,6 +337,7 @@
         return 0
 
     lax.fori_loop(0, batch // TILE, step, 0)
+    first_ref[...] = held_ref[:TILE, :]
     for i in range(batch // TILE):
         leave(i).wait()
 
@@ -346,9 +347,9 @@
     width = rows_in[0].shape[1]
     return pl.pallas_call(
         cold_kernel,
-        out_shape=pltpu.HBM((batch, hidden), BF16),
+        out_shape=(pltpu.HBM((batch, hidden), BF16), jax.ShapeDtypeStruct((TILE, hidden), BF16)),
         in_specs=[VMEM] * (len(rows_in) + 1) + [HBM, VMEM],
-        out_specs=HBM,
+        out_specs=(HBM, VMEM),
         scratch_shapes=[
             pltpu.VMEM((width, hidden), BF16),
             pltpu.VMEM((batch, width), BF16),
@@ -427,9 +428,9 @@
     )(ids, lengths)
 
 
-def own_kernel(own_ref, pre_hbm, w_in_hbm, *refs):
-    counts, rest = refs[:-6], refs[-6:]
-    pool_ref, count_ref, pre_ref, w_hot_ref, held_ref, sems = rest
+def own_kernel(own_ref, w_in_hbm, *refs):
+    counts, rest = refs[:-5], refs[-5:]
+    pool_ref, count_ref, w_hot_ref, held_ref, sems = rest
     half = own_ref.shape[0]
     needed, later, low = [], [], 0
     for part in counts:
@@ -438,7 +439,6 @@
         later.append((part.at[:, pl.ds(half, half)], count_ref.at[here]))
         low += part.shape[0]
     later.append((w_in_hbm.at[pl.ds(0, w_hot_ref.shape[0])], w_hot_ref))
-    later.append((pre_hbm.at[pl.ds(0, pre_ref.shape[0])], pre_ref))
     copies = [
         pltpu.make_async_copy(source, target, sems.at[i])
         for i, (source, target) in enumerate(needed + later)
@@ -458,25 +458,24 @@
         copy.wait()
 
 
-def own_pool(counts, fresh_own, pre, w_in):
+def own_pool(counts, fresh_own, w_in):
     half, width = fresh_own.shape
-    batch, hidden = pre.shape
+    batch, hidden = sum(c.shape[0] for c in counts), w_in.shape[1]
     return pl.pallas_call(
         own_kernel,
         out_shape=(
             pltpu.VMEM((batch, width), F32),
             pltpu.VMEM((batch, half), BF16),
-            pltpu.VMEM((TILE, hidden), BF16),
             pltpu.VMEM((width, hidden), BF16),
         ),
-        in_specs=[VMEM] + [HBM] * (2 + len(counts)),
-        out_specs=(VMEM, VMEM, VMEM, VMEM),
+        in_specs=[VMEM] + [HBM] * (1 + len(counts)),
+        out_specs=(VMEM, VMEM, VMEM),
         scratch_shapes=[
-            pltpu.VMEM((batch, half), BF16), pltpu.SemaphoreType.DMA((2 * len(counts) + 2,))
+            pltpu.VMEM((batch, half), BF16), pltpu.SemaphoreType.DMA((2 * len(counts) + 1,))
         ],
         compiler_params=params(16),
         cost_estimate=cost(2 * batch * half * width, 3 * batch * width * 4),
-    )(fresh_own, in_hbm(pre), in_hbm(w_in), *(in_hbm(c) for c in counts))
+    )(fresh_own, in_hbm(w_in), *(in_hbm(c) for c in counts))
 
 
 def mlp_kernel(
@@ -516,8 +515,11 @@
             def _():
                 load_w(i).start()
 
-        pre = dot(pool.astype(BF16), w_hot_ref[...]) + pre_ref[i].astype(F32)
-        hidden_ref[here, :] = jnp.maximum(pre, 0.0).astype(BF16)
+        feature = pool.astype(BF16)
+        for low in range(0, w_hot_ref.shape[1], PIECE):
+            piece = slice(low, low + PIECE)
+            pre = dot(feature, w_hot_ref[:, piece]) + pre_ref[i, :, piece].astype(F32)
+            hidden_ref[here, piece] = jnp.maximum(pre, 0.0).astype(BF16)
         return 0
 
     lax.fori_loop(0, tiles, first_layer, 0)
@@ -530,7 +532,10 @@
             leave(n - 2).wait()
 
         here = pl.ds(pl.multiple_of(n * columns, columns), columns)
-        out_ref[lax.rem(n, 2)] = dot(hidden_ref[...], w_out_ref[n]) + b_ref[:, here]
+        slot = lax.rem(n, 2)
+        for low in range(0, hidden_ref.shape[0], TILE):
+            rows = slice(low, low + TILE)
+            out_ref[slot, rows, :] = dot(hidden_ref[rows, :], w_out_ref[n]) + b_ref[:, here]
         leave(n).start()
         return 0
 
@@ -628,13 +633,11 @@
     samples, ids_late, *further = after(spread, cold_sample[0, 0], ids, *rows_in[2:-1])
     rows_in[2:-1] = [along(block, 2 + s) for s, block in enumerate(further)]
     count_high = count_matrix(ids_late, lengths, hot, own, early, blocks_in_all - early)
-    pre = cold_half(samples, rows_in, w_in, b_in, batch)
+    pre, first_pre = cold_half(samples, rows_in, w_in, b_in, batch)
     fresh_own, *_ = lax.optimization_barrier((fresh_own, pre, count_high))
     fresh_own = fresh_own.reshape(hot // 2, width)
     fresh_other = lax.ppermute(fresh_own, "table", swap)
-    pool, counts_other, first_pre, w_hot = own_pool(
-        [count_low, count_high], fresh_own, pre, w_in
-    )
+    pool, counts_other, w_hot = own_pool([count_low, count_high], fresh_own, w_in)
     fresh_other, pool = lax.optimization_barrier((fresh_other, pool))
     result = mlp(pool, counts_other, fresh_other, w_hot, first_pre, pre, w_out, b_out)
     return (result[None, None], new_master, new_first, new_second)

time: 71 us -> 71.4 us (level)
  local copies, waits for them, and re-layouts: 0.05 us -> 1.02 us
    unnamed x16 -> x20, local copies, waits for them, and re-layouts: 0.05 us -> 1.02 us
where the time goes in v6:
time: 71.4 us; the launch traced here: 71.2 us
  Pallas kernels  39.5 us (55%)
  starting transfers between devices  24.3 us (34%)
  waiting for transfers between devices  5.54 us (8%)
  local copies, waits for them, and re-layouts  1.02 us (1%)
  between operations  0.86 us (1%)
    pallas_call x1, Pallas kernels, mlp(): pl.pallas_call(mlp_kernel, out_shape=jax.ShapeDtypeStruct((batch, wide),...  14.9 us
    pallas_call x2, Pallas kernels, count_matrix(): pl.pallas_call(functools.partial(count_kernel, low_block, own), out_shape...  8.16 us
    all_to_all x1, starting transfers between devices, on_device(): lax.all_to_all(chip.reshape(n_dp, lines * own, width), 'dp', split_axis=0...  7.7 us
    ppermute x6, starting transfers between devices, along(): return lax.ppermute(array, 'table', pairs)  7.21 us
    pallas_call x1, Pallas kernels, cold_half(): pl.pallas_call(cold_kernel, out_shape=(pltpu.HBM((batch, hidden), BF16),...  5.46 us
    pallas_call x2, Pallas kernels, pick(): pl.pallas_call(functools.partial(pick_kernel, grad is not None), out_shap...  5.31 us
    ppermute x1, starting transfers between devices, on_device(): fresh_other = lax.ppermute(fresh_own, 'table', swap)  4.25 us
    all_to_all x1, waiting for transfers between devices, on_device(): lax.all_to_all(chip.reshape(n_dp, lines * own, width), 'dp', split_axis=0...  3.93 us
  transfers between devices with their start and end apart: 11, of which 3 were waited for; matrix products, arithmetic and copies ran while one was open for 0% of the time, Pallas kernels for 33%

profile of v6, /device:TPU:1, one launch (start us, length us, event | category | flops | bytes accessed | tf_op | source)
XLA Modules:
  0.0 71.2 jit_solution(2958640588327167744)
XLA Ops:
  0.6 1.2 %shard_map.165 = bf16[512,512]{1,0:T(8,128)(2,1)S(1)} custom-call(f32[16,4,2,8,512]{4,3,2,1,0:T(8,128)} %bitcast.26), custom_call_target="tpu_custom_call" | custom-call | bytes 1572864 | tf_op jit(solution)/shard_map/pallas_call | solution.py:101
  1.9 1.5 %collective-permute-start = (bf16[512,512]{1,0:T(8,128)(2,1)S(1)}, bf16[512,512]{1,0:T(8,128)(2,1)S(1)}, u32[]{:S(2)}, u32[]{:S(2)}) collective-permute-start(bf16[512,512]{1,0:T(8,128)(2,1)S(1)} %shard_map.165), channel_id=1, source_target_pairs={{0,1},{1,0},{2,3},{3,2},{4,5},{5,4},{6,7},{7,6},{8,9},{9,8},{10,11... | collective-permute-start | bytes 1572872 | tf_op jit(solution)/shard_map/ppermute | solution.py:606
  3.4 2.7 %shard_map.166 = (bf16[512,512]{1,0:T(8,128)(2,1)S(1)}, f32[16,4,8,512]{3,2,1,0:T(8,128)S(1)}) custom-call(s32[8,128]{1,0:T(8,128)} %bitcast.29, s32[1,8]{1,0:T(1,128)} %bitcast.31, bf16[2048,512]{1,0:T(8,128)(2,1)} %table_hbm.3, f32[16,4,2,8,512]{4,3,2,1,0:T(8,128)} %bitcast.27), custom_call_target="tpu_custom_call" | custom-call | flops 1073741824 | bytes 2097152 | tf_op jit(solution)/shard_map/pallas_call | solution.py:269
  6.1 0.0 copy-start.3
  6.1 0.0 copy-start.6
  6.1 0.1 collective-permute-start.1
  6.2 0.0 collective-permute-done.other_ref
  6.2 0.9 %shard_map.167 = bf16[512,512]{1,0:T(8,128)(2,1)} custom-call(f32[16,4,8,512]{3,2,1,0:T(8,128)S(1)} %get-tuple-element.30.mine_ref, bf16[512,512]{1,0:T(8,128)(2,1)S(1)} %collective-permute-done.other_ref), custom_call_target="tpu_custom_call" | custom-call | bytes 2097152 | tf_op jit(solution)/shard_map/pallas_call | solution.py:131
  7.1 7.7 %all-to-all-start = ((bf16[16,32,512]{2,1,0:T(8,128)(2,1)}), bf16[16,32,512]{2,1,0:T(8,128)(2,1)S(1)}, u32[]{:S(2)}, u32[]{:S(2)}) async-start(bf16[16,32,512]{2,1,0:T(8,128)(2,1)} %bitcast.28), calls=%async_computation | async-start | bytes 1048576 | tf_op jit(solution)/shard_map/all_to_all | solution.py:612
  14.8 2.6 %shard_map.168.near_ref = bf16[512,512]{1,0:T(8,128)(2,1)S(1)} custom-call(s32[8,128]{1,0:T(8,128)} %bitcast.30, s32[1,8]{1,0:T(1,128)} %bitcast.32, bf16[2048,512]{1,0:T(8,128)(2,1)} %table_hbm.3), custom_call_target="tpu_custom_call" | custom-call | flops 1073741824 | bytes 2097152 | tf_op jit(solution)/shard_map/pallas_call | solution.py:269
  17.4 0.0 copy-start
  17.4 0.0 copy-start.1
  17.5 0.0 copy-start.2
  17.5 0.0 collective-permute-done.1.far_ref
  17.5 0.1 shard_map.169
  17.6 0.0 copy-done.3
  17.6 0.0 copy-done.6
  17.6 3.8 %shard_map.170.refs_0_ = bf16[512,1024]{1,0:T(8,128)(2,1)} custom-call(s32[1,4096]{1,0:T(1,128)S(1)} %bitcast.19, s32[1,1024]{1,0:T(1,128)S(1)} %bitcast.23), custom_call_target="tpu_custom_call" | custom-call | flops 1610612736 | bytes 1048576 | tf_op jit(solution)/shard_map/pallas_call | solution.py:416
  21.4 0.0 copy-start.4
  21.4 0.0 copy-start.7
  21.4 3.9 %all-to-all-done.parts_ref = bf16[16,32,512]{2,1,0:T(8,128)(2,1)S(1)} async-done(((bf16[16,32,512]{2,1,0:T(8,128)(2,1)}), bf16[16,32,512]{2,1,0:T(8,128)(2,1)S(1)}, u32[]{:S(2)}, u32[]{:S(2)}) %all-to-all-start) | async-done | bytes 524320 | tf_op jit(solution)/shard_map/all_to_all | solution.py:612
  25.4 0.1 shard_map.171.share_ref
  25.4 3.0 %collective-permute-start.4 = (f32[32,512]{1,0:T(8,128)S(1)}, f32[32,512]{1,0:T(8,128)S(1)}, u32[]{:S(2)}, u32[]{:S(2)}) collective-permute-start(f32[32,512]{1,0:T(8,128)S(1)} %shard_map.171.share_ref), channel_id=1, source_target_pairs={{0,4},{1,5},{2,6},{3,7},{4,0},{5,1},{6,2},{7,3},{8,12},{9,13},{10,... | collective-permute-start | bytes 196616 | tf_op jit(solution)/shard_map/ppermute | solution.py:602
  28.4 0.8 %collective-permute-start.3 = (f32[32,512]{1,0:T(8,128)S(1)}, f32[32,512]{1,0:T(8,128)S(1)}, u32[]{:S(2)}, u32[]{:S(2)}) collective-permute-start(f32[32,512]{1,0:T(8,128)S(1)} %shard_map.171.share_ref), channel_id=1, source_target_pairs={{0,6},{1,7},{2,0},{3,1},{4,2},{5,3},{6,4},{7,5},{8,14},{9,15},{10,... | collective-permute-start | bytes 196616 | tf_op jit(solution)/shard_map/ppermute | solution.py:602
  29.2 0.7 collective-permute-start.2
  29.9 0.4 collective-permute-start.5
  30.3 2.3 %collective-permute-start.7 = (bf16[256,512]{1,0:T(8,128)(2,1)S(1)}, bf16[256,512]{1,0:T(8,128)(2,1)S(1)}, u32[]{:S(2)}, u32[]{:S(2)}) collective-permute-start(bf16[256,512]{1,0:T(8,128)(2,1)S(1)} %get-tuple-element.41), channel_id=1, source_target_pairs={{0,6},{1,7},{2,0},{3,1},{4,2},{5,3},{6,4},{7,5},{8,14},{9,15},{10,... | collective-permute-start | bytes 786440 | tf_op jit(solution)/shard_map/ppermute | solution.py:602
  32.6 0.0 collective-permute-done.4.in3_ref
  32.6 0.0 collective-permute-done.3.in2_ref
  32.6 1.1 %collective-permute-done.2.in1_ref = f32[32,512]{1,0:T(8,128)S(1)} collective-permute-done((f32[32,512]{1,0:T(8,128)S(1)}, f32[32,512]{1,0:T(8,128)S(1)}, u32[]{:S(2)}, u32[]{:S(2)}) %collective-permute-start.2) | collective-permute-done | bytes 65568 | tf_op jit(solution)/shard_map/ppermute | solution.py:602
  33.7 0.0 copy-done
  33.7 0.0 copy-done.1
  33.7 0.0 copy-done.2
  33.7 0.9 %shard_map.172 = (bf16[16,32,512]{2,1,0:T(8,128)(2,1)}, f32[8,512]{1,0:T(8,128)}, f32[8,512]{1,0:T(8,128)}, f32[8,512]{1,0:T(8,128)}) custom-call(f32[32,512]{1,0:T(8,128)S(1)} %shard_map.171.share_ref, f32[32,512]{1,0:T(8,128)S(1)} %collective-permute-done.2.in1_ref, f32[32,512]{1,0:T(8,128)S(1)} %collective-permute-done.3.in2_ref, ...), custom_call_target="tpu_custom_call" | custom-call | flops 327680 | bytes 983040 | tf_op jit(solution)/shard_map/pallas_call | solution.py:190
  34.6 0.1 collective-permute-start.6
  34.7 3.6 %all-to-all-start.1 = ((bf16[16,32,512]{2,1,0:T(8,128)(2,1)}), bf16[16,32,512]{2,1,0:T(8,128)(2,1)S(1)}, u32[]{:S(2)}, u32[]{:S(2)}) async-start(bf16[16,32,512]{2,1,0:T(8,128)(2,1)} %get-tuple-element.36), calls=%async_computation.1 | async-start | bytes 1048576 | tf_op jit(solution)/shard_map/all_to_all | solution.py:632
  38.3 4.3 %shard_map.174.refs_1_ = bf16[512,1024]{1,0:T(8,128)(2,1)} custom-call(s32[1,4096]{1,0:T(1,128)S(1)} %bitcast.20, s32[1,1024]{1,0:T(1,128)S(1)} %bitcast.24), custom_call_target="tpu_custom_call" | custom-call | flops 1610612736 | bytes 1048576 | tf_op jit(solution)/shard_map/pallas_call | solution.py:416
  42.6 0.0 collective-permute-done.5.refs_1_
  42.6 0.0 collective-permute-done.7.refs_3_
  42.6 0.5 collective-permute-done.6.refs_2_
  43.1 0.0 copy-done.4
  43.2 5.5 %shard_map.173 = (bf16[1024,2048]{1,0:T(8,128)(2,1)}, bf16[256,2048]{1,0:T(8,128)(2,1)S(1)}) custom-call(s32[8,128]{1,0:T(8,128)S(1)} %bitcast.25, bf16[256,512]{1,0:T(8,128)(2,1)S(1)} %get-tuple-element.33.refs_0_, bf16[256,512]{1,0:T(8,128)(2,1)S(1)} %collective-permute-done.5.refs_1_, bf16[256,512]{1,0:T(8,128)(2,1)S(1)} %collective-permute-done.6.refs_2_, ...), custom_call_target="tpu_custom_call" | custom-call | flops 3221225472 | bytes 4194304 | tf_op jit(solution)/shard_map/pallas_call | solution.py:348
  48.6 1.0 %copy-done.8 = bf16[256,2048]{1,0:T(8,128)(2,1)} copy-done((bf16[256,2048]{1,0:T(8,128)(2,1)}, bf16[256,2048]{1,0:T(8,128)(2,1)S(1)}, u32[]{:S(2)}) %copy-start.8) | copy-done | bytes 1048600
  49.6 0.0 all-to-all-done.1
  49.6 4.3 %collective-permute-start.8 = (bf16[512,512]{1,0:T(8,128)(2,1)S(1)}, bf16[512,512]{1,0:T(8,128)(2,1)S(1)}, u32[]{:S(2)}, u32[]{:S(2)}) collective-permute-start(bf16[512,512]{1,0:T(8,128)(2,1)S(1)} %bitcast.14), channel_id=1, source_target_pairs={{0,1},{1,0},{2,3},{3,2},{4,5},{5,4},{6,7},{7,6},{8,9},{9,8},{10,11... | collective-permute-start | bytes 1572872 | tf_op jit(solution)/shard_map/ppermute | solution.py:639
  53.9 2.5 %shard_map.175 = (f32[1024,512]{1,0:T(8,128)S(1)}, bf16[1024,512]{1,0:T(8,128)(2,1)S(1)}, bf16[512,2048]{1,0:T(8,128)(2,1)S(1)}) custom-call(bf16[512,512]{1,0:T(8,128)(2,1)S(1)} %bitcast.15, bf16[1024,2048]{1,0:T(8,128)(2,1)} %w_in_hbm.1, bf16[512,1024]{1,0:T(8,128)(2,1)} %shard_map.170.refs_0_, bf16[512,1024]{1,0:T(8,128)(2,1)} %shard_map.174.refs_1_), custom_call_target="tpu_custom_call" | custom-call | flops 536870912 | bytes 6291456 | tf_op jit(solution)/shard_map/pallas_call | solution.py:464
  56.3 0.0 collective-permute-done.8.other_ref
  56.3 14.9 %shard_map.176 = f32[1024,2048]{1,0:T(8,128)} custom-call(f32[1024,512]{1,0:T(8,128)S(1)} %get-tuple-element.46.pool_ref, bf16[1024,512]{1,0:T(8,128)(2,1)S(1)} %get-tuple-element.47.count_ref, bf16[512,512]{1,0:T(8,128)(2,1)S(1)} %collective-permute-done.8.other_ref, bf16[512,2048]{1,0:T(8,128)(2,1)S(1)} %get-tuple-element.49.w_hot_ref, ...), custom_call_target="tpu_custom_call" | custom-call | flops 11274289152 | bytes 8388608 | tf_op jit(solution)/shard_map/pallas_call | solution.py:552
  (6 shorter events, 0.0 us)
Async XLA Ops:
  1.9 4.3 %collective-permute-start = (bf16[512,512]{1,0:T(8,128)(2,1)S(1)}, bf16[512,512]{1,0:T(8,128)(2,1)S(1)}, u32[]{:S(2)}, u32[]{:S(2)}) collective-permute-start(bf16[512,512]{1,0:T(8,128)(2,1)S(1)} %shard_map.165), channel_id=1, source_target_pairs={{0,1},{1,0},{2,3},{3,2},{4,5},{5,4},{6,7},{7,6},{8,9},{9,8},{10,11... | collective-permute-start | bytes 1572872 | tf_op jit(solution)/shard_map/ppermute | solution.py:606
  6.1 11.5 %copy-start.3 = (s32[1,1,4096]{2,1,0:T(1,128)S(1)}, s32[1,1,4096]{2,1,0:T(1,128)}, u32[]{:S(2)}) copy-start(s32[1,1,4096]{2,1,0:T(1,128)} %param.18) | copy-start | bytes 49156
  6.1 11.5 %copy-start.6 = (s32[1,1,1024]{2,1,0:T(1,128)S(1)}, s32[1,1,1024]{2,1,0:T(1,128)}, u32[]{:S(2)}) copy-start(s32[1,1,1024]{2,1,0:T(1,128)} %param.19) | copy-start | bytes 12292
  6.1 11.4 %collective-permute-start.1 = (bf16[512,512]{1,0:T(8,128)(2,1)S(1)}, bf16[512,512]{1,0:T(8,128)(2,1)S(1)}, u32[]{:S(2)}, u32[]{:S(2)}) collective-permute-start(bf16[512,512]{1,0:T(8,128)(2,1)S(1)} %get-tuple-element.32), channel_id=1, source_target_pairs={{0,1},{1,0},{2,3},{3,2},{4,5},{5,4},{6,7},{7,6},{8,9},{9,8},{10,11... | collective-permute-start | bytes 1572872 | tf_op jit(solution)/shard_map/ppermute | solution.py:615
  7.1 18.3 %all-to-all-start = ((bf16[16,32,512]{2,1,0:T(8,128)(2,1)}), bf16[16,32,512]{2,1,0:T(8,128)(2,1)S(1)}, u32[]{:S(2)}, u32[]{:S(2)}) async-start(bf16[16,32,512]{2,1,0:T(8,128)(2,1)} %bitcast.28), calls=%async_computation | async-start | bytes 1048576 | tf_op jit(solution)/shard_map/all_to_all | solution.py:612
  17.4 16.2 %copy-start = (f32[64,512]{1,0:T(8,128)S(1)}, f32[64,512]{1,0:T(8,128)}, u32[]{:S(2)}) copy-start(f32[64,512]{1,0:T(8,128)} %param.17) | copy-start | bytes 393220
  17.4 16.2 %copy-start.1 = (f32[64,512]{1,0:T(8,128)S(1)}, f32[64,512]{1,0:T(8,128)}, u32[]{:S(2)}) copy-start(f32[64,512]{1,0:T(8,128)} %param.15) | copy-start | bytes 393220
  17.5 16.2 %copy-start.2 = (f32[64,512]{1,0:T(8,128)S(1)}, f32[64,512]{1,0:T(8,128)}, u32[]{:S(2)}) copy-start(f32[64,512]{1,0:T(8,128)} %param.16) | copy-start | bytes 393220
  21.4 21.7 %copy-start.4 = (f32[2048]{0:T(1024)S(1)}, f32[2048]{0:T(1024)}, u32[]{:S(2)}) copy-start(f32[2048]{0:T(1024)} %param.25) | copy-start | bytes 24580
  21.4 21.7 %copy-start.7 = (s32[1,1,8,128]{3,2,1,0:T(8,128)S(1)}, s32[1,1,8,128]{3,2,1,0:T(8,128)}, u32[]{:S(2)}) copy-start(s32[1,1,8,128]{3,2,1,0:T(8,128)} %param.23) | copy-start | bytes 12292
  25.4 7.1 %collective-permute-start.4 = (f32[32,512]{1,0:T(8,128)S(1)}, f32[32,512]{1,0:T(8,128)S(1)}, u32[]{:S(2)}, u32[]{:S(2)}) collective-permute-start(f32[32,512]{1,0:T(8,128)S(1)} %shard_map.171.share_ref), channel_id=1, source_target_pairs={{0,4},{1,5},{2,6},{3,7},{4,0},{5,1},{6,2},{7,3},{8,12},{9,13},{10,... | collective-permute-start | bytes 196616 | tf_op jit(solution)/shard_map/ppermute | solution.py:602
  28.4 4.2 %collective-permute-start.3 = (f32[32,512]{1,0:T(8,128)S(1)}, f32[32,512]{1,0:T(8,128)S(1)}, u32[]{:S(2)}, u32[]{:S(2)}) collective-permute-start(f32[32,512]{1,0:T(8,128)S(1)} %shard_map.171.share_ref), channel_id=1, source_target_pairs={{0,6},{1,7},{2,0},{3,1},{4,2},{5,3},{6,4},{7,5},{8,14},{9,15},{10,... | collective-permute-start | bytes 196616 | tf_op jit(solution)/shard_map/ppermute | solution.py:602
  29.2 4.5 %collective-permute-start.2 = (f32[32,512]{1,0:T(8,128)S(1)}, f32[32,512]{1,0:T(8,128)S(1)}, u32[]{:S(2)}, u32[]{:S(2)}) collective-permute-start(f32[32,512]{1,0:T(8,128)S(1)} %shard_map.171.share_ref), channel_id=1, source_target_pairs={{0,2},{1,3},{2,4},{3,5},{4,6},{5,7},{6,0},{7,1},{8,10},{9,11},{10,... | collective-permute-start | bytes 196616 | tf_op jit(solution)/shard_map/ppermute | solution.py:602
  29.9 12.7 %collective-permute-start.5 = (bf16[256,512]{1,0:T(8,128)(2,1)S(1)}, bf16[256,512]{1,0:T(8,128)(2,1)S(1)}, u32[]{:S(2)}, u32[]{:S(2)}) collective-permute-start(bf16[256,512]{1,0:T(8,128)(2,1)S(1)} %get-tuple-element.39), channel_id=1, source_target_pairs={{0,2},{1,3},{2,4},{3,5},{4,6},{5,7},{6,0},{7,1},{8,10},{9,11},{10,... | collective-permute-start | bytes 786440 | tf_op jit(solution)/shard_map/ppermute | solution.py:602
  30.3 12.3 %collective-permute-start.7 = (bf16[256,512]{1,0:T(8,128)(2,1)S(1)}, bf16[256,512]{1,0:T(8,128)(2,1)S(1)}, u32[]{:S(2)}, u32[]{:S(2)}) collective-permute-start(bf16[256,512]{1,0:T(8,128)(2,1)S(1)} %get-tuple-element.41), channel_id=1, source_target_pairs={{0,6},{1,7},{2,0},{3,1},{4,2},{5,3},{6,4},{7,5},{8,14},{9,15},{10,... | collective-permute-start | bytes 786440 | tf_op jit(solution)/shard_map/ppermute | solution.py:602
  34.6 8.5 %collective-permute-start.6 = (bf16[256,512]{1,0:T(8,128)(2,1)S(1)}, bf16[256,512]{1,0:T(8,128)(2,1)S(1)}, u32[]{:S(2)}, u32[]{:S(2)}) collective-permute-start(bf16[256,512]{1,0:T(8,128)(2,1)S(1)} %get-tuple-element.40), channel_id=1, source_target_pairs={{0,4},{1,5},{2,6},{3,7},{4,0},{5,1},{6,2},{7,3},{8,12},{9,13},{10,... | collective-permute-start | bytes 786440 | tf_op jit(solution)/shard_map/ppermute | solution.py:602
  34.7 14.9 %all-to-all-start.1 = ((bf16[16,32,512]{2,1,0:T(8,128)(2,1)}), bf16[16,32,512]{2,1,0:T(8,128)(2,1)S(1)}, u32[]{:S(2)}, u32[]{:S(2)}) async-start(bf16[16,32,512]{2,1,0:T(8,128)(2,1)} %get-tuple-element.36), calls=%async_computation.1 | async-start | bytes 1048576 | tf_op jit(solution)/shard_map/all_to_all | solution.py:632
  48.6 1.0 %copy-start.8 = (bf16[256,2048]{1,0:T(8,128)(2,1)}, bf16[256,2048]{1,0:T(8,128)(2,1)S(1)}, u32[]{:S(2)}) copy-start(bf16[256,2048]{1,0:T(8,128)(2,1)S(1)} %get-tuple-element.50.first_pre_ref) | copy-start | bytes 3145732
  49.6 6.7 %copy-start.5 = (f32[2048]{0:T(1024)S(1)}, f32[2048]{0:T(1024)}, u32[]{:S(2)}) copy-start(f32[2048]{0:T(1024)} %param.27) | copy-start | bytes 24580
  49.6 6.7 %copy-start.9 = (bf16[256,2048]{1,0:T(8,128)(2,1)S(1)}, bf16[256,2048]{1,0:T(8,128)(2,1)}, u32[]{:S(2)}) copy-start(bf16[256,2048]{1,0:T(8,128)(2,1)} %copy-done.8) | copy-start | bytes 3145732
  49.6 6.7 %collective-permute-start.8 = (bf16[512,512]{1,0:T(8,128)(2,1)S(1)}, bf16[512,512]{1,0:T(8,128)(2,1)S(1)}, u32[]{:S(2)}, u32[]{:S(2)}) collective-permute-start(bf16[512,512]{1,0:T(8,128)(2,1)S(1)} %bitcast.14), channel_id=1, source_target_pairs={{0,1},{1,0},{2,3},{3,2},{4,5},{5,4},{6,7},{7,6},{8,9},{9,8},{10,11... | collective-permute-start | bytes 1572872 | tf_op jit(solution)/shard_map/ppermute | solution.py:639

commit v7 on v5

--- a/solution.py
+++ b/solution.py
@@ -607,8 +607,8 @@
     parts = lax.all_to_all(
         chip.reshape(n_dp, lines * own, width), "dp", split_axis=0, concat_axis=0, tiled=True
     )
+    index_near, far = after(chip, index, far)
     far_in = lax.ppermute(far, "table", swap)
-    (index_near,) = after(chip, index)
     (near,) = pick(index_near, counts, cold_table)
     blocks = merge(near, far_in, lines)
     rows_in = [along(blocks[s], s) if s in (1, lines - 1) else blocks[s] for s in range(lines)]

time: 71 us -> 71.1 us (level)
  transfers between devices with their start and end apart: 11 -> 11, of which waited for: 3 -> 3; matrix products, arithmetic and copies ran while one was open for 0% -> 0% of each run, Pallas kernels for 33% -> 32%
where the time goes in v7:
time: 71.1 us; the launch traced here: 70.7 us
  Pallas kernels  39.8 us (56%)
  starting transfers between devices  24.4 us (34%)
  waiting for transfers between devices  5.53 us (8%)
  between operations  0.86 us (1%)
    pallas_call x1, Pallas kernels, mlp(): pl.pallas_call(mlp_kernel, out_shape=jax.ShapeDtypeStruct((batch, wide),...  15 us
    pallas_call x2, Pallas kernels, count_matrix(): pl.pallas_call(functools.partial(count_kernel, low_block, own), out_shape...  8.19 us
    all_to_all x1, starting transfers between devices, on_device(): lax.all_to_all(chip.reshape(n_dp, lines * own, width), 'dp', split_axis=0...  7.69 us
    ppermute x6, starting transfers between devices, along(): return lax.ppermute(array, 'table', pairs)  7.21 us
    pallas_call x1, Pallas kernels, cold_half(): pl.pallas_call(cold_kernel, out_shape=pltpu.HBM((batch, hidden), BF16), i...  5.61 us
    pallas_call x2, Pallas kernels, pick(): pl.pallas_call(functools.partial(pick_kernel, grad is not None), out_shap...  5.31 us
    ppermute x1, starting transfers between devices, on_device(): fresh_other = lax.ppermute(fresh_own, 'table', swap)  4.31 us
    all_to_all x1, starting transfers between devices, on_device(): lax.all_to_all(spread, 'dp', split_axis=0, concat_axis=0, tiled=True)  3.57 us
  transfers between devices with their start and end apart: 11, of which 3 were waited for; matrix products, arithmetic and copies ran while one was open for 0% of the time, Pallas kernels for 32%

profile of v7, /device:TPU:1, one launch (start us, length us, event | category | flops | bytes accessed | tf_op | source)
XLA Modules:
  0.0 70.7 jit_solution(11502422592374883004)
XLA Ops:
  0.6 1.2 %shard_map.165 = bf16[512,512]{1,0:T(8,128)(2,1)S(1)} custom-call(f32[16,4,2,8,512]{4,3,2,1,0:T(8,128)} %bitcast.26), custom_call_target="tpu_custom_call" | custom-call | bytes 1572864 | tf_op jit(solution)/shard_map/pallas_call | solution.py:101
  1.9 1.5 %collective-permute-start = (bf16[512,512]{1,0:T(8,128)(2,1)S(1)}, bf16[512,512]{1,0:T(8,128)(2,1)S(1)}, u32[]{:S(2)}, u32[]{:S(2)}) collective-permute-start(bf16[512,512]{1,0:T(8,128)(2,1)S(1)} %shard_map.165), channel_id=1, source_target_pairs={{0,1},{1,0},{2,3},{3,2},{4,5},{5,4},{6,7},{7,6},{8,9},{9,8},{10,11... | collective-permute-start | bytes 1572872 | tf_op jit(solution)/shard_map/ppermute | solution.py:601
  3.4 2.7 %shard_map.166 = (bf16[512,512]{1,0:T(8,128)(2,1)S(1)}, f32[16,4,8,512]{3,2,1,0:T(8,128)S(1)}) custom-call(s32[8,128]{1,0:T(8,128)} %bitcast.29, s32[1,8]{1,0:T(1,128)} %bitcast.31, bf16[2048,512]{1,0:T(8,128)(2,1)} %table_hbm.3, f32[16,4,2,8,512]{4,3,2,1,0:T(8,128)} %bitcast.27), custom_call_target="tpu_custom_call" | custom-call | flops 1073741824 | bytes 2097152 | tf_op jit(solution)/shard_map/pallas_call | solution.py:269
  6.1 0.0 copy-start.3
  6.1 0.0 copy-start.6
  6.1 0.0 collective-permute-done.other_ref
  6.1 0.9 %shard_map.167 = bf16[512,512]{1,0:T(8,128)(2,1)} custom-call(f32[16,4,8,512]{3,2,1,0:T(8,128)S(1)} %get-tuple-element.30.mine_ref, bf16[512,512]{1,0:T(8,128)(2,1)S(1)} %collective-permute-done.other_ref), custom_call_target="tpu_custom_call" | custom-call | bytes 2097152 | tf_op jit(solution)/shard_map/pallas_call | solution.py:131
  7.0 0.1 collective-permute-start.1
  7.1 7.7 %all-to-all-start = ((bf16[16,32,512]{2,1,0:T(8,128)(2,1)}), bf16[16,32,512]{2,1,0:T(8,128)(2,1)S(1)}, u32[]{:S(2)}, u32[]{:S(2)}) async-start(bf16[16,32,512]{2,1,0:T(8,128)(2,1)} %bitcast.28), calls=%async_computation | async-start | bytes 1048576 | tf_op jit(solution)/shard_map/all_to_all | solution.py:607
  14.8 2.6 %shard_map.168.near_ref = bf16[512,512]{1,0:T(8,128)(2,1)S(1)} custom-call(s32[8,128]{1,0:T(8,128)} %bitcast.30, s32[1,8]{1,0:T(1,128)} %bitcast.32, bf16[2048,512]{1,0:T(8,128)(2,1)} %table_hbm.3), custom_call_target="tpu_custom_call" | custom-call | flops 1073741824 | bytes 2097152 | tf_op jit(solution)/shard_map/pallas_call | solution.py:269
  17.4 0.0 copy-start
  17.4 0.0 copy-start.1
  17.4 0.0 copy-start.2
  17.5 0.0 collective-permute-done.1.far_ref
  17.5 0.1 shard_map.169
  17.5 0.0 copy-done.3
  17.6 0.0 copy-done.6
  17.6 4.3 %shard_map.170.refs_0_ = bf16[512,1024]{1,0:T(8,128)(2,1)} custom-call(s32[1,4096]{1,0:T(1,128)S(1)} %bitcast.19, s32[1,1024]{1,0:T(1,128)S(1)} %bitcast.23), custom_call_target="tpu_custom_call" | custom-call | flops 1610612736 | bytes 1048576 | tf_op jit(solution)/shard_map/pallas_call | solution.py:415
  21.9 0.0 copy-start.4
  21.9 0.0 copy-start.7
  21.9 3.4 %all-to-all-done.parts_ref = bf16[16,32,512]{2,1,0:T(8,128)(2,1)S(1)} async-done(((bf16[16,32,512]{2,1,0:T(8,128)(2,1)}), bf16[16,32,512]{2,1,0:T(8,128)(2,1)S(1)}, u32[]{:S(2)}, u32[]{:S(2)}) %all-to-all-start) | async-done | bytes 524320 | tf_op jit(solution)/shard_map/all_to_all | solution.py:607
  25.4 0.1 shard_map.171.share_ref
  25.4 3.0 %collective-permute-start.4 = (f32[32,512]{1,0:T(8,128)S(1)}, f32[32,512]{1,0:T(8,128)S(1)}, u32[]{:S(2)}, u32[]{:S(2)}) collective-permute-start(f32[32,512]{1,0:T(8,128)S(1)} %shard_map.171.share_ref), channel_id=1, source_target_pairs={{0,4},{1,5},{2,6},{3,7},{4,0},{5,1},{6,2},{7,3},{8,12},{9,13},{10,... | collective-permute-start | bytes 196616 | tf_op jit(solution)/shard_map/ppermute | solution.py:597
  28.4 0.8 %collective-permute-start.3 = (f32[32,512]{1,0:T(8,128)S(1)}, f32[32,512]{1,0:T(8,128)S(1)}, u32[]{:S(2)}, u32[]{:S(2)}) collective-permute-start(f32[32,512]{1,0:T(8,128)S(1)} %shard_map.171.share_ref), channel_id=1, source_target_pairs={{0,6},{1,7},{2,0},{3,1},{4,2},{5,3},{6,4},{7,5},{8,14},{9,15},{10,... | collective-permute-start | bytes 196616 | tf_op jit(solution)/shard_map/ppermute | solution.py:597
  29.2 0.7 collective-permute-start.2
  29.9 0.4 collective-permute-start.5
  30.3 2.3 %collective-permute-start.7 = (bf16[256,512]{1,0:T(8,128)(2,1)S(1)}, bf16[256,512]{1,0:T(8,128)(2,1)S(1)}, u32[]{:S(2)}, u32[]{:S(2)}) collective-permute-start(bf16[256,512]{1,0:T(8,128)(2,1)S(1)} %get-tuple-element.42), channel_id=1, source_target_pairs={{0,6},{1,7},{2,0},{3,1},{4,2},{5,3},{6,4},{7,5},{8,14},{9,15},{10,... | collective-permute-start | bytes 786440 | tf_op jit(solution)/shard_map/ppermute | solution.py:597
  32.6 0.0 collective-permute-done.4.in3_ref
  32.6 0.0 collective-permute-done.3.in2_ref
  32.6 1.1 %collective-permute-done.2.in1_ref = f32[32,512]{1,0:T(8,128)S(1)} collective-permute-done((f32[32,512]{1,0:T(8,128)S(1)}, f32[32,512]{1,0:T(8,128)S(1)}, u32[]{:S(2)}, u32[]{:S(2)}) %collective-permute-start.2) | collective-permute-done | bytes 65568 | tf_op jit(solution)/shard_map/ppermute | solution.py:597
  33.7 0.0 copy-done
  33.7 0.0 copy-done.1
  33.7 0.0 copy-done.2
  33.7 0.9 %shard_map.172 = (bf16[16,32,512]{2,1,0:T(8,128)(2,1)}, f32[8,512]{1,0:T(8,128)}, f32[8,512]{1,0:T(8,128)}, f32[8,512]{1,0:T(8,128)}) custom-call(f32[32,512]{1,0:T(8,128)S(1)} %shard_map.171.share_ref, f32[32,512]{1,0:T(8,128)S(1)} %collective-permute-done.2.in1_ref, f32[32,512]{1,0:T(8,128)S(1)} %collective-permute-done.3.in2_ref, ...), custom_call_target="tpu_custom_call" | custom-call | flops 327680 | bytes 983040 | tf_op jit(solution)/shard_map/pallas_call | solution.py:190
  34.6 0.1 collective-permute-start.6
  34.7 3.6 %all-to-all-start.1 = ((bf16[16,32,512]{2,1,0:T(8,128)(2,1)}), bf16[16,32,512]{2,1,0:T(8,128)(2,1)S(1)}, u32[]{:S(2)}, u32[]{:S(2)}) async-start(bf16[16,32,512]{2,1,0:T(8,128)(2,1)} %get-tuple-element.37), calls=%async_computation.1 | async-start | bytes 1048576 | tf_op jit(solution)/shard_map/all_to_all | solution.py:627
  38.3 3.9 %shard_map.174.refs_1_ = bf16[512,1024]{1,0:T(8,128)(2,1)} custom-call(s32[1,4096]{1,0:T(1,128)S(1)} %bitcast.20, s32[1,1024]{1,0:T(1,128)S(1)} %bitcast.24), custom_call_target="tpu_custom_call" | custom-call | flops 1610612736 | bytes 1048576 | tf_op jit(solution)/shard_map/pallas_call | solution.py:415
  42.1 0.0 collective-permute-done.5.refs_1_
  42.1 0.0 collective-permute-done.7.refs_3_
  42.2 1.0 %collective-permute-done.6.refs_2_ = bf16[256,512]{1,0:T(8,128)(2,1)S(1)} collective-permute-done((bf16[256,512]{1,0:T(8,128)(2,1)S(1)}, bf16[256,512]{1,0:T(8,128)(2,1)S(1)}, u32[]{:S(2)}, u32[]{:S(2)}) %collective-permute-start.6) | collective-permute-done | bytes 262176 | tf_op jit(solution)/shard_map/ppermute | solution.py:597
  43.1 0.0 copy-done.4
  43.1 5.6 %shard_map.173.pre_hbm = bf16[1024,2048]{1,0:T(8,128)(2,1)} custom-call(s32[8,128]{1,0:T(8,128)S(1)} %bitcast.25, bf16[256,512]{1,0:T(8,128)(2,1)S(1)} %get-tuple-element.34.refs_0_, bf16[256,512]{1,0:T(8,128)(2,1)S(1)} %collective-permute-done.5.refs_1_, bf16[256,512]{1,0:T(8,128)(2,1)S(1)} %collective-permute-done.6.refs_2_, ...), custom_call_target="tpu_custom_call" | custom-call | flops 3221225472 | bytes 4194304 | tf_op jit(solution)/shard_map/pallas_call | solution.py:347
  48.8 0.0 all-to-all-done.1
  48.8 0.0 copy-start.5
  48.8 4.3 %collective-permute-start.8 = (bf16[512,512]{1,0:T(8,128)(2,1)S(1)}, bf16[512,512]{1,0:T(8,128)(2,1)S(1)}, u32[]{:S(2)}, u32[]{:S(2)}) collective-permute-start(bf16[512,512]{1,0:T(8,128)(2,1)S(1)} %bitcast.14), channel_id=1, source_target_pairs={{0,1},{1,0},{2,3},{3,2},{4,5},{5,4},{6,7},{7,6},{8,9},{9,8},{10,11... | collective-permute-start | bytes 1572872 | tf_op jit(solution)/shard_map/ppermute | solution.py:634
  53.1 2.5 %shard_map.175 = (f32[1024,512]{1,0:T(8,128)S(1)}, bf16[1024,512]{1,0:T(8,128)(2,1)S(1)}, bf16[256,2048]{1,0:T(8,128)(2,1)S(1)}, bf16[512,2048]{1,0:T(8,128)(2,1)S(1)}) custom-call(bf16[512,512]{1,0:T(8,128)(2,1)S(1)} %bitcast.15, bf16[1024,2048]{1,0:T(8,128)(2,1)} %shard_map.173.pre_hbm, bf16[1024,2048]{1,0:T(8,128)(2,1)} %w_in_hbm.1, ...), custom_call_target="tpu_custom_call" | custom-call | flops 536870912 | bytes 6291456 | tf_op jit(solution)/shard_map/pallas_call | solution.py:464
  55.6 0.0 collective-permute-done.8.other_ref
  55.7 15.0 %shard_map.176 = f32[1024,2048]{1,0:T(8,128)} custom-call(f32[1024,512]{1,0:T(8,128)S(1)} %get-tuple-element.46.pool_ref, bf16[1024,512]{1,0:T(8,128)(2,1)S(1)} %get-tuple-element.47.count_ref, bf16[512,512]{1,0:T(8,128)(2,1)S(1)} %collective-permute-done.8.other_ref, bf16[512,2048]{1,0:T(8,128)(2,1)S(1)} %get-tuple-element.49.w_hot_ref, ...), custom_call_target="tpu_custom_call" | custom-call | flops 11274289152 | bytes 8388608 | tf_op jit(solution)/shard_map/pallas_call | solution.py:547
  (2 shorter events, 0.0 us)
Async XLA Ops:
  1.9 4.2 %collective-permute-start = (bf16[512,512]{1,0:T(8,128)(2,1)S(1)}, bf16[512,512]{1,0:T(8,128)(2,1)S(1)}, u32[]{:S(2)}, u32[]{:S(2)}) collective-permute-start(bf16[512,512]{1,0:T(8,128)(2,1)S(1)} %shard_map.165), channel_id=1, source_target_pairs={{0,1},{1,0},{2,3},{3,2},{4,5},{5,4},{6,7},{7,6},{8,9},{9,8},{10,11... | collective-permute-start | bytes 1572872 | tf_op jit(solution)/shard_map/ppermute | solution.py:601
  6.1 11.5 %copy-start.3 = (s32[1,1,4096]{2,1,0:T(1,128)S(1)}, s32[1,1,4096]{2,1,0:T(1,128)}, u32[]{:S(2)}) copy-start(s32[1,1,4096]{2,1,0:T(1,128)} %param.18) | copy-start | bytes 49156
  6.1 11.5 %copy-start.6 = (s32[1,1,1024]{2,1,0:T(1,128)S(1)}, s32[1,1,1024]{2,1,0:T(1,128)}, u32[]{:S(2)}) copy-start(s32[1,1,1024]{2,1,0:T(1,128)} %param.19) | copy-start | bytes 12292
  7.0 10.5 %collective-permute-start.1 = (bf16[512,512]{1,0:T(8,128)(2,1)S(1)}, bf16[512,512]{1,0:T(8,128)(2,1)S(1)}, u32[]{:S(2)}, u32[]{:S(2)}) collective-permute-start(bf16[512,512]{1,0:T(8,128)(2,1)S(1)} %get-tuple-element.33), channel_id=1, source_target_pairs={{0,1},{1,0},{2,3},{3,2},{4,5},{5,4},{6,7},{7,6},{8,9},{9,8},{10,11... | collective-permute-start | bytes 1572872 | tf_op jit(solution)/shard_map/ppermute | solution.py:611
  7.1 18.3 %all-to-all-start = ((bf16[16,32,512]{2,1,0:T(8,128)(2,1)}), bf16[16,32,512]{2,1,0:T(8,128)(2,1)S(1)}, u32[]{:S(2)}, u32[]{:S(2)}) async-start(bf16[16,32,512]{2,1,0:T(8,128)(2,1)} %bitcast.28), calls=%async_computation | async-start | bytes 1048576 | tf_op jit(solution)/shard_map/all_to_all | solution.py:607
  17.4 16.2 %copy-start = (f32[64,512]{1,0:T(8,128)S(1)}, f32[64,512]{1,0:T(8,128)}, u32[]{:S(2)}) copy-start(f32[64,512]{1,0:T(8,128)} %param.17) | copy-start | bytes 393220
  17.4 16.2 %copy-start.1 = (f32[64,512]{1,0:T(8,128)S(1)}, f32[64,512]{1,0:T(8,128)}, u32[]{:S(2)}) copy-start(f32[64,512]{1,0:T(8,128)} %param.15) | copy-start | bytes 393220
  17.4 16.2 %copy-start.2 = (f32[64,512]{1,0:T(8,128)S(1)}, f32[64,512]{1,0:T(8,128)}, u32[]{:S(2)}) copy-start(f32[64,512]{1,0:T(8,128)} %param.16) | copy-start | bytes 393220
  21.9 21.2 %copy-start.4 = (f32[2048]{0:T(1024)S(1)}, f32[2048]{0:T(1024)}, u32[]{:S(2)}) copy-start(f32[2048]{0:T(1024)} %param.25) | copy-start | bytes 24580
  21.9 21.2 %copy-start.7 = (s32[1,1,8,128]{3,2,1,0:T(8,128)S(1)}, s32[1,1,8,128]{3,2,1,0:T(8,128)}, u32[]{:S(2)}) copy-start(s32[1,1,8,128]{3,2,1,0:T(8,128)} %param.23) | copy-start | bytes 12292
  25.4 7.1 %collective-permute-start.4 = (f32[32,512]{1,0:T(8,128)S(1)}, f32[32,512]{1,0:T(8,128)S(1)}, u32[]{:S(2)}, u32[]{:S(2)}) collective-permute-start(f32[32,512]{1,0:T(8,128)S(1)} %shard_map.171.share_ref), channel_id=1, source_target_pairs={{0,4},{1,5},{2,6},{3,7},{4,0},{5,1},{6,2},{7,3},{8,12},{9,13},{10,... | collective-permute-start | bytes 196616 | tf_op jit(solution)/shard_map/ppermute | solution.py:597
  28.4 4.2 %collective-permute-start.3 = (f32[32,512]{1,0:T(8,128)S(1)}, f32[32,512]{1,0:T(8,128)S(1)}, u32[]{:S(2)}, u32[]{:S(2)}) collective-permute-start(f32[32,512]{1,0:T(8,128)S(1)} %shard_map.171.share_ref), channel_id=1, source_target_pairs={{0,6},{1,7},{2,0},{3,1},{4,2},{5,3},{6,4},{7,5},{8,14},{9,15},{10,... | collective-permute-start | bytes 196616 | tf_op jit(solution)/shard_map/ppermute | solution.py:597
  29.2 4.5 %collective-permute-start.2 = (f32[32,512]{1,0:T(8,128)S(1)}, f32[32,512]{1,0:T(8,128)S(1)}, u32[]{:S(2)}, u32[]{:S(2)}) collective-permute-start(f32[32,512]{1,0:T(8,128)S(1)} %shard_map.171.share_ref), channel_id=1, source_target_pairs={{0,2},{1,3},{2,4},{3,5},{4,6},{5,7},{6,0},{7,1},{8,10},{9,11},{10,... | collective-permute-start | bytes 196616 | tf_op jit(solution)/shard_map/ppermute | solution.py:597
  29.9 12.2 %collective-permute-start.5 = (bf16[256,512]{1,0:T(8,128)(2,1)S(1)}, bf16[256,512]{1,0:T(8,128)(2,1)S(1)}, u32[]{:S(2)}, u32[]{:S(2)}) collective-permute-start(bf16[256,512]{1,0:T(8,128)(2,1)S(1)} %get-tuple-element.40), channel_id=1, source_target_pairs={{0,2},{1,3},{2,4},{3,5},{4,6},{5,7},{6,0},{7,1},{8,10},{9,11},{10,... | collective-permute-start | bytes 786440 | tf_op jit(solution)/shard_map/ppermute | solution.py:597
  30.3 11.9 %collective-permute-start.7 = (bf16[256,512]{1,0:T(8,128)(2,1)S(1)}, bf16[256,512]{1,0:T(8,128)(2,1)S(1)}, u32[]{:S(2)}, u32[]{:S(2)}) collective-permute-start(bf16[256,512]{1,0:T(8,128)(2,1)S(1)} %get-tuple-element.42), channel_id=1, source_target_pairs={{0,6},{1,7},{2,0},{3,1},{4,2},{5,3},{6,4},{7,5},{8,14},{9,15},{10,... | collective-permute-start | bytes 786440 | tf_op jit(solution)/shard_map/ppermute | solution.py:597
  34.6 8.5 %collective-permute-start.6 = (bf16[256,512]{1,0:T(8,128)(2,1)S(1)}, bf16[256,512]{1,0:T(8,128)(2,1)S(1)}, u32[]{:S(2)}, u32[]{:S(2)}) collective-permute-start(bf16[256,512]{1,0:T(8,128)(2,1)S(1)} %get-tuple-element.41), channel_id=1, source_target_pairs={{0,4},{1,5},{2,6},{3,7},{4,0},{5,1},{6,2},{7,3},{8,12},{9,13},{10,... | collective-permute-start | bytes 786440 | tf_op jit(solution)/shard_map/ppermute | solution.py:597
  34.7 14.1 %all-to-all-start.1 = ((bf16[16,32,512]{2,1,0:T(8,128)(2,1)}), bf16[16,32,512]{2,1,0:T(8,128)(2,1)S(1)}, u32[]{:S(2)}, u32[]{:S(2)}) async-start(bf16[16,32,512]{2,1,0:T(8,128)(2,1)} %get-tuple-element.37), calls=%async_computation.1 | async-start | bytes 1048576 | tf_op jit(solution)/shard_map/all_to_all | solution.py:627
  48.8 6.9 %copy-start.5 = (f32[2048]{0:T(1024)S(1)}, f32[2048]{0:T(1024)}, u32[]{:S(2)}) copy-start(f32[2048]{0:T(1024)} %param.27) | copy-start | bytes 24580
  48.8 6.9 %collective-permute-start.8 = (bf16[512,512]{1,0:T(8,128)(2,1)S(1)}, bf16[512,512]{1,0:T(8,128)(2,1)S(1)}, u32[]{:S(2)}, u32[]{:S(2)}) collective-permute-start(bf16[512,512]{1,0:T(8,128)(2,1)S(1)} %bitcast.14), channel_id=1, source_target_pairs={{0,1},{1,0},{2,3},{3,2},{4,5},{5,4},{6,7},{7,6},{8,9},{9,8},{10,11... | collective-permute-start | bytes 1572872 | tf_op jit(solution)/shard_map/ppermute | solution.py:634
